TPU v7x, 128 devices: a whole 4x4x4 slice. The times are simulated.
128 devices in a mesh: fsdp: 4 (over y), context: 16 (over x, z), tensor: 2 (over core).
Axes of the slice: x: 4, y: 4, z: 4, core: 2. Of those that a mesh axis runs over, the one named last changes fastest.
Arguments:
- tokens: bfloat16 [4, 2048, 2048], P('fsdp', 'context'), may hold values from -6 to 6
- cotangent: bfloat16 [4, 2048, 2048], P('fsdp', 'context'), may hold values from -6 to 6
- doc_lengths: int32 [4, 8], P('fsdp'), may hold values from 0 to 2048, as said below
- padding: int32 [4, 2048], P('fsdp', 'context'), may hold values from 0 to 1, as said below
- expert_ids: int32 [4, 2048, 8], P('fsdp', 'context'), may hold values from 0 to 63, as said below
- norm1_gain: bfloat16 [2048], P('fsdp'), may hold values from 0.5 to 1.5
- w_query: bfloat16 [2048, 4096], P('fsdp', 'tensor'), may hold values from -0.125 to 0.125
- key_weight: bfloat16 [2048, 512], P('fsdp', 'tensor'), may hold values from -0.125 to 0.125
- value_weight: bfloat16 [2048, 512], P('fsdp', 'tensor'), may hold values from -0.125 to 0.125
- q_gain: bfloat16 [128], P('fsdp'), may hold values from 0.5 to 1.5
- k_gain: bfloat16 [128], P('fsdp'), may hold values from 0.5 to 1.5
- w_out: bfloat16 [4096, 2048], P('tensor', 'fsdp'), may hold values from -0.375 to 0.375
- norm2_gain: bfloat16 [2048], P('fsdp'), may hold values from 0.5 to 1.5
- w_router: bfloat16 [2048, 64], P('fsdp'), may hold values from -0.0625 to 0.0625
- w_gate: bfloat16 [64, 2048, 768], P('context', 'fsdp', 'tensor'), may hold values from -0.125 to 0.125
- w_up: bfloat16 [64, 2048, 768], P('context', 'fsdp', 'tensor'), may hold values from -0.125 to 0.125
- w_down: bfloat16 [64, 768, 2048], P('context', 'tensor', 'fsdp'), may hold values from -0.625 to 0.625
Outputs:
- output: float32 [4, 2048, 2048], P('fsdp', 'context')
- loss: float32 [], replicated
- expert_load: float32 [64], replicated
- grad_tokens: float32 [4, 2048, 2048], P('fsdp', 'context')
- grad_norm1_gain: float32 [2048], P('fsdp')
- grad_w_query: float32 [2048, 4096], P('fsdp', 'tensor')
- grad_w_key: float32 [2048, 512], P('fsdp', 'tensor')
- grad_w_value: float32 [2048, 512], P('fsdp', 'tensor')
- grad_q_gain: float32 [128], P('fsdp')
- grad_k_gain: float32 [128], P('fsdp')
- grad_w_out: float32 [4096, 2048], P('tensor', 'fsdp')
- grad_norm2_gain: float32 [2048], P('fsdp')
- grad_w_router: float32 [2048, 64], P('fsdp')
- grad_w_gate: float32 [64, 2048, 768], P('context', 'fsdp', 'tensor')
- grad_w_up: float32 [64, 2048, 768], P('context', 'fsdp', 'tensor')
- grad_w_down: float32 [64, 768, 2048], P('context', 'tensor', 'fsdp')
Inputs may be any that keep to these rules, and one draw needn't show every extreme that they name: `doc_lengths`: each row sums to 2048. In one row, chosen by the seed, the first entry is 2048 and the others are 0. Each sequence ends with a run of 1 to 512 padding positions; all earlier positions are 0. `expert_ids`: each token names 8 different experts. In each aligned block of 128 positions of one sequence every expert is named by 0 or by exactly 32 tokens, and half of the experts by 32.
All inputs are finite; a program needn't handle non-finite values.
Results may differ from a plain program's by a relative error of at most 0.025.
Values may be sent and summed in bfloat16 or wider, within the bound.
No kernel may reach another device: no remote copies, remote signals or barrier semaphores. Data moves between devices by JAX's collectives and lax.ppermute only.
A program may use at most 320 MiB of HBM per device.

v0:
```python
from functools import partial

import jax
import jax.numpy as jnp
from jax import lax
from jax.sharding import PartitionSpec as P

WINDOW = 1024


epsilon = 1e-06
theta_base = 1000000.0
negative = -1e30


def shifted(x, axis, by):
    count = lax.axis_size(axis)
    pairs = [(i, i + by) for i in range(count) if 0 <= i + by < count]
    return lax.ppermute(x, axis, pairs)


def rms_scale(value_rows, gain_vec):
    inverse = lax.rsqrt(jnp.mean(value_rows * value_rows, axis=-1, keepdims=True) + epsilon)
    return value_rows * inverse * gain_vec


def rotate(value_rows, cosine, sine_table):
    half_size = value_rows.shape[-1] // 2
    first_half = value_rows[..., :half_size]
    second_half = value_rows[..., half_size:]
    return jnp.concatenate(
        [
            first_half * cosine - second_half * sine_table,
            second_half * cosine + first_half * sine_table,
        ],
        axis=-1,
    )


def head_prep(cosine, sine_table, projected, gain_vec):
    return rotate(rms_scale(projected, gain_vec), cosine, sine_table)


def doc_layout(doc_lengths, positions):
    ends = jnp.cumsum(doc_lengths, axis=-1)
    passed = positions[..., :, None] >= ends[..., None, :]
    doc_index = jnp.sum(passed.astype(jnp.int32), axis=-1)
    starts = jnp.sum(jnp.where(passed, doc_lengths[..., None, :], 0), axis=-1)
    return (doc_index, starts)


def attend_block(query_rows, keys, value_rows, allowed, score_scale):
    scores = (
        jnp.einsum("gqd,kd->gqk", query_rows, keys, preferred_element_type=jnp.float32)
        * score_scale
    )
    scores = jnp.where(allowed[None], scores, negative)
    row_peak = jnp.max(scores, axis=-1, keepdims=True)
    exponent = jnp.exp(scores - row_peak)
    row_total = jnp.sum(exponent, axis=-1, keepdims=True)
    weights_low = (exponent / row_total).astype(jnp.bfloat16)
    mixed_heads = jnp.einsum(
        "gqk,kd->gqd", weights_low, value_rows, preferred_element_type=jnp.float32
    )
    return (mixed_heads.astype(jnp.bfloat16), (row_peak + jnp.log(row_total))[..., 0])


def attend_back(query_rows, keys, value_rows, allowed, log_total, grad_mixed, score_scale):
    scores = (
        jnp.einsum("gqd,kd->gqk", query_rows, keys, preferred_element_type=jnp.float32)
        * score_scale
    )
    scores = jnp.where(allowed[None], scores, negative)
    soft_weights = jnp.exp(scores - log_total[..., None])
    weights_low = soft_weights.astype(jnp.bfloat16)
    grad_weights = jnp.einsum(
        "gqd,kd->gqk", grad_mixed, value_rows, preferred_element_type=jnp.float32
    )
    row_dot = jnp.sum(soft_weights * grad_weights, axis=-1, keepdims=True)
    grad_scores = (soft_weights * (grad_weights - row_dot)).astype(jnp.bfloat16)
    grad_queries = (
        jnp.einsum("gqk,kd->gqd", grad_scores, keys, preferred_element_type=jnp.float32)
        * score_scale
    )
    grad_keys = (
        jnp.einsum("gqk,gqd->kd", grad_scores, query_rows, preferred_element_type=jnp.float32)
        * score_scale
    )
    grad_values = jnp.einsum(
        "gqk,gqd->kd", weights_low, grad_mixed, preferred_element_type=jnp.float32
    )
    return (grad_queries, grad_keys, grad_values)


def reduce_over_fsdp(grad_list):
    return (
        lax.psum_scatter(
            grad_list[0].astype(jnp.bfloat16), "fsdp", scatter_dimension=0, tiled=True
        ).astype(jnp.float32),
        lax.psum_scatter(
            grad_list[1].astype(jnp.bfloat16), "fsdp", scatter_dimension=0, tiled=True
        ).astype(jnp.float32),
        lax.psum_scatter(
            grad_list[2].astype(jnp.bfloat16), "fsdp", scatter_dimension=0, tiled=True
        ).astype(jnp.float32),
        lax.psum_scatter(
            grad_list[3].astype(jnp.bfloat16), "fsdp", scatter_dimension=0, tiled=True
        ).astype(jnp.float32),
        lax.psum_scatter(
            grad_list[4].astype(jnp.bfloat16), "fsdp", scatter_dimension=0, tiled=True
        ).astype(jnp.float32),
        lax.psum_scatter(
            grad_list[5].astype(jnp.bfloat16), "fsdp", scatter_dimension=0, tiled=True
        ).astype(jnp.float32),
        lax.psum_scatter(
            grad_list[6].astype(jnp.bfloat16), "fsdp", scatter_dimension=1, tiled=True
        ).astype(jnp.float32),
        lax.psum_scatter(
            grad_list[7].astype(jnp.bfloat16), "fsdp", scatter_dimension=0, tiled=True
        ).astype(jnp.float32),
        lax.psum_scatter(
            grad_list[8].astype(jnp.bfloat16), "fsdp", scatter_dimension=0, tiled=True
        ).astype(jnp.float32),
        lax.psum_scatter(
            grad_list[9].astype(jnp.bfloat16), "fsdp", scatter_dimension=1, tiled=True
        ).astype(jnp.float32),
        lax.psum_scatter(
            grad_list[10].astype(jnp.bfloat16), "fsdp", scatter_dimension=1, tiled=True
        ).astype(jnp.float32),
        lax.psum_scatter(
            grad_list[11].astype(jnp.bfloat16), "fsdp", scatter_dimension=2, tiled=True
        ).astype(jnp.float32),
    )


def sum_over_context(grad_list):
    return (
        lax.psum(grad_list[0].astype(jnp.bfloat16), "context").astype(jnp.float32),
        lax.psum(grad_list[1].astype(jnp.bfloat16), "context").astype(jnp.float32),
        lax.psum(grad_list[2].astype(jnp.bfloat16), "context").astype(jnp.float32),
        lax.psum(grad_list[3].astype(jnp.bfloat16), "context").astype(jnp.float32),
        lax.psum(grad_list[4].astype(jnp.bfloat16), "context").astype(jnp.float32),
        lax.psum(grad_list[5].astype(jnp.bfloat16), "context").astype(jnp.float32),
        lax.psum(grad_list[6].astype(jnp.bfloat16), "context").astype(jnp.float32),
        lax.psum(grad_list[7].astype(jnp.bfloat16), "context").astype(jnp.float32),
        lax.psum(grad_list[8].astype(jnp.bfloat16), "context").astype(jnp.float32),
    )


def body(
    tokens,
    cotangent,
    doc_lengths,
    padding,
    expert_ids,
    norm1_gain,
    w_query,
    key_weight,
    value_weight,
    q_gain,
    k_gain,
    w_out,
    norm2_gain,
    w_router,
    w_gate,
    w_up,
    w_down,
):
    seq_count, span_len, model_width = tokens.shape
    context_count = lax.axis_size("context")
    context_index = lax.axis_index("context")
    gathered = (
        lax.all_gather(norm1_gain, "fsdp", axis=0, tiled=True),
        lax.all_gather(w_query, "fsdp", axis=0, tiled=True),
        lax.all_gather(key_weight, "fsdp", axis=0, tiled=True),
        lax.all_gather(value_weight, "fsdp", axis=0, tiled=True),
        lax.all_gather(q_gain, "fsdp", axis=0, tiled=True),
        lax.all_gather(k_gain, "fsdp", axis=0, tiled=True),
        lax.all_gather(w_out, "fsdp", axis=1, tiled=True),
        lax.all_gather(norm2_gain, "fsdp", axis=0, tiled=True),
        lax.all_gather(w_router, "fsdp", axis=0, tiled=True),
        lax.all_gather(w_gate, "fsdp", axis=1, tiled=True),
        lax.all_gather(w_up, "fsdp", axis=1, tiled=True),
        lax.all_gather(w_down, "fsdp", axis=2, tiled=True),
    )
    (
        norm1_full,
        query_full,
        key_full,
        value_full,
        qgain_full,
        kgain_full,
        out_full,
        norm2_full,
        router_full,
        gate_full,
        up_full,
        down_full,
    ) = gathered
    row_count = seq_count * span_len
    head_dim = qgain_full.shape[0]
    query_heads = query_full.shape[1] // head_dim
    key_heads = key_full.shape[1] // head_dim
    heads_per_group = query_heads // key_heads
    item_count = seq_count * key_heads
    score_scale = head_dim ** (-0.5)
    residual = tokens.astype(jnp.float32)
    grad_result = cotangent.astype(jnp.float32)
    positions = context_index * span_len + jnp.arange(span_len, dtype=jnp.int32)
    doc_index, starts = doc_layout(doc_lengths, positions)
    offsets = (positions[None, :] - starts).astype(jnp.float32)
    frequency = theta_base ** (-jnp.arange(head_dim // 2, dtype=jnp.float32) * 2.0 / head_dim)
    angles = offsets[:, :, None] * frequency
    cosine = jnp.cos(angles)[:, :, None, :]
    sine_table = jnp.sin(angles)[:, :, None, :]
    gain1 = norm1_full.astype(jnp.float32)
    normed1_low = rms_scale(residual, gain1).astype(jnp.bfloat16).reshape(row_count, model_width)
    query_proj = jnp.dot(normed1_low, query_full, preferred_element_type=jnp.float32).reshape(
        seq_count, span_len, query_heads, head_dim
    )
    key_projected = jnp.dot(normed1_low, key_full, preferred_element_type=jnp.float32).reshape(
        seq_count, span_len, key_heads, head_dim
    )
    value_low = (
        jnp.dot(normed1_low, value_full, preferred_element_type=jnp.float32)
        .astype(jnp.bfloat16)
        .reshape(seq_count, span_len, key_heads * head_dim)
    )
    query_gain = qgain_full.astype(jnp.float32)
    key_gain = kgain_full.astype(jnp.float32)
    query_prep = partial(head_prep, cosine, sine_table)
    query_rows = query_prep(query_proj, query_gain).astype(jnp.bfloat16)
    keys_low = (
        query_prep(key_projected, key_gain)
        .astype(jnp.bfloat16)
        .reshape(seq_count, span_len, key_heads * head_dim)
    )
    padding_low = padding.astype(jnp.bfloat16)
    halo_count = min((WINDOW + span_len - 2) // span_len, context_count - 1)
    key_parts_list = [keys_low]
    value_list = [value_low]
    padding_list = [padding_low]
    for distance in range(1, halo_count + 1):
        far_keys, far_values, far_padding = shifted(
            (keys_low, value_low, padding_low), "context", distance
        )
        key_parts_list.insert(0, far_keys)
        value_list.insert(0, far_values)
        padding_list.insert(0, far_padding)
    all_keys = jnp.concatenate(key_parts_list, axis=1)
    all_values = jnp.concatenate(value_list, axis=1)
    all_padding = jnp.concatenate(padding_list, axis=1)
    key_count = all_keys.shape[1]
    key_positions = (context_index - halo_count) * span_len + jnp.arange(key_count, dtype=jnp.int32)
    key_docs, key_starts = doc_layout(doc_lengths, key_positions)
    distance_grid = positions[:, None] - key_positions[None, :]
    near_enough = (distance_grid >= 0) & (distance_grid < WINDOW) & (key_positions >= 0)[None, :]
    allowed = (
        (doc_index[:, :, None] == key_docs[:, None, :])
        & near_enough[None]
        & ((all_padding[:, None, :] == 0) | (distance_grid == 0)[None])
    )
    query_items = (
        query_rows.reshape(seq_count, span_len, key_heads, heads_per_group, head_dim)
        .transpose(0, 2, 3, 1, 4)
        .reshape(item_count, heads_per_group, span_len, head_dim)
    )
    key_items = (
        all_keys.reshape(seq_count, key_count, key_heads, head_dim)
        .transpose(0, 2, 1, 3)
        .reshape(item_count, key_count, head_dim)
    )
    value_items = (
        all_values.reshape(seq_count, key_count, key_heads, head_dim)
        .transpose(0, 2, 1, 3)
        .reshape(item_count, key_count, head_dim)
    )
    item_masks = jnp.repeat(allowed, key_heads, axis=0)

    def forward_item(operands):
        return attend_block(operands[0], operands[1], operands[2], operands[3], score_scale)

    mixed_items, log_totals = lax.map(
        forward_item, (query_items, key_items, value_items, item_masks)
    )
    heads_low = (
        mixed_items.reshape(seq_count, key_heads, heads_per_group, span_len, head_dim)
        .transpose(0, 3, 1, 2, 4)
        .reshape(row_count, query_heads * head_dim)
    )
    attn_part = jnp.dot(heads_low, out_full, preferred_element_type=jnp.float32)
    branch = lax.psum(attn_part.astype(jnp.bfloat16), "tensor").astype(jnp.float32)
    residual2 = residual + branch.reshape(seq_count, span_len, model_width)
    gain2 = norm2_full.astype(jnp.float32)
    normed2_low = rms_scale(residual2, gain2).astype(jnp.bfloat16).reshape(row_count, model_width)
    logits = jnp.dot(normed2_low, router_full, preferred_element_type=jnp.float32)
    router_probs = jax.nn.softmax(logits, axis=-1)
    expert_count = router_probs.shape[1]
    top_count = expert_ids.shape[2]
    token_experts = expert_ids.reshape(row_count, top_count)
    chosen = token_experts[:, :, None] == jnp.arange(expert_count, dtype=jnp.int32)[None, None, :]
    picked = jnp.sum(jnp.where(chosen, router_probs[:, None, :], 0.0), axis=2)
    picked_total = jnp.sum(picked, axis=1, keepdims=True)
    route_gates = picked / picked_total
    kept_rows = (1 - padding).astype(jnp.float32).reshape(row_count)
    counts = jnp.sum(jnp.sum(chosen.astype(jnp.float32), axis=1) * kept_rows[:, None], axis=0)
    prob_sums = jnp.sum(router_probs * kept_rows[:, None], axis=0)
    counts_all, probs_all, kept_all = lax.psum(
        (counts, prob_sums, jnp.sum(kept_rows)), ("fsdp", "context")
    )
    load_share = counts_all / (kept_all * top_count)
    balance_loss = expert_count * jnp.sum(load_share * (probs_all / kept_all))
    expert_load = expert_count * load_share
    local_experts = gate_full.shape[0]
    capacity = seq_count * (2 * span_len * top_count // expert_count)
    assign_count = row_count * top_count
    onehot_rows = chosen.reshape(assign_count, expert_count).astype(jnp.int32)
    slot_ranks = jnp.sum((jnp.cumsum(onehot_rows, axis=0) - onehot_rows) * onehot_rows, axis=1)
    slot_index = token_experts.reshape(assign_count) * capacity + slot_ranks
    slot_total = expert_count * capacity
    slot_source = (
        jnp.zeros((slot_total,), jnp.int32)
        .at[slot_index]
        .set(jnp.arange(assign_count, dtype=jnp.int32))
    )
    slot_filled = jnp.zeros((slot_total,), jnp.bool_).at[slot_index].set(True)
    send_rows = jnp.where(
        slot_filled[:, None], normed2_low[slot_source // top_count], jnp.zeros((), jnp.bfloat16)
    )
    flat_grad = grad_result.reshape(row_count, model_width)
    weighted_grad = (
        (route_gates[:, :, None] * flat_grad[:, None, :])
        .astype(jnp.bfloat16)
        .reshape(assign_count, model_width)
    )
    send_grads = jnp.where(
        slot_filled[:, None], weighted_grad[slot_source], jnp.zeros((), jnp.bfloat16)
    )
    buffer_shape = (context_count, local_experts, capacity, model_width)
    got_rows, got_grads = (
        lax.all_to_all(
            send_rows.reshape(buffer_shape), "context", split_axis=0, concat_axis=0, tiled=True
        ),
        lax.all_to_all(
            send_grads.reshape(buffer_shape), "context", split_axis=0, concat_axis=0, tiled=True
        ),
    )
    gate_pre = jnp.einsum("sexd,edf->sexf", got_rows, gate_full, preferred_element_type=jnp.float32)
    up_pre = jnp.einsum("sexd,edf->sexf", got_rows, up_full, preferred_element_type=jnp.float32)
    sigmoid_gate = jax.nn.sigmoid(gate_pre)
    activated = gate_pre * sigmoid_gate
    hidden_low = (activated * up_pre).astype(jnp.bfloat16)
    expert_out = jnp.einsum(
        "sexf,efd->sexd", hidden_low, down_full, preferred_element_type=jnp.float32
    )
    grad_hidden = jnp.einsum(
        "sexd,efd->sexf", got_grads, down_full, preferred_element_type=jnp.float32
    )
    grad_down = jnp.einsum(
        "sexf,sexd->efd", hidden_low, got_grads, preferred_element_type=jnp.float32
    )
    grad_gate_pre = (
        grad_hidden * up_pre * sigmoid_gate * (1.0 + gate_pre * (1.0 - sigmoid_gate))
    ).astype(jnp.bfloat16)
    grad_up_pre = (grad_hidden * activated).astype(jnp.bfloat16)
    grad_gate = jnp.einsum(
        "sexd,sexf->edf", got_rows, grad_gate_pre, preferred_element_type=jnp.float32
    )
    grad_up = jnp.einsum(
        "sexd,sexf->edf", got_rows, grad_up_pre, preferred_element_type=jnp.float32
    )
    grad_rows = jnp.einsum(
        "sexf,edf->sexd", grad_gate_pre, gate_full, preferred_element_type=jnp.float32
    ) + jnp.einsum("sexf,edf->sexd", grad_up_pre, up_full, preferred_element_type=jnp.float32)
    back_out, back_grad = (
        lax.all_to_all(
            expert_out.astype(jnp.bfloat16), "context", split_axis=0, concat_axis=0, tiled=True
        ).astype(expert_out.dtype),
        lax.all_to_all(
            grad_rows.astype(jnp.bfloat16), "context", split_axis=0, concat_axis=0, tiled=True
        ).astype(grad_rows.dtype),
    )
    out_rows = back_out.reshape(slot_total, model_width)[slot_index].reshape(
        row_count, top_count, model_width
    )
    grad_in_rows = back_grad.reshape(slot_total, model_width)[slot_index].reshape(
        row_count, top_count, model_width
    )
    mixture_part = jnp.sum(route_gates[:, :, None] * out_rows, axis=1)
    gate_grad_part = jnp.sum(out_rows * flat_grad[:, None, :], axis=2)
    normed2_grad_part = jnp.sum(grad_in_rows, axis=1)
    expert_mix = lax.psum(mixture_part.astype(jnp.bfloat16), "tensor").astype(jnp.float32)
    result = residual2 + expert_mix.reshape(seq_count, span_len, model_width)
    grad_normed2, gate_grads = (
        lax.psum(normed2_grad_part.astype(jnp.bfloat16), "tensor").astype(jnp.float32),
        lax.psum(gate_grad_part.astype(jnp.bfloat16), "tensor").astype(jnp.float32),
    )
    grad_picked = (
        gate_grads - jnp.sum(gate_grads * route_gates, axis=1, keepdims=True)
    ) / picked_total
    grad_probs = jnp.sum(jnp.where(chosen, grad_picked[:, :, None], 0.0), axis=1)
    grad_logits = (
        router_probs * (grad_probs - jnp.sum(grad_probs * router_probs, axis=1, keepdims=True))
    ).astype(jnp.bfloat16)
    grad_router = jnp.einsum(
        "rd,re->de", normed2_low, grad_logits, preferred_element_type=jnp.float32
    )
    grad_normed2 = grad_normed2 + jnp.einsum(
        "re,de->rd", grad_logits, router_full, preferred_element_type=jnp.float32
    )
    norm2_value, norm2_back = jax.vjp(rms_scale, residual2, gain2)
    grad_res2_part, grad_gain2 = norm2_back(grad_normed2.reshape(seq_count, span_len, model_width))
    grad_res2 = grad_result + grad_res2_part
    grad_branch = grad_res2.reshape(row_count, model_width).astype(jnp.bfloat16)
    grad_out_proj = jnp.einsum(
        "rh,rd->hd", heads_low, grad_branch, preferred_element_type=jnp.float32
    )
    grad_heads = jnp.einsum(
        "rd,hd->rh", grad_branch, out_full, preferred_element_type=jnp.float32
    ).astype(jnp.bfloat16)
    grad_items = (
        grad_heads.reshape(seq_count, span_len, key_heads, heads_per_group, head_dim)
        .transpose(0, 2, 3, 1, 4)
        .reshape(item_count, heads_per_group, span_len, head_dim)
    )

    def backward_item(operands):
        return attend_back(
            operands[0],
            operands[1],
            operands[2],
            operands[3],
            operands[4],
            operands[5],
            score_scale,
        )

    grad_query_items, grad_key_items, grad_value_items = lax.map(
        backward_item, (query_items, key_items, value_items, item_masks, log_totals, grad_items)
    )
    grad_key_all = (
        grad_key_items.reshape(seq_count, key_heads, key_count, head_dim)
        .transpose(0, 2, 1, 3)
        .reshape(seq_count, key_count, key_heads * head_dim)
    )
    grad_value_all = (
        grad_value_items.reshape(seq_count, key_heads, key_count, head_dim)
        .transpose(0, 2, 1, 3)
        .reshape(seq_count, key_count, key_heads * head_dim)
    )
    own_start = halo_count * span_len
    grad_keys = grad_key_all[:, own_start:]
    grad_values = grad_value_all[:, own_start:]
    for distance in range(1, halo_count + 1):
        lower_row = (halo_count - distance) * span_len
        came_keys, came_values = (
            shifted(
                grad_key_all[:, lower_row : lower_row + span_len].astype(jnp.bfloat16),
                "context",
                -distance,
            ).astype(jnp.float32),
            shifted(
                grad_value_all[:, lower_row : lower_row + span_len].astype(jnp.bfloat16),
                "context",
                -distance,
            ).astype(jnp.float32),
        )
        grad_keys = grad_keys + came_keys
        grad_values = grad_values + came_values
    grad_queries = (
        grad_query_items.reshape(seq_count, key_heads, heads_per_group, span_len, head_dim)
        .transpose(0, 3, 1, 2, 4)
        .reshape(seq_count, span_len, query_heads, head_dim)
    )
    query_value, query_back = jax.vjp(query_prep, query_proj, query_gain)
    grad_query_proj, grad_query_gain = query_back(grad_queries)
    key_value, key_back = jax.vjp(query_prep, key_projected, key_gain)
    grad_key_proj, grad_key_gain = key_back(
        grad_keys.reshape(seq_count, span_len, key_heads, head_dim)
    )
    grad_query_low = grad_query_proj.reshape(row_count, query_heads * head_dim).astype(jnp.bfloat16)
    grad_key_low = grad_key_proj.reshape(row_count, key_heads * head_dim).astype(jnp.bfloat16)
    grad_value_low = grad_values.reshape(row_count, key_heads * head_dim).astype(jnp.bfloat16)
    grad_query = jnp.einsum(
        "rd,rh->dh", normed1_low, grad_query_low, preferred_element_type=jnp.float32
    )
    grad_key = jnp.einsum(
        "rd,rh->dh", normed1_low, grad_key_low, preferred_element_type=jnp.float32
    )
    grad_value = jnp.einsum(
        "rd,rh->dh", normed1_low, grad_value_low, preferred_element_type=jnp.float32
    )
    input_part = jnp.einsum(
        "rh,dh->rd", grad_query_low, query_full, preferred_element_type=jnp.float32
    )
    input_part = input_part + jnp.einsum(
        "rh,dh->rd", grad_key_low, key_full, preferred_element_type=jnp.float32
    )
    input_part = input_part + jnp.einsum(
        "rh,dh->rd", grad_value_low, value_full, preferred_element_type=jnp.float32
    )
    grad_normed1, grad_query_gain, grad_key_gain = (
        lax.psum(input_part.astype(jnp.bfloat16), "tensor").astype(jnp.float32),
        lax.psum(grad_query_gain.astype(jnp.bfloat16), "tensor").astype(jnp.float32),
        lax.psum(grad_key_gain.astype(jnp.bfloat16), "tensor").astype(jnp.float32),
    )
    norm1_value, norm1_back = jax.vjp(rms_scale, residual, gain1)
    grad_res1_part, grad_gain1 = norm1_back(grad_normed1.reshape(seq_count, span_len, model_width))
    grad_input = grad_res2 + grad_res1_part
    dense_grads = (
        grad_gain1,
        grad_query,
        grad_key,
        grad_value,
        grad_query_gain,
        grad_key_gain,
        grad_out_proj,
        grad_gain2,
        grad_router,
    )
    expert_grads = (grad_gate, grad_up, grad_down)
    summed = sum_over_context(dense_grads)
    final_grads = tuple(reduce_over_fsdp(tuple(summed) + expert_grads))
    return (
        result,
        balance_loss,
        expert_load,
        grad_input,
        final_grads[0],
        final_grads[1],
        final_grads[2],
        final_grads[3],
        final_grads[4],
        final_grads[5],
        final_grads[6],
        final_grads[7],
        final_grads[8],
        final_grads[9],
        final_grads[10],
        final_grads[11],
    )


def solution(mesh):
    in_specs = (
        P("fsdp", "context", None),
        P("fsdp", "context", None),
        P("fsdp", None),
        P("fsdp", "context"),
        P("fsdp", "context", None),
        P("fsdp"),
        P("fsdp", "tensor"),
        P("fsdp", "tensor"),
        P("fsdp", "tensor"),
        P("fsdp"),
        P("fsdp"),
        P("tensor", "fsdp"),
        P("fsdp"),
        P("fsdp", None),
        P("context", "fsdp", "tensor"),
        P("context", "fsdp", "tensor"),
        P("context", "tensor", "fsdp"),
    )
    out_specs = (
        P("fsdp", "context", None),
        P(),
        P(),
        P("fsdp", "context", None),
        P("fsdp"),
        P("fsdp", "tensor"),
        P("fsdp", "tensor"),
        P("fsdp", "tensor"),
        P("fsdp"),
        P("fsdp"),
        P("tensor", "fsdp"),
        P("fsdp"),
        P("fsdp", None),
        P("context", "fsdp", "tensor"),
        P("context", "fsdp", "tensor"),
        P("context", "tensor", "fsdp"),
    )
    return jax.shard_map(body, mesh=mesh, in_specs=in_specs, out_specs=out_specs, check_vma=False)
```

profile of v0, /device:TPU:1, one launch (start us, length us, event | category | flops | bytes accessed | tf_op | source)
XLA Modules:
  0.0 1538.5 jit_solution(15583226195931768917)
XLA Ops:
  64.8 13.5 collective-permute-start.8
  127.3 14.9 collective-permute-start.16
  175.9 57.8 %all-gather.16.cloned.1.call-done = bf16[2048,2048]{1,0:T(8,128)(2,1)} async-done(((bf16[2048,512]{1,0:T(8,128)(2,1)}), bf16[2048,2048]{1,0:T(8,128)(2,1)}) %all-gather.16.cloned.1.call-update) | async-done | bytes 8388624 | tf_op jit(solution)/shard_map/all_gather | solution.py:179
  249.5 18.0 %reduce-window.18 = s32[64,8,128]{2,1,0:T(8,128)S(1)} reduce-window(s32[64,8,128]{2,1,0:T(8,128)S(1)} %fusion.119, s32[]{:T(128)} %copy.372), window={size=1x1x128 pad=0_0x0_0x127_0}, to_apply=%region_17.18 | reduce-window | flops 8323072 | bytes 524292 | tf_op jit(solution)/shard_map/reduce-window
  291.3 10.9 gather_fusion
  304.7 19.1 %gather_fusion.2 = bf16[2048,2048]{1,0:T(8,128)(2,1)} fusion(bf16[1024,2048]{1,0:T(8,128)(2,1)} %fusion.43, s32[2048]{0:T(1024)S(1)} %get-tuple-element.233), kind=kCustom, calls=%fused_computation.2 | custom fusion | bytes 16785408 | tf_op jit(solution)/shard_map/gather | solution.py:337
  323.8 11.5 broadcast_select_fusion
  342.8 96.5 %all-to-all-done = bf16[16,4,32,2048]{3,2,1,0:T(8,128)(2,1)} async-done(((bf16[16,4,32,2048]{3,2,1,0:T(8,128)(2,1)}), bf16[16,4,32,2048]{3,2,1,0:T(8,128)(2,1)}, u32[]{:S(2)}, u32[]{:S(2)}) %all-to-all-start) | async-done | bytes 8388640 | tf_op jit(solution)/shard_map/all_to_all | solution.py:341
  448.9 11.5 fusion.50
  460.4 11.3 fusion.52
  471.7 75.5 %all-to-all-done.2 = bf16[16,4,32,2048]{3,2,1,0:T(8,128)(2,1)} async-done(((bf16[16,4,32,2048]{3,2,1,0:T(8,128)(2,1)}), bf16[16,4,32,2048]{3,2,1,0:T(8,128)(2,1)}, u32[]{:S(2)}, u32[]{:S(2)}) %all-to-all-start.2) | async-done | bytes 8388640 | tf_op jit(solution)/shard_map/all_to_all | solution.py:344
  547.2 14.5 fusion.71
  561.7 11.3 convert_bitcast_fusion
  581.3 11.0 all-to-all-start.1
  592.3 13.7 fusion.54
  606.0 12.2 fusion.42
  626.6 63.2 %all-to-all-done.1 = bf16[16,4,32,2048]{3,2,1,0:T(8,128)(2,1)} async-done(((bf16[16,4,32,2048]{3,2,1,0:T(8,128)(2,1)}), bf16[16,4,32,2048]{3,2,1,0:T(8,128)(2,1)}, u32[]{:S(2)}, u32[]{:S(2)}) %all-to-all-start.1) | async-done | bytes 8388640 | tf_op jit(solution)/shard_map/all_to_all | solution.py:376
  700.2 11.3 bitcast_convert_fusion.4
  711.5 15.2 gather_fusion.1
  738.8 77.8 %all-to-all-done.3 = bf16[16,4,32,2048]{3,2,1,0:T(8,128)(2,1)} async-done(((bf16[16,4,32,2048]{3,2,1,0:T(8,128)(2,1)}), bf16[16,4,32,2048]{3,2,1,0:T(8,128)(2,1)}, u32[]{:S(2)}, u32[]{:S(2)}) %all-to-all-start.3) | async-done | bytes 8388640 | tf_op jit(solution)/shard_map/all_to_all | solution.py:379
  816.6 11.3 bitcast_convert_fusion.3
  827.9 14.7 gather_fusion.3
  849.9 35.0 %all-reduce.24.cloned.1.call-done = bf16[128,2048]{1,0:T(8,128)(2,1)} async-done(((bf16[128,2048]{1,0:T(8,128)(2,1)}), bf16[128,2048]{1,0:T(8,128)(2,1)}) %all-reduce.24.cloned.1.call-update) | async-done | bytes 524304 | tf_op jit(solution)/shard_map/psum | solution.py:395
  894.7 19.7 %while.27 = (s32[]{:T(128)}, f32[2,8,128,128]{3,2,1,0:T(8,128)}, f32[2,1152,128]{1,2,0:T(8,128)}, f32[2,1152,128]{1,2,0:T(8,128)}, pred[2,128,1152]{2,1,0:T(8,12...) while((s32[]{:T(128)}, f32[2,8,128,128]{3,2,1,0:T(8,128)}, ...), condition=%wide.region_42.43_spmd, body=%wide.region_40.42_spmd.sunk | while | flops 1520843776 | bytes 41853060 | solution.py:438
  1003.1 11.1 bitcast_convert_fusion.2
  1014.3 11.0 bitcast_convert_fusion.1
  1025.5 69.0 %reduce-scatter.21.cloned.1.call-done = bf16[2048,512]{1,0:T(8,128)(2,1)} async-done(((bf16[2048,2048]{1,0:T(8,128)(2,1)}), bf16[2048,512]{1,0:T(8,128)(2,1)}) %reduce-scatter.21.cloned.1.call-update) | async-done | bytes 2097168 | tf_op jit(solution)/shard_map/reduce_scatter | solution.py:115
  1094.5 82.7 %reduce-scatter.15.cloned.1.call-done = bf16[512,2048]{1,0:T(8,128)(2,1)} async-done(((bf16[2048,2048]{1,0:T(8,128)(2,1)}), bf16[512,2048]{1,0:T(8,128)(2,1)}) %reduce-scatter.15.cloned.1.call-update) | async-done | bytes 2097168 | tf_op jit(solution)/shard_map/reduce_scatter | solution.py:100
  1179.2 151.5 %all-reduce.10 = (f32[64]{0:T(128)S(1)}, f32[]{:T(128)}, f32[64]{0:T(128)S(1)}) all-reduce(f32[64]{0:T(128)S(1)} %copy-done.78, f32[]{:T(128)} %convert_reduce_fusion.2, f32[64]{0:T(128)S(1)} %copy-done.77), channel_id=1, replica_groups=mesh['fsdp'=4,'context'=16,'tensor'=2] {'fsdp','context'}, use_global_device_ids=true, to_apply=%region_26.27 | all-reduce | flops 129 | bytes 1032 | tf_op jit(solution)/shard_map/psum | solution.py:308
  1342.0 32.7 %all-reduce.15 = (bf16[32]{0:T(256)(128)(2,1)S(1)}, bf16[32]{0:T(256)(128)(2,1)S(1)}) all-reduce(bf16[32]{0:T(256)(128)(2,1)S(1)} %dynamic-slice.5, bf16[32]{0:T(256)(128)(2,1)S(1)} %dynamic-slice.7), channel_id=1, replica_groups=mesh['fsdp'=4,'context'=16,'tensor'=2] {'tensor'}, use_global_device_ids=true, to_apply=%region_57.58 | all-reduce | flops 64 | bytes 256 | tf_op jit(solution)/shard_map/psum | solution.py:504
  1374.7 28.6 %all-reduce.11 = (bf16[512]{0:T(512)(128)(2,1)S(1)}, bf16[32]{0:T(256)(128)(2,1)S(1)}, bf16[32]{0:T(256)(128)(2,1)S(1)}, bf16[512]{0:T(512)(128)(2,1)S(1)}) all-reduce(bf16[512]{0:T(512)(128)(2,1)S(1)} %dynamic-slice.3, bf16[32]{0:T(256)(128)(2,1)S(1)} %get-tuple-element.184, ...), channel_id=1, replica_groups=mesh['fsdp'=4,'context'=16,'tensor'=2] {'context'}, use_global_device_ids=true, to_apply=%region_48.49 | all-reduce | flops 1088 | bytes 4352 | tf_op jit(solution)/shard_map/psum | solution.py:138
  1418.5 100.0 %all-reduce.26.cloned.1.call-done = (bf16[512,2048]{1,0:T(8,128)(2,1)}, bf16[512,256]{1,0:T(8,128)(2,1)}, bf16[512,256]{1,0:T(8,128)(2,1)}, bf16[2048,512]{1,0:T(8,128)(2,1)}, bf16[512,64]{0,1:T(8,128)(2,1)}) async-done(((bf16[512,2048]{1,0:T(8,128)(2,1)}, bf16[512,256]{1,0:T(8,128)(2,1)}, bf16[512,256]{1,0:T(8,128)(2,1)}, bf16[2048,512]{1,0:T(8,128)(2,1)}, bf16[512,64]{0,1:T(8,128)(2,1)}), ...) | async-done | bytes 4784144 | tf_op jit(solution)/shard_map/psum | solution.py:139
  (533 shorter events, 407.1 us)
Async XLA Ops:
  7.3 54.1 %all-gather.12.cloned.1.call-start = ((), (), s32[]{:S(2)}) async-start(), calls=%async_computation.13 | async-start | bytes 1310720 | tf_op jit(solution)/shard_map/all_gather | solution.py:175
  8.0 70.4 %all-gather.14.cloned.1.call-start = ((), (), s32[]{:S(2)}) async-start(), calls=%async_computation.14 | async-start | bytes 1310720 | tf_op jit(solution)/shard_map/all_gather | solution.py:176
  8.7 150.6 %all-gather.10.cloned.1.call-start = ((), (), s32[]{:S(2)}) async-start(), calls=%async_computation.12 | async-start | bytes 10485760 | tf_op jit(solution)/shard_map/all_gather | solution.py:174
  9.5 224.3 %all-gather.16.cloned.1.call-start = ((), (), s32[]{:S(2)}) async-start(), calls=%async_computation.15 | async-start | bytes 10485760 | tf_op jit(solution)/shard_map/all_gather | solution.py:179
  10.8 50.2 %collective-permute-start.7 = (bf16[1,128]{1,0:T(2,128)(2,1)S(1)}, bf16[1,128]{1,0:T(2,128)(2,1)S(1)}, u32[]{:S(2)}, u32[]{:S(2)}) collective-permute-start(bf16[1,128]{1,0:T(2,128)(2,1)S(1)} %get-tuple-element.240), channel_id=1, source_target_pairs={{0,2},{2,4},{4,6},{6,8},{8,10},{10,12},{12,14},{14,16},{16,18},{18... | collective-permute-start | bytes 776 | tf_op jit(solution)/shard_map/ppermute | solution.py:19
  15.1 45.8 %collective-permute-start.6 = (bf16[1,128]{1,0:T(2,128)(2,1)S(1)}, bf16[1,128]{1,0:T(2,128)(2,1)S(1)}, u32[]{:S(2)}, u32[]{:S(2)}) collective-permute-start(bf16[1,128]{1,0:T(2,128)(2,1)S(1)} %get-tuple-element.240), channel_id=1, source_target_pairs={{0,4},{2,6},{4,8},{6,10},{8,12},{10,14},{12,16},{14,18},{16,20},{1... | collective-permute-start | bytes 776 | tf_op jit(solution)/shard_map/ppermute | solution.py:19
  20.4 40.5 %collective-permute-start.5 = (bf16[1,128]{1,0:T(2,128)(2,1)S(1)}, bf16[1,128]{1,0:T(2,128)(2,1)S(1)}, u32[]{:S(2)}, u32[]{:S(2)}) collective-permute-start(bf16[1,128]{1,0:T(2,128)(2,1)S(1)} %get-tuple-element.240), channel_id=1, source_target_pairs={{0,6},{2,8},{4,10},{6,12},{8,14},{10,16},{12,18},{14,20},{16,22},{... | collective-permute-start | bytes 776 | tf_op jit(solution)/shard_map/ppermute | solution.py:19
  23.9 36.9 %collective-permute-start.4 = (bf16[1,128]{1,0:T(2,128)(2,1)S(1)}, bf16[1,128]{1,0:T(2,128)(2,1)S(1)}, u32[]{:S(2)}, u32[]{:S(2)}) collective-permute-start(bf16[1,128]{1,0:T(2,128)(2,1)S(1)} %get-tuple-element.240), channel_id=1, source_target_pairs={{0,8},{2,10},{4,12},{6,14},{8,16},{10,18},{12,20},{14,22},{16,24},... | collective-permute-start | bytes 776 | tf_op jit(solution)/shard_map/ppermute | solution.py:19
  30.2 256.6 %all-reduce.22.cloned.1.call-start = ((), (), s32[]{:S(2)}) async-start(), calls=%async_computation.16 | async-start | bytes 1048576 | tf_op jit(solution)/shard_map/psum | solution.py:292
  64.8 24.5 %collective-permute-start.8 = (bf16[1,128,256]{2,1,0:T(8,128)(2,1)S(1)}, bf16[1,128,256]{2,1,0:T(8,128)(2,1)S(1)}, u32[]{:S(2)}, u32[]{:S(2)}) collective-permute-start(bf16[1,128,256]{2,1,0:T(8,128)(2,1)S(1)} %convert_element_type.363), channel_id=1, source_target_pairs={{0,16},{2,18},{4,20},{6,22},{8,24},{10,26},{12,28},{14,30},{1,17},... | collective-permute-start | bytes 196616 | tf_op jit(solution)/shard_map/ppermute | solution.py:19
  80.1 79.0 %collective-permute-start.23 = (bf16[1,128,256]{2,1,0:T(8,128)(2,1)S(1)}, bf16[1,128,256]{2,1,0:T(8,128)(2,1)S(1)}, u32[]{:S(2)}, u32[]{:S(2)}) collective-permute-start(bf16[1,128,256]{2,1,0:T(8,128)(2,1)S(1)} %fusion.87), channel_id=1, source_target_pairs={{0,2},{2,4},{4,6},{6,8},{8,10},{10,12},{12,14},{14,16},{16,18},{18... | collective-permute-start | bytes 196616 | tf_op jit(solution)/shard_map/ppermute | solution.py:19
  81.4 77.7 %collective-permute-start.22 = (bf16[1,128,256]{2,1,0:T(8,128)(2,1)S(1)}, bf16[1,128,256]{2,1,0:T(8,128)(2,1)S(1)}, u32[]{:S(2)}, u32[]{:S(2)}) collective-permute-start(bf16[1,128,256]{2,1,0:T(8,128)(2,1)S(1)} %fusion.87), channel_id=1, source_target_pairs={{0,4},{2,6},{4,8},{6,10},{8,12},{10,14},{12,16},{14,18},{16,20},{1... | collective-permute-start | bytes 196616 | tf_op jit(solution)/shard_map/ppermute | solution.py:19
  82.7 76.3 %collective-permute-start.21 = (bf16[1,128,256]{2,1,0:T(8,128)(2,1)S(1)}, bf16[1,128,256]{2,1,0:T(8,128)(2,1)S(1)}, u32[]{:S(2)}, u32[]{:S(2)}) collective-permute-start(bf16[1,128,256]{2,1,0:T(8,128)(2,1)S(1)} %fusion.87), channel_id=1, source_target_pairs={{0,6},{2,8},{4,10},{6,12},{8,14},{10,16},{12,18},{14,20},{16,22},{... | collective-permute-start | bytes 196616 | tf_op jit(solution)/shard_map/ppermute | solution.py:19
  86.4 72.6 %collective-permute-start.20 = (bf16[1,128,256]{2,1,0:T(8,128)(2,1)S(1)}, bf16[1,128,256]{2,1,0:T(8,128)(2,1)S(1)}, u32[]{:S(2)}, u32[]{:S(2)}) collective-permute-start(bf16[1,128,256]{2,1,0:T(8,128)(2,1)S(1)} %fusion.87), channel_id=1, source_target_pairs={{0,8},{2,10},{4,12},{6,14},{8,16},{10,18},{12,20},{14,22},{16,24},... | collective-permute-start | bytes 196616 | tf_op jit(solution)/shard_map/ppermute | solution.py:19
  239.5 209.5 %all-gather.20.cloned.1.call-start = ((), (), s32[]{:S(2)}) async-start(), calls=%async_computation.18 | async-start | bytes 7864320 | tf_op jit(solution)/shard_map/all_gather | solution.py:183
  240.1 220.3 %all-gather.18.cloned.1.call-start = ((), (), s32[]{:S(2)}) async-start(), calls=%async_computation.17 | async-start | bytes 7864320 | tf_op jit(solution)/shard_map/all_gather | solution.py:182
  335.3 103.9 %all-to-all-start = ((bf16[16,4,32,2048]{3,2,1,0:T(8,128)(2,1)}), bf16[16,4,32,2048]{3,2,1,0:T(8,128)(2,1)}, u32[]{:S(2)}, u32[]{:S(2)}) async-start(bf16[16,4,32,2048]{3,2,1,0:T(8,128)(2,1)} %get-tuple-element.232), calls=%async_computation | async-start | bytes 16777216 | tf_op jit(solution)/shard_map/all_to_all | solution.py:341
  342.0 129.7 %all-gather.22.cloned.1.call-start = ((), (), s32[]{:S(2)}) async-start(), calls=%async_computation.19 | async-start | bytes 7864320 | tf_op jit(solution)/shard_map/all_gather | solution.py:184
  439.2 108.0 %all-to-all-start.2 = ((bf16[16,4,32,2048]{3,2,1,0:T(8,128)(2,1)}), bf16[16,4,32,2048]{3,2,1,0:T(8,128)(2,1)}, u32[]{:S(2)}, u32[]{:S(2)}) async-start(bf16[16,4,32,2048]{3,2,1,0:T(8,128)(2,1)} %get-tuple-element.231), calls=%async_computation.2 | async-start | bytes 16777216 | tf_op jit(solution)/shard_map/all_to_all | solution.py:344
  581.3 108.5 %all-to-all-start.1 = ((bf16[16,4,32,2048]{3,2,1,0:T(8,128)(2,1)}), bf16[16,4,32,2048]{3,2,1,0:T(8,128)(2,1)}, u32[]{:S(2)}, u32[]{:S(2)}) async-start(bf16[16,4,32,2048]{3,2,1,0:T(8,128)(2,1)} %copy.197), calls=%async_computation.1 | async-start | bytes 16777216 | tf_op jit(solution)/shard_map/all_to_all | solution.py:376
  689.8 126.8 %all-to-all-start.3 = ((bf16[16,4,32,2048]{3,2,1,0:T(8,128)(2,1)}), bf16[16,4,32,2048]{3,2,1,0:T(8,128)(2,1)}, u32[]{:S(2)}, u32[]{:S(2)}) async-start(bf16[16,4,32,2048]{3,2,1,0:T(8,128)(2,1)} %copy.200), calls=%async_computation.3 | async-start | bytes 16777216 | tf_op jit(solution)/shard_map/all_to_all | solution.py:379
  700.1 184.9 %all-reduce.24.cloned.1.call-start = ((), (), s32[]{:S(2)}) async-start(), calls=%async_computation.20 | async-start | bytes 1048576 | tf_op jit(solution)/shard_map/psum | solution.py:395
  849.1 176.3 %reduce-scatter.23.cloned.1.call-start = ((), (), s32[]{:S(2)}) async-start(), calls=%async_computation.28 | async-start | bytes 327680 | tf_op jit(solution)/shard_map/reduce_scatter | solution.py:121
  930.6 94.9 %reduce-scatter.19.cloned.1.call-start = ((), (), s32[]{:S(2)}) async-start(), calls=%async_computation.26 | async-start | bytes 1310720 | tf_op jit(solution)/shard_map/reduce_scatter | solution.py:106
  937.7 87.8 %reduce-scatter.17.cloned.1.call-start = ((), (), s32[]{:S(2)}) async-start(), calls=%async_computation.25 | async-start | bytes 1310720 | tf_op jit(solution)/shard_map/reduce_scatter | solution.py:103
  965.1 129.4 %reduce-scatter.21.cloned.1.call-start = ((), (), s32[]{:S(2)}) async-start(), calls=%async_computation.27 | async-start | bytes 10485760 | tf_op jit(solution)/shard_map/reduce_scatter | solution.py:115
  970.8 206.5 %reduce-scatter.15.cloned.1.call-start = ((), (), s32[]{:S(2)}) async-start(), calls=%async_computation.24 | async-start | bytes 10485760 | tf_op jit(solution)/shard_map/reduce_scatter | solution.py:100
  984.4 349.3 %all-reduce.28.cloned.1.call-start = ((), (), s32[]{:S(2)}) async-start(), calls=%async_computation.30 | async-start | bytes 2097152 | tf_op jit(solution)/shard_map/psum | solution.py:392
  992.7 415.7 %reduce-scatter.13.cloned.1.call-start = ((), (), s32[]{:S(2)}) async-start(), calls=%async_computation.23 | async-start | bytes 7864320 | tf_op jit(solution)/shard_map/reduce_scatter | solution.py:130
  1002.8 409.1 %reduce-scatter.9.cloned.1.call-start = ((), (), s32[]{:S(2)}) async-start(), calls=%async_computation.21 | async-start | bytes 7864320 | tf_op jit(solution)/shard_map/reduce_scatter | solution.py:124
  1014.2 401.0 %reduce-scatter.11.cloned.1.call-start = ((), (), s32[]{:S(2)}) async-start(), calls=%async_computation.22 | async-start | bytes 7864320 | tf_op jit(solution)/shard_map/reduce_scatter | solution.py:127
  1025.4 493.1 %all-reduce.26.cloned.1.call-start = ((), (), s32[]{:S(2)}) async-start(), calls=%async_computation.29 | async-start | bytes 9568256 | tf_op jit(solution)/shard_map/psum | solution.py:139
  (117 other events, 4459.5 us)
Sparse Core Ops, SparseCore 0:
  9.8 26.2 all-gather.11
  37.7 24.2 all-gather.13
  63.7 84.3 all-gather.9
  149.6 84.0 all-gather.15
  239.6 25.7 all-reduce.21
  267.0 66.6 all-gather.19
  335.6 66.3 all-gather.17
  403.7 66.3 all-gather.21
  849.2 35.6 all-reduce.23
  930.7 26.1 reduce-scatter.22
  960.0 24.0 reduce-scatter.18
  986.9 23.2 reduce-scatter.16
  1012.9 81.6 reduce-scatter.20
  1097.0 80.2 reduce-scatter.14
  1180.3 25.3 all-reduce.27
  1208.0 64.9 reduce-scatter.12
  1275.2 63.6 reduce-scatter.8
  1341.2 64.0 reduce-scatter.10
  1409.3 109.1 all-reduce.25
where the time goes:
time: 1550 us; the launch traced here: 1540 us
  waiting for transfers between devices  696 us (45%)
  blocking collectives  259 us (17%)
  matrix products  173 us (11%)
  starting transfers between devices  166 us (11%)
  other arithmetic  122 us (8%)
  local copies, waits for them, and re-layouts  101 us (7%)
  between operations  21.2 us (1%)
    psum x1, blocking collectives, body(): lax.psum((counts, prob_sums, jnp.sum(kept_rows)), ('fsdp', 'context'))  151 us
    ppermute x40, starting transfers between devices, shifted(): return lax.ppermute(x, axis, pairs)  127 us
    psum x1, waiting for transfers between devices, sum_over_context(): lax.psum(grad_list[1].astype(jnp.bfloat16), 'context').astype(jnp.float32)  100 us
    all_to_all x1, waiting for transfers between devices, body(): lax.all_to_all(send_rows.reshape(buffer_shape), 'context', split_axis=0,...  96.5 us
    reduce_scatter x1, waiting for transfers between devices, reduce_over_fsdp(): lax.psum_scatter(grad_list[1].astype(jnp.bfloat16), 'fsdp', scatter_dimen...  82.7 us
    all_to_all x1, waiting for transfers between devices, body(): lax.all_to_all(grad_rows.astype(jnp.bfloat16), 'context', split_axis=0, c...  77.8 us
    all_to_all x1, waiting for transfers between devices, body(): lax.all_to_all(send_grads.reshape(buffer_shape), 'context', split_axis=0,...  75.5 us
    reduce_scatter x1, waiting for transfers between devices, reduce_over_fsdp(): lax.psum_scatter(grad_list[6].astype(jnp.bfloat16), 'fsdp', scatter_dimen...  69 us
  transfers between devices with their start and end apart: 63, of which 31 were waited for; matrix products, arithmetic and copies ran while one was open for 18% of the time, Pallas kernels for 0%

commit v1 on v0

v1 whole, which is shorter than its diff:
```python
import jax
import jax.numpy as jnp
from jax import lax
from jax.experimental import pallas as pl
from jax.experimental.pallas import tpu as pltpu
from jax.sharding import PartitionSpec as P

WINDOW = 1024
SIDE = 4
HALF = 64
QUERY_BLOCK = 256
SLOTS = 32
EXTRA = 128
SMALL = 16

epsilon = 1e-06
theta_base = 1000000.0
negative = -1e30
f32 = jnp.float32
bf16 = jnp.bfloat16
vmem_limit = 56 * 1024 * 1024
whole = pl.BlockSpec(memory_space=pltpu.VMEM)
scalars = pl.BlockSpec(memory_space=pltpu.SMEM)


def call(kernel, in_specs, out_shape, flops=10**6, moved=10**6, **rest):
    if in_specs is not None:
        rest["in_specs"] = in_specs
    return pl.pallas_call(
        kernel,
        out_shape=[jax.ShapeDtypeStruct(shape, kind) for shape, kind in out_shape],
        compiler_params=pltpu.CompilerParams(vmem_limit_bytes=vmem_limit),
        cost_estimate=pl.CostEstimate(flops=flops, bytes_accessed=moved, transcendentals=0),
        **rest,
    )


def dot_nt(left, right):
    return lax.dot_general(left, right, (((1,), (1,)), ((), ())), preferred_element_type=f32)


def dot_tn(left, right):
    return lax.dot_general(left, right, (((0,), (0,)), ((), ())), preferred_element_type=f32)


def dot_nn(left, right):
    return jnp.dot(left, right, preferred_element_type=f32)


def join(parts, axis=0):
    return jnp.concatenate(parts, axis=axis)


def ring_moves(axis, target):
    forward = []
    backward = []
    count = lax.axis_size(axis)
    for i in range(count):
        for core, sign in ((0, 1), (1, -1)):
            forward.append((2 * i + core, 2 * target(i, sign) + core))
            backward.append((2 * i + core, 2 * target(i, -sign) + core))

    def move(pairs):
        return lambda value: lax.ppermute(value, (axis, "tensor"), pairs)

    return move(forward), move(backward)


def moves_z():
    return ring_moves("context", lambda i, step: (i // SIDE) * SIDE + (i + step) % SIDE)


def moves_x():
    return ring_moves("context", lambda i, step: (i + SIDE * step) % (SIDE * SIDE))


def moves_y():
    return ring_moves("fsdp", lambda i, step: (i + step) % SIDE)


def other_core(value):
    return lax.ppermute(value, "tensor", [(0, 1), (1, 0)])


def after(value, *events):
    return lax.optimization_barrier((value, *events))[0]


def ring_gather(value, moves):
    behind = moves[0](value)
    ahead = moves[1](value)
    far = moves[0](behind)
    return [value, ahead, far, behind]


def add_low(left, right):
    return (left.astype(f32) + right.astype(f32)).astype(bf16)


def low_sum(terms):
    return sum(term.astype(f32) for term in terms).astype(bf16)


def across(value, step):
    pairs = [(i, i ^ (SIDE * step)) for i in range(SIDE * SIDE)]
    return lax.ppermute(value, "context", pairs)


def along_z(value, step):
    pairs = [(i, (i // SIDE) * SIDE + (i + step) % SIDE) for i in range(SIDE * SIDE)]
    return lax.ppermute(value, "context", pairs)


def ring_scatter(parts, moves):
    passing = moves[0](parts[2])
    from_ahead = moves[1](parts[3])
    from_behind = moves[0](add_low(parts[1], passing))
    return parts[0], from_behind, from_ahead


def together(*values):
    return lax.optimization_barrier(values)


def stack_kernel(a, b, c, d, result):
    for i, part in enumerate((a, b, c, d)):
        result[i] = part[...]


def stack(parts):
    shape = parts[0].shape
    return call(stack_kernel, [whole] * 4, [((4,) + shape, bf16)])(*parts)[0]


def two_gathers(left, right, left_moves, right_moves, events=(), last=()):
    left_behind = left_moves[0](left)
    left_ahead = left_moves[1](left)
    right_behind = right_moves[0](right)
    right_ahead = right_moves[1](right)
    left_behind, left_ahead, right_behind, right_ahead = together(
        left_behind, left_ahead, right_behind, right_ahead, *events
    )[:4]
    left_far = left_moves[0](left_behind)
    right_far = right_moves[0](right_behind)
    left_far, right_far = together(left_far, right_far, *last)[:2]
    return [left, left_ahead, left_far, left_behind], [right, right_ahead, right_far, right_behind]


def plane_gather(first, second, events=((), (), (), ())):
    first_near, second_near = two_gathers(first, second, moves_z(), moves_x(), *events[:2])
    first_pieces, second_pieces = two_gathers(
        stack(first_near), stack(second_near), moves_x(), moves_z(), *events[2:]
    )
    return first_pieces + second_pieces


def unstack_kernel(a, b, c, r0, r1, r2, r3):
    for i, part in enumerate((r0, r1, r2, r3)):
        part[...] = (a[i].astype(f32) + b[i].astype(f32) + c[i].astype(f32)).astype(bf16)


def unstack(terms):
    shape = terms[0].shape[1:]
    return call(unstack_kernel, [whole] * 3, [(shape, bf16)] * 4)(*terms)


def total_kernel(a, b, c, d, e, f, result):
    result[:HALF] = a[...].astype(f32) + b[...].astype(f32) + c[...].astype(f32)
    result[HALF:] = d[...].astype(f32) + e[...].astype(f32) + f[...].astype(f32)


def two_scatters(left, right, left_moves, right_moves, events=(), last=()):
    left_passing = left_moves[0](left[2])
    left_from_ahead = left_moves[1](left[3])
    right_passing = right_moves[0](right[2])
    right_from_ahead = right_moves[1](right[3])
    left_passing, left_from_ahead, right_passing, right_from_ahead, *events = together(
        left_passing, left_from_ahead, right_passing, right_from_ahead, *events
    )
    left_from_behind = left_moves[0](add_low(left[1], left_passing))
    right_from_behind = right_moves[0](add_low(right[1], right_passing))
    left_from_behind, right_from_behind, *last = together(left_from_behind, right_from_behind, *last)
    left_terms = (left[0], left_from_behind, left_from_ahead)
    right_terms = (right[0], right_from_behind, right_from_ahead)
    return left_terms, right_terms, events, last


def plane_scatter(pieces, events=((), (), (), ())):
    first, second, *_ = two_scatters(pieces[:4], pieces[4:], moves_x(), moves_z(), *events[:2])
    first, second, *_ = two_scatters(unstack(first), unstack(second), moves_z(), moves_x(), *events[2:])
    width = pieces[0].shape[-1]
    return call(total_kernel, [whole] * 6, [((2 * HALF, width), f32)])(*first, *second)[0]


def scatter_chain(arrays, moves):
    done = []
    results = []

    def step(move, value):
        done.append(move(after(value, *done[-2:-1])))
        return done[-1]

    for parts in arrays:
        passing = step(moves[0], parts[2])
        from_ahead = step(moves[1], parts[3])
        from_behind = step(moves[0], add_low(parts[1], passing))
        results.append((passing, from_ahead, from_behind))
    return results


def split_low(value, count):
    parts = []
    rest = value
    for _ in range(count):
        part = rest.astype(bf16)
        parts.append(part)
        rest = rest - part.astype(f32)
    return parts


def core_columns(core, width):
    return pl.ds(pl.multiple_of(core * width, width), width)


def token_message_kernel(info, tokens, ids, padding, first, second, inverse_out):
    width = tokens.shape[1]
    half = width // 2
    rows = tokens[...].astype(f32)
    inverse = lax.rsqrt(jnp.mean(rows * rows, axis=-1, keepdims=True) + epsilon)
    inverse_out[...] = inverse
    lanes = lax.broadcasted_iota(jnp.int32, (rows.shape[0], EXTRA), 1)
    marks = jnp.zeros((rows.shape[0], EXTRA), f32)
    for k in range(8):
        marks = jnp.where(lanes == k, ids[:, k : k + 1].astype(f32), marks)
    marks = jnp.where(lanes == 8, padding[...].astype(f32), marks)
    for k, part in enumerate(split_low(inverse, 3)):
        marks = jnp.where(lanes == 9 + k, part.astype(f32), marks)
    marks = marks.astype(bf16)
    own = tokens[:, core_columns(info[0], half)]
    first[:, :half] = own[:HALF]
    first[:, half:] = marks[:HALF]
    second[:, :half] = own[HALF:]
    second[:, half:] = marks[HALF:]


def dense_message_kernel(info, query, key, value, out, router, gain1, gain2, q_gain, k_gain, result):
    size = query.shape[1]
    experts = router.shape[0]
    result[:size] = query[...].T
    result[size : 2 * size] = key[...].T
    result[2 * size : 3 * size] = value[...].T
    result[3 * size : 4 * size] = out[...]
    result[4 * size : 4 * size + experts] = router[...]
    base = 4 * size + experts
    rows = lax.broadcasted_iota(jnp.int32, (SMALL, result.shape[1]), 0)
    gains = jnp.where(rows == 0, gain1[...].astype(f32), 0.0)
    gains = jnp.where(rows == 1, gain2[...].astype(f32), gains)
    rest = jnp.zeros((1, result.shape[1] - q_gain.shape[1]), f32)
    gains = jnp.where(rows == 2, join([q_gain[...].astype(f32), rest], 1), gains)
    gains = jnp.where(rows == 3, join([k_gain[...].astype(f32), rest], 1), gains)
    result[base:] = gains.astype(bf16)


def dense_split_kernel(info, a, b, c, d, own, away, own_out, away_out, out, extra):
    shard = a.shape[1]
    rows = own.shape[0]
    size = out.shape[0]
    core = info[0]
    for i, piece in enumerate((a, b, c, d)):
        place = info[4 + i]
        columns = core_columns(place % 2, shard)

        @pl.when(place // 2 == core)
        def _():
            own[:, columns] = piece[:rows]
            own_out[:, columns] = piece[rows : rows + size]

        @pl.when(place // 2 != core)
        def _():
            away[:, columns] = piece[:rows]
            away_out[:, columns] = piece[rows : rows + size]

        columns = core_columns(place, shard)
        out[:, columns] = piece[rows : rows + size]
        extra[:, columns] = piece[rows + size :]


def slots_kernel(info, *refs):
    pieces, (chosen, pads) = refs[:8], refs[8:]
    first_expert = info[1]
    place_x, place_z, sign = info[8], info[9], info[10]
    shape = (2 * HALF, EXTRA)
    lanes = lax.broadcasted_iota(jnp.int32, shape, 1)
    rows = lax.broadcasted_iota(jnp.int32, shape, 0)
    earlier = (lanes < rows).astype(bf16)
    pad_total = jnp.zeros((1, EXTRA), f32)
    for ix in range(SIDE):
        for iz in range(SIDE):
            marks = join([pieces[ix][iz], pieces[4 + iz][ix]]).astype(f32)
            pad_total += jnp.sum(marks, axis=0, keepdims=True)
            named = jnp.zeros(shape, f32)
            for e in range(EXTRA // SLOTS):
                hit = jnp.where((lanes < 8) & (marks == (first_expert + e).astype(f32)), 1.0, 0.0)
                hit = jnp.max(hit, axis=-1, keepdims=True)
                named = jnp.where(lanes // SLOTS == e, hit, named)
            ranks = dot_nn(earlier, named.astype(bf16))
            match = (named > 0.0) & (ranks == (lanes % SLOTS).astype(f32))
            place = ((place_x + sign * ix) % SIDE) * SIDE + (place_z + sign * iz) % SIDE
            chosen[place] = jnp.where(match, 1.0, 0.0).astype(bf16)
    pads[...] = jnp.broadcast_to(pad_total, pads.shape)


def write_slots(result, place, columns, slots):
    for e in range(EXTRA // SLOTS):
        target = pl.ds(pl.multiple_of(place * SLOTS, SLOTS), SLOTS)
        result[e, target, columns] = slots[e * SLOTS : (e + 1) * SLOTS]


def read_slots(source, place, columns):
    target = pl.ds(pl.multiple_of(place * SLOTS, SLOTS), SLOTS)
    return join([source[e, target, columns] for e in range(EXTRA // SLOTS)])


def pick_rows_kernel(info, chosen, *refs):
    own, other, (result, extra) = refs[:8], refs[8:16], refs[16:]
    core, place_x, place_z, sign = info[0], info[8], info[9], info[10]
    half = result.shape[-1] // 2
    own_columns = core_columns(core, half)
    other_columns = core_columns(1 - core, half)
    for ix in range(SIDE):
        for iz in range(SIDE):
            place = ((place_x + sign * ix) % SIDE) * SIDE + (place_z + sign * iz) % SIDE
            matrix = chosen[place]
            rows = join([own[ix][iz], own[4 + iz][ix]])
            slots = dot_tn(matrix, rows).astype(bf16)
            write_slots(result, place, own_columns, slots[:, :half])
            write_slots(extra, place, slice(None), slots[:, half:])
            jx, jz = -ix % SIDE, -iz % SIDE
            rows = join([other[jx][jz, :, :half], other[4 + jz][jx, :, :half]])
            write_slots(result, place, other_columns, dot_tn(matrix, rows).astype(bf16))


def pick_spans_kernel(info, chosen, own, other, result):
    core = info[0]
    half = own.shape[-1]
    for place in range(SIDE * SIDE):
        matrix = chosen[place]
        write_slots(result, place, core_columns(core, half), dot_tn(matrix, own[place]).astype(bf16))
        write_slots(result, place, core_columns(1 - core, half), dot_tn(matrix, other[place]).astype(bf16))


def put_rows_kernel(info, chosen, own, came, extra, *pieces):
    place_x, place_z, sign = info[8], info[9], info[10]
    half = own.shape[-1]
    for ix in range(SIDE):
        for iz in range(SIDE):
            place = ((place_x + sign * ix) % SIDE) * SIDE + (place_z + sign * iz) % SIDE
            matrix = chosen[place]
            rows = read_slots(own, place, slice(None)).astype(f32) + read_slots(came, place, slice(None)).astype(f32)
            rows = dot_nn(matrix, rows.astype(bf16)).astype(bf16)
            marks = dot_nn(matrix, read_slots(extra, place, slice(None))).astype(bf16)
            pieces[ix][iz, :, :half] = rows[:HALF]
            pieces[4 + iz][ix, :, :half] = rows[HALF:]
            pieces[ix][iz, :, half:] = marks[:HALF]
            pieces[4 + iz][ix, :, half:] = marks[HALF:]


def put_sums_kernel(info, chosen, own, came, *pieces):
    place_x, place_z, sign = info[8], info[9], info[10]
    for ix in range(SIDE):
        for iz in range(SIDE):
            place = ((place_x + sign * ix) % SIDE) * SIDE + (place_z + sign * iz) % SIDE
            rows = read_slots(own, place, slice(None)).astype(f32) + read_slots(came, place, slice(None)).astype(f32)
            rows = dot_nn(chosen[place], rows.astype(bf16)).astype(bf16)
            pieces[ix][iz] = rows[:HALF]
            pieces[4 + iz][ix] = rows[HALF:]


def span_of(info, ix, iz):
    return ((info[8] + info[10] * ix) % SIDE) * SIDE + (info[9] + info[10] * iz) % SIDE


def piece_parts(info, i):
    for j in range(SIDE):
        if i < SIDE:
            yield j, span_of(info, i, j), slice(0, HALF)
        else:
            yield j, span_of(info, j, i - SIDE), slice(HALF, 2 * HALF)


def project_kernel(info, gain, own, came, *refs):
    pieces, (own_out, other_out, normed_out) = refs[:8], refs[8:]
    half = gain.shape[1]
    wide = own_out.shape[-1]
    count = SIDE * HALF
    lanes = lax.broadcasted_iota(jnp.int32, (count, EXTRA), 1)
    for i, piece in enumerate(pieces):
        rows = piece[...].reshape(count, half + EXTRA)
        marks = jnp.where((lanes >= 9) & (lanes < 12), rows[:, half:].astype(f32), 0.0)
        inverse = jnp.sum(marks, axis=-1, keepdims=True)
        normed = (rows[:, :half].astype(f32) * inverse * gain[...]).astype(bf16)
        own_rows = dot_nt(normed, own[...])
        other_rows = dot_nt(normed, came[...])
        for j, span, part in piece_parts(info, i):
            cut = slice(j * HALF, (j + 1) * HALF)
            normed_out[span, part] = normed[cut]
            own_out[span, part] = own_rows[cut]
            other_out[span, part] = other_rows[cut]


def turn(value, cosine, sine):
    return value * cosine + pltpu.roll(value, 64, 1) * sine


def block_mask(doc_rows, doc_columns, real, query_start, key_start, query_count, key_count):
    rows = lax.broadcasted_iota(jnp.int32, (query_count, key_count), 0)
    columns = lax.broadcasted_iota(jnp.int32, (query_count, key_count), 1)
    distance = rows - columns + (query_start - key_start)
    positions = lax.broadcasted_iota(jnp.int32, (1, key_count), 1) + key_start
    doc_columns = jnp.where(positions < real, doc_columns, -1)
    inside = (distance >= 0) & (distance < WINDOW) & (doc_rows == doc_columns)
    return inside | (distance == 0)


def real_count(pads, count):
    return (count - pads[0:1, 8:9]).astype(jnp.int32)


def attend_kernel(
    own, came, cosine, sine, gains, doc_rows, doc_columns, pads,
    mixed, raw, queries, keys, values, log_totals,
):
    count = queries.shape[0]
    size = queries.shape[1]
    span = mixed.shape[1]
    scale = size ** (-0.5)

    def prepare(j, carry):
        rows = pl.ds(pl.multiple_of(j * span, span), span)
        block = own[j] + came[j]
        raw[rows, :] = block[:, : 2 * size]
        cos_rows = cosine[rows, :]
        sin_rows = sine[rows, :]
        for part, target in ((0, queries), (1, keys)):
            piece = block[:, part * size : (part + 1) * size]
            inverse = lax.rsqrt(jnp.mean(piece * piece, axis=-1, keepdims=True) + epsilon)
            normed = piece * inverse * gains[part : part + 1, :]
            target[rows, :] = turn(normed, cos_rows, sin_rows).astype(bf16)
        values[rows, :] = block[:, 2 * size :].astype(bf16)
        return carry

    lax.fori_loop(0, count // span, prepare, 0)
    real = real_count(pads, float(count))
    for start in range(0, count, QUERY_BLOCK):
        low = max(0, start - WINDOW)
        high = start + QUERY_BLOCK
        scores = dot_nt(queries[start:high, :], keys[low:high, :]) * scale
        allowed = block_mask(
            doc_rows[start:high, :], doc_columns[:, low:high], real, start, low, QUERY_BLOCK, high - low
        )
        scores = jnp.where(allowed, scores, negative)
        peak = jnp.max(scores, axis=-1, keepdims=True)
        exponent = jnp.exp(scores - peak)
        total = jnp.sum(exponent, axis=-1, keepdims=True)
        weights = (exponent * (1.0 / total)).astype(bf16)
        rows = dot_nn(weights, values[low:high, :]).astype(bf16)
        mixed[start // span : high // span] = rows.reshape(QUERY_BLOCK // span, span, size)
        log_totals[start:high, :] = peak + jnp.log(total)


def attend_back_kernel(
    grad_mixed, raw, queries, keys, values, log_totals, cosine, sine, gains, doc_rows, doc_columns, pads,
    grads, gain_grads, grad_queries, grad_keys, grad_values,
):
    count = queries.shape[0]
    size = queries.shape[1]
    span = grads.shape[1]
    scale = size ** (-0.5)
    grad_keys[...] = jnp.zeros_like(grad_keys)
    grad_values[...] = jnp.zeros_like(grad_values)
    real = real_count(pads, float(count))
    for start in range(0, count, QUERY_BLOCK):
        low = max(0, start - WINDOW)
        high = start + QUERY_BLOCK
        query_rows = queries[start:high, :]
        key_rows = keys[low:high, :]
        grad_rows = grad_mixed[start:high, :]
        scores = dot_nt(query_rows, key_rows) * scale
        allowed = block_mask(
            doc_rows[start:high, :], doc_columns[:, low:high], real, start, low, QUERY_BLOCK, high - low
        )
        soft = jnp.where(allowed, jnp.exp(scores - log_totals[start:high, :]), 0.0)
        grad_soft = dot_nt(grad_rows, values[low:high, :])
        row_dot = jnp.sum(soft * grad_soft, axis=-1, keepdims=True)
        grad_scores = (soft * (grad_soft - row_dot)).astype(bf16)
        grad_queries[start:high, :] = dot_nn(grad_scores, key_rows) * scale
        grad_keys[low:high, :] += dot_tn(grad_scores, query_rows) * scale
        grad_values[low:high, :] += dot_tn(soft.astype(bf16), grad_rows)
    gain_grads[...] = jnp.zeros_like(gain_grads)

    def finish(j, carry):
        rows = pl.ds(pl.multiple_of(j * span, span), span)
        cos_rows = cosine[rows, :]
        sin_rows = sine[rows, :]
        parts = []
        for part, source in ((0, grad_queries), (1, grad_keys)):
            piece = raw[rows, part * size : (part + 1) * size]
            inverse = lax.rsqrt(jnp.mean(piece * piece, axis=-1, keepdims=True) + epsilon)
            back = turn(source[rows, :], cos_rows, -sin_rows)
            gain_grads[part : part + 1, :] += jnp.sum(back * piece * inverse, axis=0, keepdims=True)
            scaled = back * gains[part : part + 1, :]
            mean = jnp.mean(scaled * piece, axis=-1, keepdims=True)
            parts.append((inverse * scaled - piece * (inverse * inverse * inverse * mean)).astype(bf16))
        parts.append(grad_values[rows, :].astype(bf16))
        grads[j] = join(parts, 1)
        return carry

    lax.fori_loop(0, count // span, finish, 0)


def out_kernel(info, mixed, came_mixed, own, came, *pieces):
    for i, piece in enumerate(pieces):
        parts = list(piece_parts(info, i))
        left = join([mixed[span, part] for _, span, part in parts])
        right = join([came_mixed[span, part] for _, span, part in parts])
        rows = dot_nn(left, own[...]) + dot_nn(right, came[...])
        piece[...] = rows.astype(bf16).reshape(piece.shape)


def heads_back_kernel(rows, weight, result):
    for i in range(weight.shape[0]):
        result[i] = dot_nt(rows[...], weight[i]).astype(bf16)


def out_grad_kernel(mixed, came_mixed, rows, own_out, away_out):
    size = mixed.shape[-1]
    count = mixed.shape[0] * mixed.shape[1]
    grads = rows[...].reshape(count, rows.shape[-1])
    own_out[...] = dot_tn(mixed[...].reshape(count, size), grads).astype(bf16)
    away_out[...] = dot_tn(came_mixed[...].reshape(count, size), grads).astype(bf16)


def input_back_kernel(info, grads, came_grads, own, came, *refs):
    tokens, mixture, pieces, gain_grad = refs[:8], refs[8:16], refs[16:24], refs[24]
    half = own.shape[1]
    count = SIDE * HALF
    lanes = lax.broadcasted_iota(jnp.int32, (count, EXTRA), 1)
    total = jnp.zeros((1, half), f32)
    for i, piece in enumerate(pieces):
        parts = list(piece_parts(info, i))
        left = join([grads[span, part] for _, span, part in parts])
        right = join([came_grads[span, part] for _, span, part in parts])
        rows = dot_nn(left, own[...]) + dot_nn(right, came[...])
        piece[:, :, :half] = rows.astype(bf16).reshape(SIDE, HALF, half)
        piece[:, :, half:] = mixture[i][...]
        source = tokens[i][...].reshape(count, half + EXTRA)
        marks = jnp.where((lanes >= 9) & (lanes < 12), source[:, half:].astype(f32), 0.0)
        inverse = jnp.sum(marks, axis=-1, keepdims=True)
        total += jnp.sum(rows * (source[:, :half].astype(f32) * inverse), axis=0, keepdims=True)
    gain_grad[...] = jnp.broadcast_to(total, gain_grad.shape)


def project_grad_kernel(grads, came_grads, normed, own_out, away_out):
    count = normed.shape[0] * normed.shape[1]
    wide = grads.shape[-1]
    rows = normed[...].reshape(count, normed.shape[-1])
    own_out[...] = dot_tn(grads[...].reshape(count, wide), rows).astype(bf16)
    away_out[...] = dot_tn(came_grads[...].reshape(count, wide), rows).astype(bf16)


def halves(core, own, came):
    return join([jnp.where(core == 0, own, came), jnp.where(core == 0, came, own)], 1)


def chosen_experts(ids, count):
    lanes = lax.broadcasted_iota(jnp.int32, (ids.shape[0], count), 1)
    chosen = jnp.zeros((ids.shape[0], count), f32)
    for k in range(8):
        chosen = jnp.where(lanes == ids[:, k : k + 1], 1.0, chosen)
    return chosen


def router_kernel(
    info, tokens, own, came, ids, extra, residual_out, inverse_out, normed_out, probs_out, gates_out, total_out, first, second
):
    core = info[0]
    half = tokens.shape[1] // 2
    experts = probs_out.shape[1]
    residual = tokens[...].astype(f32) + halves(core, own[...], came[...])
    residual_out[...] = residual
    inverse = lax.rsqrt(jnp.mean(residual * residual, axis=-1, keepdims=True) + epsilon)
    inverse_out[...] = inverse
    gain = extra[experts + 1 : experts + 2, :].astype(f32)
    normed = (residual * inverse * gain).astype(bf16)
    normed_out[...] = normed
    logits = dot_nt(normed, extra[:experts, :])
    exponent = jnp.exp(logits - jnp.max(logits, axis=-1, keepdims=True))
    probs = exponent / jnp.sum(exponent, axis=-1, keepdims=True)
    probs_out[...] = probs
    chosen = chosen_experts(ids, experts)
    picked = probs * chosen
    total = jnp.sum(picked, axis=-1, keepdims=True)
    total_out[...] = total
    gates = picked / total
    gates_out[...] = gates
    marks = join(split_low(gates, 2), 1)
    mine = normed_out[:, core_columns(core, half)]
    first[:, :half] = mine[:HALF]
    first[:, half:] = marks[:HALF]
    second[:, :half] = mine[HALF:]
    second[:, half:] = marks[HALF:]


def router_back_kernel(
    info, own, came, residual_ref, inverse_ref, normed, probs_ref, gates_ref, total, ids, padding, cotangent, extra,
    grad_low, grad_half, grad_out, rows_out,
):
    core = info[0]
    half = cotangent.shape[1] // 2
    experts = probs_ref.shape[1]
    probs = probs_ref[...]
    gates = gates_ref[...]
    residual = residual_ref[...]
    inverse = inverse_ref[...]
    marks = own[:, half:] + came[:, half:]
    gate_grads = marks[:, :experts] + marks[:, experts:]
    chosen = chosen_experts(ids, experts)
    grad_picked = (gate_grads - jnp.sum(gate_grads * gates, axis=-1, keepdims=True)) / total[...]
    grad_probs = chosen * grad_picked
    grad_logits = (probs * (grad_probs - jnp.sum(grad_probs * probs, axis=-1, keepdims=True))).astype(bf16)
    grad_normed = halves(core, own[:, :half], came[:, :half]) + dot_nn(grad_logits, extra[:experts, :])
    scaled = grad_normed * extra[experts + 1 : experts + 2, :].astype(f32)
    mean = jnp.mean(scaled * residual, axis=-1, keepdims=True)
    grad = cotangent[...].astype(f32) + inverse * scaled - residual * (inverse * inverse * inverse * mean)
    grad_out[...] = grad
    grad_low[...] = grad.astype(bf16)
    grad_half[...] = grad_low[:, core_columns(core, half)]
    gain_grad = jnp.sum(grad_normed * residual * inverse, axis=0, keepdims=True)
    rows_out[:experts] = dot_tn(grad_logits, normed[...]).astype(bf16)
    kept = 1.0 - padding[...].astype(f32)
    shard = 4 * EXTRA
    rest = jnp.zeros((1, shard - experts), f32)

    def row(values):
        return join([values, rest] * SIDE, 1)

    counted = chosen * kept
    probs_sum = jnp.sum(probs * kept, axis=0, keepdims=True)
    probs_high = probs_sum.astype(bf16).astype(f32)
    kept_sum = jnp.broadcast_to(jnp.sum(kept, axis=0, keepdims=True), (1, experts))
    rows = (
        gain_grad,
        row(jnp.sum(counted[:HALF], axis=0, keepdims=True)),
        row(jnp.sum(counted[HALF:], axis=0, keepdims=True)),
        row(probs_high),
        row(probs_sum - probs_high),
        row(kept_sum),
    )
    numbers = lax.broadcasted_iota(jnp.int32, (SMALL, 2 * half), 0)
    small = jnp.zeros((SMALL, 2 * half), f32)
    for i, values in enumerate(rows):
        small = jnp.where(numbers == i, values, small)
    rows_out[experts:] = small.astype(bf16)


def final_rows_kernel(info, own, came, tokens, inverse_ref, extra, grad_residual, residual, grad_input, result):
    core = info[0]
    half = own.shape[1] // 2
    base = extra.shape[0] - SMALL
    rows = tokens[...].astype(f32)
    inverse = inverse_ref[...]
    scaled = halves(core, own[:, :half], came[:, :half]) * extra[base : base + 1, :].astype(f32)
    mean = jnp.mean(scaled * rows, axis=-1, keepdims=True)
    grad_input[...] = grad_residual[...] + inverse * scaled - rows * (inverse * inverse * inverse * mean)
    result[...] = residual[...] + halves(core, own[:, half:], came[:, half:])


def expert_kernel(info, rows, marks, grads, pairs_w, downs_w, back_own, back_other, back_marks, hidden_out, pairs_out):
    core = info[0]
    expert = info[1] + pl.program_id(0)
    shard = pairs_w.shape[2]
    count = rows.shape[1]
    units = hidden_out.shape[2]
    pairs = grad_raw = 0.0
    for place in range(SIDE):
        columns = slice(place * shard, (place + 1) * shard)
        pairs += dot_nn(rows[0, :, columns], pairs_w[place, 0])
        grad_raw += dot_nt(grads[0, :, columns], downs_w[place, 0])
    gate_pre = pairs[:, :units]
    up_pre = pairs[:, units:]
    lanes = lax.broadcasted_iota(jnp.int32, (count, EXTRA), 1)
    high_lane = lanes == expert
    low_lane = lanes == expert + EXTRA // 2
    gates = jnp.sum(jnp.where(high_lane | low_lane, marks[0].astype(f32), 0.0), axis=-1, keepdims=True)
    sigmoid = jax.nn.sigmoid(gate_pre)
    activated = gate_pre * sigmoid
    hidden = (activated * up_pre).astype(bf16).astype(f32)
    gate_grads = jnp.sum(hidden * grad_raw, axis=-1, keepdims=True)
    grad_hidden = gates * grad_raw
    gate_low = (grad_hidden * up_pre * sigmoid * (1.0 + gate_pre * (1.0 - sigmoid))).astype(bf16)
    up_low = (grad_hidden * activated).astype(bf16)
    hidden_out[0] = (gates * hidden).astype(bf16)
    pairs_low = join([gate_low, up_low], 1)
    pairs_out[0] = pairs_low
    for place in range(SIDE):
        near = slice((place % 2) * shard, (place % 2 + 1) * shard)
        result = dot_nt(pairs_low, pairs_w[place, 0]).astype(bf16)

        @pl.when(place // 2 == core)
        def _():
            back_own[0, :, near] = result

        @pl.when(place // 2 != core)
        def _():
            back_other[0, :, near] = result

    high = gate_grads.astype(bf16).astype(f32)
    low = gate_grads - high
    back_marks[0] = (jnp.where(high_lane, high, 0.0) + jnp.where(low_lane, low, 0.0)).astype(bf16)


def expert_grad_kernel(info, rows, pairs, *refs):
    gate_grads, up_grads = refs[:4], refs[4:]
    shard, units = gate_grads[0].shape[1:]
    for i in range(SIDE):
        result = dot_tn(rows[0, :, core_columns(info[4 + i], shard)], pairs[0]).astype(bf16)
        gate_grads[i][0] = result[:, :units]
        up_grads[i][0] = result[:, units:]


def expert_out_kernel(info, grads, hidden, downs_w, out_own, out_other, *down_grads):
    core = info[0]
    shard = downs_w.shape[3]
    for i in range(SIDE):
        place = info[4 + i]
        down_grads[i][0] = dot_tn(hidden[0], grads[0, :, core_columns(place, shard)]).astype(bf16)
        result = dot_nn(hidden[0], downs_w[place, 0]).astype(bf16)
        near = core_columns(place % 2, shard)

        @pl.when(place // 2 == core)
        def _():
            out_own[0, :, near] = result

        @pl.when(place // 2 != core)
        def _():
            out_other[0, :, near] = result


def by_expert(shape):
    if len(shape) == 4:
        return pl.BlockSpec((shape[0], 1) + tuple(shape[2:]), lambda e: (0, e, 0, 0))
    return pl.BlockSpec((1,) + tuple(shape[1:]), lambda e: (e, 0, 0))


def per_expert(kernel, info, arrays, out_shapes, flops, moved):
    return call(
        kernel,
        [scalars] + [by_expert(array.shape) for array in arrays],
        [(shape, bf16) for shape in out_shapes],
        flops=flops,
        moved=moved,
        out_specs=[by_expert(shape) for shape in out_shapes],
        grid=(arrays[0].shape[0],),
    )(info, *arrays)


def project_chunk_kernel(info, own, came, gain, gain_came, heads, heads_came, out, out_came, extra, *pieces):
    core = info[0]
    shard = pieces[0].shape[1]
    size = out.shape[0]
    numbers = lax.broadcasted_iota(jnp.int32, (SMALL, shard), 0)
    both = heads[...] + heads_came[...]
    rest = jnp.zeros((1, shard - 2 * size), f32)
    head_row = join([both[0:1], both[1:2], rest], 1)
    for i in range(SIDE):
        place = info[4 + i]
        columns = core_columns(place % 2, shard)
        near = place // 2 == core
        block = jnp.where(near, own[:, columns], came[:, columns])
        pieces[i][:size] = block[:size]
        pieces[SIDE + i][...] = block[size:]
        gain_row = jnp.where(near, gain[0:1, columns], gain_came[0:1, columns])
        small = jnp.where(numbers == 0, gain_row, jnp.where(numbers == 1, head_row, 0.0))
        pieces[i][size : 2 * size] = jnp.where(near, out[:, columns], out_came[:, columns])
        pieces[i][2 * size : 2 * size + extra.shape[0]] = extra[:, core_columns(place, shard)]
        pieces[i][2 * size + extra.shape[0] :] = small.astype(bf16)


def project_final_kernel(info, parts, query, out_grad, router, gain1, gain2, head_gains, load, loss, total):
    step = pl.program_id(0)
    size = out_grad.shape[0] // parts.shape[0]
    rest = 0.0
    for i in range(parts.shape[0]):
        block = parts[i].astype(f32)
        query[:, i * size : (i + 1) * size] = block[:size].T
        out_grad[i * size : (i + 1) * size] = block[size : 2 * size]
        rest += block[2 * size :]

    @pl.when(step == 0)
    def _():
        total[...] = rest

    @pl.when(step > 0)
    def _():
        total[...] += rest

    @pl.when(step == pl.num_programs(0) - 1)
    def _():
        experts = router.shape[0]
        router[...] = total[:experts]

        def row(i):
            return total[experts + i : experts + i + 1, :]

        gain2[...] = row(0)
        counts = row(1)[:, :experts] + row(2)[:, :experts]
        probs = row(3)[:, :experts] + row(4)[:, :experts]
        kept = row(5)[:, :experts]
        share = counts / (kept * 8.0)
        load[...] = share * float(experts)
        loss[...] = float(experts) * jnp.sum(share * (probs / kept), axis=-1, keepdims=True)
        gain1[...] = row(SMALL)
        count = head_gains.shape[1]
        for part in range(2):
            sums = row(SMALL + 1)[:, part * size : (part + 1) * size]
            sums = pltpu.roll(jnp.broadcast_to(sums, (8, size)), (size - info[2] * count) % size, 1)
            head_gains[part : part + 1] = sums[:1, :count]


def key_value_kernel(info, mine, other, key, value):
    size = key.shape[1] // 2
    for group in range(2):
        cut = slice(group * size, (group + 1) * size)
        block = jnp.where(info[11] == group, mine[...].astype(f32), other[...].astype(f32))
        key[:, cut] = block[:size].T
        value[:, cut] = block[size:].T


def body(
    tokens,
    cotangent,
    doc_lengths,
    padding,
    expert_ids,
    norm1_gain,
    w_query,
    key_weight,
    value_weight,
    q_gain,
    k_gain,
    w_out,
    norm2_gain,
    w_router,
    w_gate,
    w_up,
    w_down,
):
    core = lax.axis_index("tensor")
    context = lax.axis_index("context")
    mine = lax.axis_index("fsdp")
    place_x = context // SIDE
    place_z = context % SIDE
    sign = 1 - 2 * core
    span, width = tokens.shape[1:]
    half = width // 2
    size = 4 * q_gain.shape[0]
    expert_count = w_router.shape[1]
    local_experts, shard, hidden_units = w_gate.shape
    spans = SIDE * SIDE
    count = span * spans
    info = jnp.stack(
        [core, context * local_experts, mine, context]
        + [(mine + sign * i) % SIDE for i in range(SIDE)]
        + [place_x, place_z, sign, context // (spans // 2)]
    ).astype(jnp.int32)
    token_rows = tokens[0]
    cot_rows = cotangent[0]
    ids = expert_ids[0]
    pad_column = padding[0][:, None]

    first, second, inverse1 = call(
        token_message_kernel,
        [scalars] + [whole] * 3,
        [((HALF, half + EXTRA), bf16), ((HALF, half + EXTRA), bf16), ((span, 1), f32)],
    )(info, token_rows, ids, pad_column)

    positions = jnp.arange(count, dtype=jnp.int32)
    ends = jnp.cumsum(doc_lengths[0])
    passed = positions[:, None] >= ends[None, :]
    doc_index = jnp.sum(passed.astype(jnp.int32), axis=-1)
    starts = jnp.sum(jnp.where(passed, doc_lengths, 0), axis=-1)
    doc_rows = doc_index[:, None]
    doc_columns = doc_index[None, :]
    offsets = (positions - starts).astype(f32)
    frequency = theta_base ** (-jnp.arange(size // 2, dtype=f32) * 2.0 / size)
    angles = offsets[:, None] * frequency[None, :]
    cosine = jnp.cos(angles)
    sine = jnp.sin(angles)
    cosine = join([cosine, cosine], 1)
    sine = join([-sine, sine], 1)
    dense = call(
        dense_message_kernel,
        None,
        [((4 * size + expert_count + SMALL, shard), bf16)],
        grid_spec=pltpu.PrefetchScalarGridSpec(
            num_scalar_prefetch=1,
            grid=(1,),
            in_specs=[
                pl.BlockSpec((shard, size), lambda i, info: (0, info[3])),
                pl.BlockSpec((shard, size), lambda i, info: (0, info[11])),
                pl.BlockSpec((shard, size), lambda i, info: (0, info[11])),
                pl.BlockSpec((size, shard), lambda i, info: (info[3], 0)),
            ]
            + [whole] * 5,
            out_specs=[whole],
        ),
    )(
        after(info, first), w_query, key_weight, value_weight, w_out, w_router.T,
        norm1_gain[None], norm2_gain[None], q_gain[None], k_gain[None],
    )[0]
    dense_pieces = ring_gather(dense, moves_y())
    cot_half = lax.dynamic_slice_in_dim(cot_rows, core * half, half, axis=1)
    cot_all = lax.all_gather(cot_half, "context", axis=0)
    pairs_all = lax.all_gather(after(join([w_gate, w_up], 2), first), "fsdp", axis=0)
    first_near, second_near = two_gathers(
        first, second, moves_z(), moves_x(), (dense_pieces[3],), (dense_pieces[1],)
    )
    first_pieces, second_pieces = two_gathers(
        stack(first_near),
        stack(second_near),
        moves_x(),
        moves_z(),
        (dense_pieces[2], cosine, sine, doc_rows),
    )
    token_pieces = first_pieces + second_pieces
    extra_rows = expert_count + SMALL
    dense_own, dense_away, out_own_rows, out_away_rows, dense_out, extra = call(
        dense_split_kernel,
        [scalars] + [whole] * 4,
        [
            ((3 * size, half), bf16),
            ((3 * size, half), bf16),
            ((size, half), bf16),
            ((size, half), bf16),
            ((size, width), bf16),
            ((extra_rows, width), bf16),
        ],
    )(info, *dense_pieces)
    dense_came = other_core(dense_away)
    out_came_rows = other_core(out_away_rows)
    gain1 = lax.dynamic_slice(extra, (expert_count, core * half), (1, half)).astype(f32)
    gain_rows = extra[expert_count + 2 : expert_count + 4].reshape(2, SIDE, shard)[:, :, : size // SIDE]
    head_gains = jnp.pad(gain_rows.reshape(2, size).astype(f32), ((0, 6), (0, 0)))

    mark_spec = pl.BlockSpec((SIDE, HALF, EXTRA), lambda i: (0, 0, half // EXTRA))
    chosen, pads = call(
        slots_kernel,
        [scalars] + [mark_spec] * 8,
        [((spans, span, EXTRA), bf16), ((8, EXTRA), f32)],
        grid=(1,),
        out_specs=[whole, whole],
    )(info, *token_pieces)

    head_shape = (spans, span, size)
    own_part, away_part, normed1 = call(
        project_kernel,
        [scalars] + [whole] * 11,
        [((spans, span, 3 * size), f32), ((spans, span, 3 * size), f32), ((spans, span, half), bf16)],
        flops=4 * count * half * 3 * size,
        moved=2 * 10**7,
    )(info, gain1, after(dense_own, cot_all), dense_came, *token_pieces)
    down_all = lax.all_gather(after(w_down, token_pieces[0]), "fsdp", axis=0)
    mixed, raw, queries, keys, values, log_totals = call(
        attend_kernel,
        [whole] * 8,
        [
            (head_shape, bf16),
            ((count, 2 * size), f32),
            ((count, size), bf16),
            ((count, size), bf16),
            ((count, size), bf16),
            ((count, 1), f32),
        ],
        flops=4 * 10**9,
        moved=3 * 10**7,
    )(own_part, other_core(away_part), cosine, sine, head_gains, doc_rows, doc_columns, pads)
    mixed_came = other_core(mixed)
    piece_shape = (SIDE, HALF, half)
    branch_pieces = call(
        out_kernel, [scalars] + [whole] * 4, [(piece_shape, bf16)] * 8, flops=4 * count * size * half, moved=10**7
    )(info, mixed, mixed_came, out_own_rows, out_came_rows)
    branch = plane_scatter(branch_pieces)

    residual2, inverse2, normed2, probs, gates, picked_total, first, second = call(
        router_kernel,
        [scalars] + [whole] * 5,
        [
            ((span, width), f32),
            ((span, 1), f32),
            ((span, width), bf16),
            ((span, expert_count), f32),
            ((span, expert_count), f32),
            ((span, 1), f32),
            ((HALF, half + EXTRA), bf16),
            ((HALF, half + EXTRA), bf16),
        ],
    )(info, token_rows, branch, other_core(branch), ids, extra)
    cot_other = other_core(after(cot_all, first))
    slot_count = spans * SLOTS
    slot_grads = call(
        pick_spans_kernel,
        [scalars] + [whole] * 3,
        [((local_experts, slot_count, width), bf16)],
        flops=4 * 10**9,
        moved=2 * 10**7,
    )(info, chosen, cot_all, cot_other)[0]
    row_pieces = plane_gather(
        first, second, ((), (), (pairs_all,), (slot_grads,))
    )
    away_pieces = [other_core(piece) for piece in row_pieces]

    slot_rows, slot_marks = call(
        pick_rows_kernel,
        [scalars] + [whole] * 17,
        [((local_experts, slot_count, width), bf16), ((local_experts, slot_count, EXTRA), bf16)],
        flops=4 * 10**9,
        moved=2 * 10**7,
    )(info, chosen, *row_pieces, *away_pieces)
    expert_flops = 2 * local_experts * slot_count * width * hidden_units
    slot_half = (local_experts, slot_count, half)
    slot_hidden = (local_experts, slot_count, hidden_units)
    back_own, back_other, back_marks, hidden, pairs = per_expert(
        expert_kernel,
        info,
        [slot_rows, slot_marks, slot_grads, pairs_all, down_all],
        [slot_half, slot_half, (local_experts, slot_count, EXTRA), slot_hidden, slot_hidden[:2] + (2 * hidden_units,)],
        5 * expert_flops,
        5 * 10**7,
    )
    back_came = other_core(back_other)
    expert_grads = per_expert(
        expert_grad_kernel,
        info,
        [slot_rows, pairs],
        [(local_experts, shard, hidden_units)] * 8,
        2 * expert_flops,
        3 * 10**7,
    )
    gate_grads, up_grads = expert_grads[:4], expert_grads[4:]
    out_all = lax.all_gather(after(dense_out, slot_rows), "context", axis=0)
    grad_pieces = call(
        put_rows_kernel,
        [scalars] + [whole] * 4,
        [((SIDE, HALF, half + EXTRA), bf16)] * 8,
        flops=2 * 10**9,
        moved=2 * 10**7,
    )(info, chosen, back_own, after(back_came, gate_grads[0]), back_marks)
    out_own, out_other, *down_grads = per_expert(
        expert_out_kernel,
        info,
        [slot_grads, after(hidden, grad_pieces[0]), down_all],
        [slot_half, slot_half] + [(local_experts, hidden_units, shard)] * 4,
        2 * expert_flops,
        3 * 10**7,
    )
    mixture_pieces = call(
        put_sums_kernel,
        [scalars] + [whole] * 3,
        [(piece_shape, bf16)] * 8,
        flops=2 * 10**9,
        moved=2 * 10**7,
    )(info, chosen, out_own, other_core(out_other))
    gate_steps, up_steps, down_steps = scatter_chain([gate_grads, up_grads, down_grads], moves_y())
    grad_message = plane_scatter(grad_pieces, ((out_own, *gate_steps[:2]), (), (), (gate_steps[2], up_steps[0], mixture_pieces[0])))

    grad_low, grad_half, grad_residual2, router_rows = call(
        router_back_kernel,
        [scalars] + [whole] * 12,
        [
            ((span, width), bf16),
            ((span, half), bf16),
            ((span, width), f32),
            ((extra_rows, width), bf16),
        ],
    )(
        info, grad_message, other_core(grad_message), residual2, inverse2, normed2, probs, gates, picked_total,
        ids, pad_column, cot_rows, extra,
    )

    four_heads = pl.BlockSpec((SIDE, span, size), lambda i: (i, 0, 0))
    four_weights = pl.BlockSpec((SIDE, size, width), lambda i: (i, 0, 0))
    out_grads_all = lax.all_gather(grad_half, "context", axis=0)
    heads_back = call(
        heads_back_kernel,
        [whole, four_weights],
        [(head_shape, bf16)],
        flops=2 * span * width * width,
        moved=10**7,
        grid=(SIDE,),
        out_specs=[four_heads],
    )(grad_low, out_all)[0]
    heads_grad = lax.all_to_all(heads_back, "context", split_axis=0, concat_axis=0, tiled=True)
    grads, gain_grads = call(
        attend_back_kernel,
        [whole] * 12,
        [((spans, span, 3 * size), bf16), ((8, size), f32)],
        flops=8 * 10**9,
        moved=3 * 10**7,
        scratch_shapes=[pltpu.VMEM((count, size), f32)] * 3,
    )(
        heads_grad.reshape(count, size), raw, queries, keys, values, log_totals,
        cosine, sine, head_gains, doc_rows, doc_columns, pads,
    )
    grads_came = other_core(grads)
    project_own, project_away = call(
        project_grad_kernel,
        [whole] * 3,
        [((3 * size, half), bf16)] * 2,
        flops=4 * count * half * 3 * size,
        moved=2 * 10**7,
    )(grads, grads_came, normed1)
    out_grad_own, out_grad_away = call(
        out_grad_kernel, [whole] * 3, [((size, half), bf16)] * 2, flops=4 * count * size * half, moved=10**7
    )(after(mixed, project_own), mixed_came, out_grads_all)
    project_came = other_core(project_away)
    *input_pieces, gain1_part = call(
        input_back_kernel,
        [scalars] + [whole] * 20,
        [((SIDE, HALF, width), bf16)] * 8 + [((8, half), f32)],
        flops=4 * count * half * 3 * size,
        moved=3 * 10**7,
    )(info, grads, after(grads_came, project_own, up_steps[1], up_steps[2]), dense_own, dense_came, *token_pieces, *mixture_pieces)

    query_shape = (2 * size + SMALL + extra_rows, shard)
    key_value_shape = (2 * size, shard)
    project_pieces = call(
        project_chunk_kernel, [scalars] + [whole] * 9, [(query_shape, bf16)] * 4 + [(key_value_shape, bf16)] * 4
    )(
        info, project_own, project_came, gain1_part, other_core(gain1_part), gain_grads, other_core(gain_grads),
        out_grad_own, other_core(out_grad_away), router_rows,
    )
    query_terms = ring_scatter(project_pieces[:4], moves_y())
    key_passing = moves_y()[0](project_pieces[6])
    key_ahead = moves_y()[1](project_pieces[7])
    first, second, (key_passing, key_ahead, *query_terms), (key_ahead,) = two_scatters(
        input_pieces[:4],
        input_pieces[4:],
        moves_x(),
        moves_z(),
        (key_passing, key_ahead, *query_terms, *down_steps[:2]),
        (key_ahead,),
    )
    query_mine = low_sum(query_terms[:3])
    query_all = lax.all_gather(query_mine, "context", axis=0)
    key_behind = moves_y()[0](add_low(project_pieces[5], key_passing))
    first, second, (key_behind,), key_terms = two_scatters(
        unstack(first), unstack(second), moves_z(), moves_x(), (key_behind,), (down_steps[2],)
    )
    key_value = low_sum((project_pieces[4], key_behind, key_ahead))
    key_value = low_sum([key_value] + [along_z(key_value, step) for step in range(1, SIDE)])
    final_rows = call(total_kernel, [whole] * 6, [((span, width), f32)])(*first, *second)[0]
    key_value = low_sum([key_value, across(key_value, 1)])
    final_key, final_value = call(
        key_value_kernel, [scalars] + [whole] * 2, [((shard, 2 * size), f32)] * 2
    )(info, key_value, across(key_value, 2))
    grad_input, result = call(final_rows_kernel, [scalars] + [whole] * 7, [((span, width), f32)] * 2)(
        info, final_rows, other_core(final_rows), token_rows, inverse1, extra, grad_residual2, residual2
    )
    (
        final_query, final_out, final_router, final_gain1, final_gain2, final_head_gains, expert_load, balance_loss
    ) = call(
        project_final_kernel,
        [scalars, pl.BlockSpec((SIDE,) + query_shape, lambda i: (i, 0, 0))],
        [
            ((shard, spans * size), f32),
            ((spans * size, shard), f32),
            ((expert_count, shard), f32),
            ((1, shard), f32),
            ((1, shard), f32),
            ((2, size // SIDE), f32),
            ((1, expert_count), f32),
            ((1, 1), f32),
        ],
        grid=(SIDE,),
        out_specs=[
            pl.BlockSpec((shard, SIDE * size), lambda i: (0, i)),
            pl.BlockSpec((SIDE * size, shard), lambda i: (i, 0)),
        ]
        + [whole] * 6,
        scratch_shapes=[pltpu.VMEM((SMALL + extra_rows, shard), f32)],
    )(info, after(query_all, grad_input))

    def finished(parts, steps):
        return parts[0].astype(f32) + steps[1].astype(f32) + steps[2].astype(f32)

    final_gate = finished(gate_grads, gate_steps)
    final_up = finished(up_grads, up_steps)
    final_down = finished(down_grads, down_steps)

    return (
        result[None],
        balance_loss.reshape(()),
        expert_load.reshape(expert_count),
        grad_input[None],
        final_gain1.reshape(shard),
        final_query,
        final_key,
        final_value,
        final_head_gains[0],
        final_head_gains[1],
        final_out,
        final_gain2.reshape(shard),
        final_router.T,
        final_gate,
        final_up,
        final_down,
    )


def solution(mesh):
    in_specs = (
        P("fsdp", "context", None),
        P("fsdp", "context", None),
        P("fsdp", None),
        P("fsdp", "context"),
        P("fsdp", "context", None),
        P("fsdp"),
        P("fsdp", "tensor"),
        P("fsdp", "tensor"),
        P("fsdp", "tensor"),
        P("fsdp"),
        P("fsdp"),
        P("tensor", "fsdp"),
        P("fsdp"),
        P("fsdp", None),
        P("context", "fsdp", "tensor"),
        P("context", "fsdp", "tensor"),
        P("context", "tensor", "fsdp"),
    )
    out_specs = (
        P("fsdp", "context", None),
        P(),
        P(),
        P("fsdp", "context", None),
        P("fsdp"),
        P("fsdp", "tensor"),
        P("fsdp", "tensor"),
        P("fsdp", "tensor"),
        P("fsdp"),
        P("fsdp"),
        P("tensor", "fsdp"),
        P("fsdp"),
        P("fsdp", None),
        P("context", "fsdp", "tensor"),
        P("context", "fsdp", "tensor"),
        P("context", "tensor", "fsdp"),
    )
    return jax.shard_map(body, mesh=mesh, in_specs=in_specs, out_specs=out_specs, check_vma=False)
```

time: 1550 us -> 671 us (0.43)
  waiting for transfers between devices: 696 us -> 209 us
  blocking collectives: 259 us -> 0 us
  Pallas kernels: 0 us -> 238 us
  matrix products: 173 us -> 0 us
  other arithmetic: 122 us -> 43 us
  local copies, waits for them, and re-layouts: 101 us -> 27.4 us
  starting transfers between devices: 166 us -> 128 us
    all_to_all x4 -> x1, waiting for transfers between devices: 313 us -> 8.15 us  [body(): lax.all_to_all(heads_back, 'context', split_axis=0, concat_axis=0, tiled=...]
    pallas_call x0 -> x38, Pallas kernels: none -> 238 us  [the longest x3 58.9 us: per_expert(): call(kernel, [scalars] + [by_expert(array.shape) for array in arrays], [(...]
    psum x4 -> x0, blocking collectives: 219 us -> none  [the longest x1 151 us: body(): lax.psum((counts, prob_sums, jnp.sum(kept_rows)), ('fsdp', 'context'))]
    dot_general x38 -> x0, matrix products: 173 us -> none  [the longest x1 14.5 us: body(): jnp.einsum('sexd,efd->sexf', got_grads, down_full, preferred_element_type...]
    ppermute x40 -> x106, waiting for transfers between devices: 34.3 us -> 201 us  [the longest x78 170 us: move(): return lambda value: lax.ppermute(value, (axis, 'tensor'), pairs)]
    reduce_scatter x8 -> x0, waiting for transfers between devices: 152 us -> none  [the longest x1 82.7 us: reduce_over_fsdp(): lax.psum_scatter(grad_list[1].astype(jnp.bfloat16), 'fsdp', scatter_dimen...]
    psum x4 -> x0, waiting for transfers between devices: 135 us -> none  [the longest x1 100 us: sum_over_context(): lax.psum(grad_list[1].astype(jnp.bfloat16), 'context').astype(jnp.float32)]
    gather x4 -> x0, local copies, waits for them, and re-layouts: 60 us -> none  [the longest x1 19.1 us: body(): weighted_grad[slot_source]]
  transfers between devices with their start and end apart: 63 -> 113, of which waited for: 31 -> 63; matrix products, arithmetic and copies ran while one was open for 18% -> 7% of each run, Pallas kernels for 0% -> 35%
where the time goes in v1:
time: 671 us; the launch traced here: 661 us
  Pallas kernels  238 us (35%)
  waiting for transfers between devices  209 us (31%)
  starting transfers between devices  128 us (19%)
  other arithmetic  43 us (6%)
  local copies, waits for them, and re-layouts  27.4 us (4%)
  between operations  15.5 us (2%)
    ppermute x78, waiting for transfers between devices, move(): return lambda value: lax.ppermute(value, (axis, 'tensor'), pairs)  170 us
    ppermute x78, starting transfers between devices, move(): return lambda value: lax.ppermute(value, (axis, 'tensor'), pairs)  101 us
    pallas_call x3, Pallas kernels, per_expert(): call(kernel, [scalars] + [by_expert(array.shape) for array in arrays], [(...  58.9 us
    unnamed x185, local copies, waits for them, and re-layouts  18.9 us
    convert_element_type x17, other arithmetic, add_low(): return (left.astype(f32) + right.astype(f32)).astype(bf16)  17.7 us
    pallas_call x1, Pallas kernels, body(): call(attend_back_kernel, [whole] * 12, [((spans, span, 3 * size), bf16),...  16.5 us
    ppermute x3, waiting for transfers between devices, along_z(): return lax.ppermute(value, 'context', pairs)  15.7 us
    pallas_call x6, Pallas kernels, unstack(): return call(unstack_kernel, [whole] * 3, [(shape, bf16)] * 4)(*terms)  15.5 us
  transfers between devices with their start and end apart: 113, of which 63 were waited for; matrix products, arithmetic and copies ran while one was open for 7% of the time, Pallas kernels for 35%

profile of v1, /device:TPU:1, one launch (start us, length us, event | category | flops | bytes accessed | tf_op | source)
XLA Modules:
  0.0 660.8 jit_solution(4099694059083276408)
XLA Ops:
  70.1 7.0 %collective-permute-done.10.refs_7_ = bf16[4,64,1152]{2,1,0:T(8,128)(2,1)S(1)} collective-permute-done((bf16[4,64,1152]{2,1,0:T(8,128)(2,1)}, bf16[4,64,1152]{2,1,0:T(8,128)(2,1)S(1)}, u32[]{:S(2)}, u32[]{:S(2)}) %collective-permute-start.10) | collective-permute-done | bytes 589856 | tf_op jit(solution)/shard_map/ppermute | solution.py:64
  91.1 12.7 %shard_map.294 = (f32[16,128,384]{2,1,0:T(8,128)}, f32[16,128,384]{2,1,0:T(8,128)}, bf16[16,128,1024]{2,1,0:T(8,128)(2,1)}) custom-call(s32[12]{0:T(128)} %stack.51.info, f32[1,1024]{1,0:T(1,128)} %dynamic-slice_convert_fusion.gain, bf16[384,1024]{1,0:T(8,128)(2,1)} %get-tuple-element.254.own, bf16[384,1024]{1,0:T(8,128)(2,1)} %collective-permute-done.15.came, ...), custom_call_target="tpu_custom_call" | custom-call | flops 3221225472 | bytes 20000000 | tf_op jit(solution)/shard_map/pallas_call | solution.py:965
  113.3 13.5 %shard_map.295 = (bf16[16,128,128]{2,1,0:T(8,128)(2,1)}, f32[2048,256]{1,0:T(8,128)}, bf16[2048,128]{1,0:T(8,128)(2,1)}, bf16[2048,128]{1,0:T(8,128)(2,1)}, bf16...) custom-call(f32[16,128,384]{2,1,0:T(8,128)} %get-tuple-element.256.own, f32[16,128,384]{2,1,0:T(8,128)} %copy-done.73, ...), custom_call_target="tpu_custom_call" | custom-call | flops 4000000000 | bytes 30000000 | tf_op jit(solution)/shard_map/pallas_call | solution.py:973
  130.3 5.2 shard_map.296
  138.4 9.1 %collective-permute-done.19 = bf16[4,64,1024]{2,1,0:T(8,128)(2,1)S(1)} collective-permute-done((bf16[4,64,1024]{2,1,0:T(8,128)(2,1)}, bf16[4,64,1024]{2,1,0:T(8,128)(2,1)S(1)}, u32[]{:S(2)}, u32[]{:S(2)}) %collective-permute-start.19) | collective-permute-done | bytes 524320 | tf_op jit(solution)/shard_map/ppermute | solution.py:64
  223.9 7.1 %collective-permute-done.40.refs_7_ = bf16[4,64,1152]{2,1,0:T(8,128)(2,1)S(1)} collective-permute-done((bf16[4,64,1152]{2,1,0:T(8,128)(2,1)}, bf16[4,64,1152]{2,1,0:T(8,128)(2,1)S(1)}, u32[]{:S(2)}, u32[]{:S(2)}) %collective-permute-start.40) | collective-permute-done | bytes 589856 | tf_op jit(solution)/shard_map/ppermute | solution.py:64
  235.1 5.4 collective-permute-done.39.refs_1_
  242.6 9.3 %shard_map.303.grads = bf16[4,512,2048]{2,1,0:T(8,128)(2,1)} custom-call(s32[12]{0:T(128)} %stack.51.info, bf16[16,128,128]{2,1,0:T(8,128)(2,1)} %get-tuple-element.251.chosen, bf16[16,128,1024]{2,1,0:T(8,128)(2,1)} %all-gather.12.cloned.1.call-done.own, bf16[16,128,1024]{2,1,0:T(8,128)(2,1)} %collective-permute-done.44.other), custom_call_target="tpu_custom_call" | custom-call | flops 4000000000 | bytes 20000000 | tf_op jit(solution)/shard_map/pallas_call | solution.py:1010
  258.4 9.6 %shard_map.304 = (bf16[4,512,2048]{2,1,0:T(8,128)(2,1)}, bf16[4,512,128]{2,1,0:T(8,128)(2,1)}) custom-call(s32[12]{0:T(128)} %stack.51.info, bf16[16,128,128]{2,1,0:T(8,128)(2,1)} %get-tuple-element.251.chosen, bf16[4,64,1152]{2,1,0:T(8,128)(2,1)} %shard_map.301.refs_0_, bf16[4,64,1152]{2,1,0:T(8,128)(2,1)} %copy-done.79, bf16[4,64,1152]{2,1,0:T(8,128)(2,1)} %copy-done.80, ...), custom_call_target="tpu_custom_call" | custom-call | flops 4000000000 | bytes 20000000 | tf_op jit(solution)/shard_map/pallas_call | solution.py:1022
  268.4 30.1 %shard_map.305 = (bf16[4,512,1024]{2,1,0:T(8,128)(2,1)}, bf16[4,512,1024]{2,1,0:T(8,128)(2,1)}, bf16[4,512,128]{2,1,0:T(8,128)(2,1)}, bf16[4,512,384]{2,1,0:T(8,128)(2,1)}, bf16[4,512,768]{2,1,0:T(8,128)(2,1)}) custom-call(s32[12]{0:T(128)} %stack.51.info, bf16[4,512,2048]{2,1,0:T(8,128)(2,1)} %get-tuple-element.306.rows, ...), custom_call_target="tpu_custom_call" | custom-call | flops 16106127360 | bytes 50000000 | tf_op jit(solution)/shard_map/pallas_call | solution.py:756
  298.9 12.4 %shard_map.306 = (bf16[4,512,384]{2,1,0:T(8,128)(2,1)}, bf16[4,512,384]{2,1,0:T(8,128)(2,1)}, bf16[4,512,384]{2,1,0:T(8,128)(2,1)}, bf16[4,512,384]{2,1,0:T(8,12...) custom-call(s32[12]{0:T(128)} %stack.51.info, ...), custom_call_target="tpu_custom_call" | custom-call | flops 6442450944 | bytes 30000000 | tf_op jit(solution)/shard_map/pallas_call | solution.py:756
  315.9 7.4 %shard_map.307 = (bf16[4,64,1152]{2,1,0:T(8,128)(2,1)}, bf16[4,64,1152]{2,1,0:T(8,128)(2,1)}, bf16[4,64,1152]{2,1,0:T(8,128)(2,1)}, bf16[4,64,1152]{2,1,0:T(8,12...) custom-call(s32[12]{0:T(128)} %stack.51.info, ...), custom_call_target="tpu_custom_call" | custom-call | flops 2000000000 | bytes 20000000 | tf_op jit(solution)/shard_map/pallas_call | solution.py:1051
  323.2 16.4 %shard_map.308 = (bf16[4,512,1024]{2,1,0:T(8,128)(2,1)}, bf16[4,512,1024]{2,1,0:T(8,128)(2,1)}, bf16[4,384,512]{2,1,0:T(8,128)(2,1)}, bf16[4,384,512]{2,1,0:T(8,...) custom-call(s32[12]{0:T(128)} %stack.51.info, bf16[4,512,2048]{2,1,0:T(8,128)(2,1)} %shard_map.303.grads, ...), custom_call_target="tpu_custom_call" | custom-call | flops 6442450944 | bytes 30000000 | tf_op jit(solution)/shard_map/pallas_call | solution.py:756
  342.0 5.5 collective-permute-done.58
  389.7 6.9 %collective-permute-done.63.c = bf16[64,1152]{1,0:T(8,128)(2,1)S(1)} collective-permute-done((bf16[64,1152]{1,0:T(8,128)(2,1)}, bf16[64,1152]{1,0:T(8,128)(2,1)S(1)}, u32[]{:S(2)}, u32[]{:S(2)}) %collective-permute-start.63) | collective-permute-done | bytes 147488 | tf_op jit(solution)/shard_map/ppermute | solution.py:64
  401.4 6.9 %shard_map.311 = (bf16[4,64,1024]{2,1,0:T(8,128)(2,1)}, bf16[4,64,1024]{2,1,0:T(8,128)(2,1)}, bf16[4,64,1024]{2,1,0:T(8,128)(2,1)}, bf16[4,64,1024]{2,1,0:T(8,12...) custom-call(s32[12]{0:T(128)} %stack.51.info, ...), custom_call_target="tpu_custom_call" | custom-call | flops 2000000000 | bytes 20000000 | tf_op jit(solution)/shard_map/pallas_call | solution.py:1066
  414.5 5.0 shard_map.313
  419.5 6.4 shard_map.314
  425.9 7.5 %all-to-all-start = ((bf16[16,128,128]{2,1,0:T(8,128)(2,1)}), bf16[16,128,128]{2,1,0:T(8,128)(2,1)}, u32[]{:S(2)}, u32[]{:S(2)}) async-start(bf16[16,128,128]{2,1,0:T(8,128)(2,1)} %shard_map.314), calls=%async_computation | async-start | bytes 1048576 | tf_op jit(solution)/shard_map/all_to_all | solution.py:1102
  438.0 8.1 %all-to-all-done = bf16[16,128,128]{2,1,0:T(8,128)(2,1)} async-done(((bf16[16,128,128]{2,1,0:T(8,128)(2,1)}), bf16[16,128,128]{2,1,0:T(8,128)(2,1)}, u32[]{:S(2)}, u32[]{:S(2)}) %all-to-all-start) | async-done | bytes 524320 | tf_op jit(solution)/shard_map/all_to_all | solution.py:1102
  446.1 16.5 %shard_map.315 = (bf16[16,128,384]{2,1,0:T(8,128)(2,1)}, f32[8,128]{1,0:T(8,128)}) custom-call(bf16[2048,128]{1,0:T(8,128)(2,1)} %bitcast.27.grad_mixed, f32[2048,256]{1,0:T(8,128)} %get-tuple-element.363.raw, bf16[2048,128]{1,0:T(8,128)(2,1)} %get-tuple-element.364.queries, bf16[2048,128]{1,0:T(8,128)(2,1)} %get-tuple-element.365.keys, ...), custom_call_target="tpu_custom_call" | custom-call | flops 8000000000 | bytes 30000000 | tf_op jit(solution)/shard_map/pallas_call | solution.py:1103
  473.8 7.5 %shard_map.316 = (bf16[384,1024]{1,0:T(8,128)(2,1)}, bf16[384,1024]{1,0:T(8,128)(2,1)}) custom-call(bf16[16,128,384]{2,1,0:T(8,128)(2,1)} %get-tuple-element.368.grads, bf16[16,128,384]{2,1,0:T(8,128)(2,1)} %copy-done.17, bf16[16,128,1024]{2,1,0:T(8,128)(2,1)} %get-tuple-element.369.normed), custom_call_target="tpu_custom_call" | custom-call | flops 3221225472 | bytes 20000000 | tf_op jit(solution)/shard_map/pallas_call | solution.py:1115
  487.1 12.8 %shard_map.317 = (bf16[4,64,2048]{2,1,0:T(8,128)(2,1)}, bf16[4,64,2048]{2,1,0:T(8,128)(2,1)}, bf16[4,64,2048]{2,1,0:T(8,128)(2,1)}, bf16[4,64,2048]{2,1,0:T(8,12...) custom-call(s32[12]{0:T(128)} %stack.51.info, ...), custom_call_target="tpu_custom_call" | custom-call | flops 3221225472 | bytes 30000000 | tf_op jit(solution)/shard_map/pallas_call | solution.py:1126
  516.4 5.0 collective-permute-done.85
  523.0 5.9 collective-permute-done.84
  551.1 8.3 %collective-permute-done.91.b = bf16[4,64,2048]{2,1,0:T(8,128)(2,1)S(1)} collective-permute-done((bf16[4,64,2048]{2,1,0:T(8,128)(2,1)S(1)}, bf16[4,64,2048]{2,1,0:T(8,128)(2,1)S(1)}, u32[]{:S(2)}, u32[]{:S(2)}) %collective-permute-start.91) | collective-permute-done | bytes 1048608 | tf_op jit(solution)/shard_map/ppermute | solution.py:64
  559.4 7.1 %collective-permute-done.90.b = bf16[4,64,2048]{2,1,0:T(8,128)(2,1)S(1)} collective-permute-done((bf16[4,64,2048]{2,1,0:T(8,128)(2,1)S(1)}, bf16[4,64,2048]{2,1,0:T(8,128)(2,1)S(1)}, u32[]{:S(2)}, u32[]{:S(2)}) %collective-permute-start.90) | collective-permute-done | bytes 1048608 | tf_op jit(solution)/shard_map/ppermute | solution.py:64
  579.7 5.9 collective-permute-done.92
  594.2 8.3 %collective-permute-done.101 = bf16[256,512]{1,0:T(8,128)(2,1)S(1)} collective-permute-done((bf16[256,512]{1,0:T(8,128)(2,1)S(1)}, bf16[256,512]{1,0:T(8,128)(2,1)S(1)}, u32[]{:S(2)}, u32[]{:S(2)}) %collective-permute-start.101) | collective-permute-done | bytes 262176 | tf_op jit(solution)/shard_map/ppermute | solution.py:111
  606.2 5.0 collective-permute-done.102
  613.8 5.9 collective-permute-done.97.b
  645.4 6.9 %shard_map.324 = (f32[512,2048]{1,0:T(8,128)}, f32[2048,512]{1,0:T(8,128)}, f32[64,512]{1,0:T(8,128)}, f32[1,512]{1,0:T(1,128)}, f32[1,512]{1,0:T(1,128)}, /*ind...) custom-call(s32[12]{0:T(128)} %stack.51.info, bf16[16,352,512]{2,1,0:T(8,128)(2,1)} %bitcast.42), custom_call_target="tpu_custom_call" | custom-call | flops 1000000 | bytes 1000000 | tf_op jit(solution)/shard_map/pallas_call | solution.py:1171
  (467 shorter events, 358.6 us)
Async XLA Ops:
  7.2 83.1 %all-gather.12.cloned.1.call-start = ((), (), s32[]{:S(2)}) async-start(), calls=%async_computation.1 | async-start | bytes 4456448 | tf_op jit(solution)/shard_map/all_gather | solution.py:923
  9.0 231.4 %all-gather.14.cloned.1.call-start = ((), (), s32[]{:S(2)}) async-start(), calls=%async_computation.2 | async-start | bytes 15728640 | tf_op jit(solution)/shard_map/all_gather | solution.py:924
  18.1 250.3 %all-gather.16.cloned.1.call-start = ((), (), s32[]{:S(2)}) async-start(), calls=%async_computation.3 | async-start | bytes 7864320 | tf_op jit(solution)/shard_map/all_gather | solution.py:972
  53.1 24.0 %collective-permute-start.10 = (bf16[4,64,1152]{2,1,0:T(8,128)(2,1)}, bf16[4,64,1152]{2,1,0:T(8,128)(2,1)S(1)}, u32[]{:S(2)}, u32[]{:S(2)}) collective-permute-start(bf16[4,64,1152]{2,1,0:T(8,128)(2,1)} %shard_map.291.refs_4_), channel_id=1, source_target_pairs={{0,2},{1,7},{2,4},{3,1},{4,6},{5,3},{6,0},{7,5},{8,10},{9,15},{10,... | collective-permute-start | bytes 1769480 | tf_op jit(solution)/shard_map/ppermute | solution.py:64
  53.1 25.4 %collective-permute-start.11 = (bf16[4,64,1152]{2,1,0:T(8,128)(2,1)}, bf16[4,64,1152]{2,1,0:T(8,128)(2,1)S(1)}, u32[]{:S(2)}, u32[]{:S(2)}) collective-permute-start(bf16[4,64,1152]{2,1,0:T(8,128)(2,1)} %shard_map.291.refs_4_), channel_id=1, source_target_pairs={{0,6},{1,3},{2,0},{3,5},{4,2},{5,7},{6,4},{7,1},{8,14},{9,11},{10,... | collective-permute-start | bytes 1769480 | tf_op jit(solution)/shard_map/ppermute | solution.py:64
  56.6 21.9 %collective-permute-start.8 = (bf16[4,64,1152]{2,1,0:T(8,128)(2,1)}, bf16[4,64,1152]{2,1,0:T(8,128)(2,1)S(1)}, u32[]{:S(2)}, u32[]{:S(2)}) collective-permute-start(bf16[4,64,1152]{2,1,0:T(8,128)(2,1)} %shard_map.290.refs_0_), channel_id=1, source_target_pairs={{0,8},{1,25},{2,10},{3,27},{4,12},{5,29},{6,14},{7,31},{8,16},{9,1... | collective-permute-start | bytes 1769480 | tf_op jit(solution)/shard_map/ppermute | solution.py:64
  68.2 22.1 %collective-permute-start.15 = (bf16[384,1024]{1,0:T(8,128)(2,1)}, bf16[384,1024]{1,0:T(8,128)(2,1)}, u32[]{:S(2)}, u32[]{:S(2)}) collective-permute-start(bf16[384,1024]{1,0:T(8,128)(2,1)} %get-tuple-element.255), channel_id=1, source_target_pairs={{0,1},{1,0},{2,3},{3,2},{4,5},{5,4},{6,7},{7,6},{8,9},{9,8},{10,11... | collective-permute-start | bytes 2359304 | tf_op jit(solution)/shard_map/ppermute | solution.py:82
  106.8 312.8 %all-gather.18.cloned.1.call-start = ((), (), s32[]{:S(2)}) async-start(), calls=%async_computation.4 | async-start | bytes 8912896 | tf_op jit(solution)/shard_map/all_gather | solution.py:1050
  197.4 45.1 %collective-permute-start.44 = (bf16[16,128,1024]{2,1,0:T(8,128)(2,1)}, bf16[16,128,1024]{2,1,0:T(8,128)(2,1)}, u32[]{:S(2)}, u32[]{:S(2)}) collective-permute-start(bf16[16,128,1024]{2,1,0:T(8,128)(2,1)} %all-gather.12.cloned.1.call-done.own), channel_id=1, source_target_pairs={{0,1},{1,0},{2,3},{3,2},{4,5},{5,4},{6,7},{7,6},{8,9},{9,8},{10,11... | collective-permute-start | bytes 12582920 | tf_op jit(solution)/shard_map/ppermute | solution.py:82
  268.1 214.1 %all-gather.20.cloned.1.call-start = ((), (), s32[]{:S(2)}) async-start(), calls=%async_computation.5 | async-start | bytes 4456448 | tf_op jit(solution)/shard_map/all_gather | solution.py:1092
  311.4 36.1 %collective-permute-start.58 = (bf16[4,512,384]{2,1,0:T(8,128)(2,1)}, bf16[4,512,384]{2,1,0:T(8,128)(2,1)S(1)}, u32[]{:S(2)}, u32[]{:S(2)}) collective-permute-start(bf16[4,512,384]{2,1,0:T(8,128)(2,1)} %get-tuple-element.324), channel_id=1, source_target_pairs={{0,32},{1,97},{32,64},{33,1},{64,96},{65,33},{96,0},{97,65},{2,34}... | collective-permute-start | bytes 4718600 | tf_op jit(solution)/shard_map/ppermute | solution.py:64
  313.8 35.8 %collective-permute-start.59 = (bf16[4,512,384]{2,1,0:T(8,128)(2,1)}, bf16[4,512,384]{2,1,0:T(8,128)(2,1)S(1)}, u32[]{:S(2)}, u32[]{:S(2)}) collective-permute-start(bf16[4,512,384]{2,1,0:T(8,128)(2,1)} %get-tuple-element.325), channel_id=1, source_target_pairs={{0,96},{1,33},{32,0},{33,65},{64,32},{65,97},{96,64},{97,1},{2,98}... | collective-permute-start | bytes 4718600 | tf_op jit(solution)/shard_map/ppermute | solution.py:64
  339.6 59.8 %collective-permute-start.70 = (bf16[4,512,1024]{2,1,0:T(8,128)(2,1)}, bf16[4,512,1024]{2,1,0:T(8,128)(2,1)S(1)}, u32[]{:S(2)}, u32[]{:S(2)}) collective-permute-start(bf16[4,512,1024]{2,1,0:T(8,128)(2,1)} %get-tuple-element.347), channel_id=1, source_target_pairs={{0,1},{1,0},{2,3},{3,2},{4,5},{5,4},{6,7},{7,6},{8,9},{9,8},{10,11... | collective-permute-start | bytes 12582920 | tf_op jit(solution)/shard_map/ppermute | solution.py:82
  370.4 37.9 %collective-permute-start.68 = (bf16[4,512,384]{2,1,0:T(8,128)(2,1)S(1)}, bf16[4,512,384]{2,1,0:T(8,128)(2,1)}, u32[]{:S(2)}, u32[]{:S(2)}) collective-permute-start(bf16[4,512,384]{2,1,0:T(8,128)(2,1)S(1)} %add_convert_fusion.2), channel_id=1, source_target_pairs={{0,32},{1,97},{32,64},{33,1},{64,96},{65,33},{96,0},{97,65},{2,34}... | collective-permute-start | bytes 4718600 | tf_op jit(solution)/shard_map/ppermute | solution.py:64
  372.1 36.2 %collective-permute-start.69 = (bf16[4,512,384]{2,1,0:T(8,128)(2,1)}, bf16[4,512,384]{2,1,0:T(8,128)(2,1)S(1)}, u32[]{:S(2)}, u32[]{:S(2)}) collective-permute-start(bf16[4,512,384]{2,1,0:T(8,128)(2,1)} %get-tuple-element.346), channel_id=1, source_target_pairs={{0,32},{1,97},{32,64},{33,1},{64,96},{65,33},{96,0},{97,65},{2,34}... | collective-permute-start | bytes 4718600 | tf_op jit(solution)/shard_map/ppermute | solution.py:64
  425.9 20.2 %all-to-all-start = ((bf16[16,128,128]{2,1,0:T(8,128)(2,1)}), bf16[16,128,128]{2,1,0:T(8,128)(2,1)}, u32[]{:S(2)}, u32[]{:S(2)}) async-start(bf16[16,128,128]{2,1,0:T(8,128)(2,1)} %shard_map.314), calls=%async_computation | async-start | bytes 1048576 | tf_op jit(solution)/shard_map/all_to_all | solution.py:1102
  433.5 211.9 %all-gather.22.cloned.1.call-start = ((), (), s32[]{:S(2)}) async-start(), calls=%async_computation.6 | async-start | bytes 6127616 | tf_op jit(solution)/shard_map/all_gather | solution.py:1154
  433.5 34.1 %collective-permute-start.73 = (bf16[4,512,384]{2,1,0:T(8,128)(2,1)}, bf16[4,512,384]{2,1,0:T(8,128)(2,1)}, u32[]{:S(2)}, u32[]{:S(2)}) collective-permute-start(bf16[4,512,384]{2,1,0:T(8,128)(2,1)} %get-tuple-element.372), channel_id=1, source_target_pairs={{0,96},{1,33},{32,0},{33,65},{64,32},{65,97},{96,64},{97,1},{2,98}... | collective-permute-start | bytes 4718600 | tf_op jit(solution)/shard_map/ppermute | solution.py:64
  436.3 35.2 %collective-permute-start.74 = (bf16[4,512,384]{2,1,0:T(8,128)(2,1)}, bf16[4,512,384]{2,1,0:T(8,128)(2,1)S(1)}, u32[]{:S(2)}, u32[]{:S(2)}) collective-permute-start(bf16[4,512,384]{2,1,0:T(8,128)(2,1)} %add_convert_fusion.1), channel_id=1, source_target_pairs={{0,32},{1,97},{32,64},{33,1},{64,96},{65,33},{96,0},{97,65},{2,34}... | collective-permute-start | bytes 4718600 | tf_op jit(solution)/shard_map/ppermute | solution.py:64
  467.6 41.7 %collective-permute-start.88 = (bf16[4,384,512]{2,1,0:T(8,128)(2,1)}, bf16[4,384,512]{2,1,0:T(8,128)(2,1)S(1)}, u32[]{:S(2)}, u32[]{:S(2)}) collective-permute-start(bf16[4,384,512]{2,1,0:T(8,128)(2,1)} %get-tuple-element.404), channel_id=1, source_target_pairs={{0,32},{1,97},{32,64},{33,1},{64,96},{65,33},{96,0},{97,65},{2,34}... | collective-permute-start | bytes 4718600 | tf_op jit(solution)/shard_map/ppermute | solution.py:64
  471.4 40.4 %collective-permute-start.89 = (bf16[4,384,512]{2,1,0:T(8,128)(2,1)}, bf16[4,384,512]{2,1,0:T(8,128)(2,1)}, u32[]{:S(2)}, u32[]{:S(2)}) collective-permute-start(bf16[4,384,512]{2,1,0:T(8,128)(2,1)} %get-tuple-element.406), channel_id=1, source_target_pairs={{0,96},{1,33},{32,0},{33,65},{64,32},{65,97},{96,64},{97,1},{2,98}... | collective-permute-start | bytes 4718600 | tf_op jit(solution)/shard_map/ppermute | solution.py:64
  481.2 23.3 %collective-permute-start.79 = (bf16[384,1024]{1,0:T(8,128)(2,1)}, bf16[384,1024]{1,0:T(8,128)(2,1)}, u32[]{:S(2)}, u32[]{:S(2)}) collective-permute-start(bf16[384,1024]{1,0:T(8,128)(2,1)} %get-tuple-element.389), channel_id=1, source_target_pairs={{0,1},{1,0},{2,3},{3,2},{4,5},{5,4},{6,7},{7,6},{8,9},{9,8},{10,11... | collective-permute-start | bytes 2359304 | tf_op jit(solution)/shard_map/ppermute | solution.py:82
  501.5 27.4 %collective-permute-start.75 = (bf16[4,64,2048]{2,1,0:T(8,128)(2,1)}, bf16[4,64,2048]{2,1,0:T(8,128)(2,1)}, u32[]{:S(2)}, u32[]{:S(2)}) collective-permute-start(bf16[4,64,2048]{2,1,0:T(8,128)(2,1)} %get-tuple-element.385), channel_id=1, source_target_pairs={{0,8},{1,25},{2,10},{3,27},{4,12},{5,29},{6,14},{7,31},{8,16},{9,1... | collective-permute-start | bytes 3145736 | tf_op jit(solution)/shard_map/ppermute | solution.py:64
  509.3 22.2 %collective-permute-start.76 = (bf16[4,64,2048]{2,1,0:T(8,128)(2,1)}, bf16[4,64,2048]{2,1,0:T(8,128)(2,1)}, u32[]{:S(2)}, u32[]{:S(2)}) collective-permute-start(bf16[4,64,2048]{2,1,0:T(8,128)(2,1)} %get-tuple-element.386), channel_id=1, source_target_pairs={{0,24},{1,9},{2,26},{3,11},{4,28},{5,13},{6,30},{7,15},{8,0},{9,17... | collective-permute-start | bytes 3145736 | tf_op jit(solution)/shard_map/ppermute | solution.py:64
  509.4 23.8 %collective-permute-start.77 = (bf16[4,64,2048]{2,1,0:T(8,128)(2,1)S(1)}, bf16[4,64,2048]{2,1,0:T(8,128)(2,1)}, u32[]{:S(2)}, u32[]{:S(2)}) collective-permute-start(bf16[4,64,2048]{2,1,0:T(8,128)(2,1)S(1)} %copy-done.75), channel_id=1, source_target_pairs={{0,2},{1,7},{2,4},{3,1},{4,6},{5,3},{6,0},{7,5},{8,10},{9,15},{10,... | collective-permute-start | bytes 3145736 | tf_op jit(solution)/shard_map/ppermute | solution.py:64
  511.8 24.7 %collective-permute-start.78 = (bf16[4,64,2048]{2,1,0:T(8,128)(2,1)S(1)}, bf16[4,64,2048]{2,1,0:T(8,128)(2,1)}, u32[]{:S(2)}, u32[]{:S(2)}) collective-permute-start(bf16[4,64,2048]{2,1,0:T(8,128)(2,1)S(1)} %copy-done.74), channel_id=1, source_target_pairs={{0,6},{1,3},{2,0},{3,5},{4,2},{5,7},{6,4},{7,1},{8,14},{9,11},{10,... | collective-permute-start | bytes 3145736 | tf_op jit(solution)/shard_map/ppermute | solution.py:64
  546.6 19.9 %collective-permute-start.90 = (bf16[4,64,2048]{2,1,0:T(8,128)(2,1)S(1)}, bf16[4,64,2048]{2,1,0:T(8,128)(2,1)S(1)}, u32[]{:S(2)}, u32[]{:S(2)}) collective-permute-start(bf16[4,64,2048]{2,1,0:T(8,128)(2,1)S(1)} %add_convert_fusion.4), channel_id=1, source_target_pairs={{0,8},{1,25},{2,10},{3,27},{4,12},{5,29},{6,14},{7,31},{8,16},{9,1... | collective-permute-start | bytes 3145736 | tf_op jit(solution)/shard_map/ppermute | solution.py:64
  547.5 28.8 %collective-permute-start.96 = (bf16[256,512]{1,0:T(8,128)(2,1)}, bf16[256,512]{1,0:T(8,128)(2,1)}, u32[]{:S(2)}, u32[]{:S(2)}) collective-permute-start(bf16[256,512]{1,0:T(8,128)(2,1)} %add_convert_fusion.16), channel_id=1, source_target_pairs={{0,32},{1,97},{32,64},{33,1},{64,96},{65,33},{96,0},{97,65},{2,34}... | collective-permute-start | bytes 786440 | tf_op jit(solution)/shard_map/ppermute | solution.py:64
  576.2 37.6 %collective-permute-start.99 = (bf16[4,384,512]{2,1,0:T(8,128)(2,1)S(1)}, bf16[4,384,512]{2,1,0:T(8,128)(2,1)S(1)}, u32[]{:S(2)}, u32[]{:S(2)}) collective-permute-start(bf16[4,384,512]{2,1,0:T(8,128)(2,1)S(1)} %add_convert_fusion), channel_id=1, source_target_pairs={{0,32},{1,97},{32,64},{33,1},{64,96},{65,33},{96,0},{97,65},{2,34}... | collective-permute-start | bytes 4718600 | tf_op jit(solution)/shard_map/ppermute | solution.py:64
  589.3 21.9 %collective-permute-start.102 = (bf16[256,512]{1,0:T(8,128)(2,1)S(1)}, bf16[256,512]{1,0:T(8,128)(2,1)S(1)}, u32[]{:S(2)}, u32[]{:S(2)}) collective-permute-start(bf16[256,512]{1,0:T(8,128)(2,1)S(1)} %add_convert_fusion.13), channel_id=1, source_target_pairs={{0,4},{2,6},{4,0},{6,2},{8,12},{10,14},{12,8},{14,10},{16,20},{18,... | collective-permute-start | bytes 786440 | tf_op jit(solution)/shard_map/ppermute | solution.py:111
  589.3 24.2 %collective-permute-start.103 = (bf16[256,512]{1,0:T(8,128)(2,1)S(1)}, bf16[256,512]{1,0:T(8,128)(2,1)S(1)}, u32[]{:S(2)}, u32[]{:S(2)}) collective-permute-start(bf16[256,512]{1,0:T(8,128)(2,1)S(1)} %add_convert_fusion.13), channel_id=1, source_target_pairs={{0,6},{2,0},{4,2},{6,4},{8,14},{10,8},{12,10},{14,12},{16,22},{18,... | collective-permute-start | bytes 786440 | tf_op jit(solution)/shard_map/ppermute | solution.py:111
  592.8 21.0 %collective-permute-start.98 = (bf16[64,2048]{1,0:T(8,128)(2,1)S(1)}, bf16[64,2048]{1,0:T(8,128)(2,1)}, u32[]{:S(2)}, u32[]{:S(2)}) collective-permute-start(bf16[64,2048]{1,0:T(8,128)(2,1)S(1)} %add_convert_fusion.14), channel_id=1, source_target_pairs={{0,8},{1,25},{2,10},{3,27},{4,12},{5,29},{6,14},{7,31},{8,16},{9,1... | collective-permute-start | bytes 786440 | tf_op jit(solution)/shard_map/ppermute | solution.py:64
  (173 other events, 1671.3 us)
Sparse Core Ops, SparseCore 0:
  10.7 65.0 all-gather.11
  78.0 120.9 all-gather.13
  200.7 66.6 all-gather.15
  269.9 71.5 all-gather.17
  419.6 56.1 all-gather.19
  540.6 78.8 all-gather.21

commit v2 on v1

--- a/solution.py
+++ b/solution.py
@@ -103,6 +103,11 @@
 
 def across(value, step):
     pairs = [(i, i ^ (SIDE * step)) for i in range(SIDE * SIDE)]
+    return lax.ppermute(value, "context", pairs)
+
+
+def along_x(value, step):
+    pairs = [(i, (i + SIDE * step) % (SIDE * SIDE)) for i in range(SIDE * SIDE)]
     return lax.ppermute(value, "context", pairs)
 
 
@@ -146,8 +151,36 @@
     return [left, left_ahead, left_far, left_behind], [right, right_ahead, right_far, right_behind]
 
 
+def two_short_gathers(left, right, events=()):
+    left_moves, right_moves = moves_z(), moves_x()
+    values = (
+        left_moves[1](left),
+        along_z(left, 2),
+        left_moves[0](left),
+        right_moves[1](right),
+        along_x(right, 2),
+        right_moves[0](right),
+    )
+    values = together(*values, *events)[:6]
+    return [left, *values[:3]], [right, *values[3:]]
+
+
+def two_short_scatters(left, right, events=()):
+    left_moves, right_moves = moves_z(), moves_x()
+    values = (
+        left_moves[1](left[3]),
+        along_z(left[2], 2),
+        left_moves[0](left[1]),
+        right_moves[1](right[3]),
+        along_x(right[2], 2),
+        right_moves[0](right[1]),
+    )
+    values = together(*values, *events)[:6]
+    return (left[0], *values[:3]), (right[0], *values[3:])
+
+
 def plane_gather(first, second, events=((), (), (), ())):
-    first_near, second_near = two_gathers(first, second, moves_z(), moves_x(), *events[:2])
+    first_near, second_near = two_short_gathers(first, second, events[0])
     first_pieces, second_pieces = two_gathers(
         stack(first_near), stack(second_near), moves_x(), moves_z(), *events[2:]
     )
@@ -164,9 +197,11 @@
     return call(unstack_kernel, [whole] * 3, [(shape, bf16)] * 4)(*terms)
 
 
-def total_kernel(a, b, c, d, e, f, result):
-    result[:HALF] = a[...].astype(f32) + b[...].astype(f32) + c[...].astype(f32)
-    result[HALF:] = d[...].astype(f32) + e[...].astype(f32) + f[...].astype(f32)
+def total_kernel(*refs):
+    result = refs[8]
+    for i in range(2):
+        a, b, c, d = (part[...].astype(f32) for part in refs[4 * i : 4 * i + 4])
+        result[i * HALF : (i + 1) * HALF] = (a + b) + (c + d)
 
 
 def two_scatters(left, right, left_moves, right_moves, events=(), last=()):
@@ -185,27 +220,15 @@
     return left_terms, right_terms, events, last
 
 
-def plane_scatter(pieces, events=((), (), (), ())):
+def plane_scatter(pieces, events=((), (), ())):
     first, second, *_ = two_scatters(pieces[:4], pieces[4:], moves_x(), moves_z(), *events[:2])
-    first, second, *_ = two_scatters(unstack(first), unstack(second), moves_z(), moves_x(), *events[2:])
-    width = pieces[0].shape[-1]
-    return call(total_kernel, [whole] * 6, [((2 * HALF, width), f32)])(*first, *second)[0]
-
-
-def scatter_chain(arrays, moves):
-    done = []
-    results = []
-
-    def step(move, value):
-        done.append(move(after(value, *done[-2:-1])))
-        return done[-1]
-
-    for parts in arrays:
-        passing = step(moves[0], parts[2])
-        from_ahead = step(moves[1], parts[3])
-        from_behind = step(moves[0], add_low(parts[1], passing))
-        results.append((passing, from_ahead, from_behind))
-    return results
+    first, second = two_short_scatters(unstack(first), unstack(second), events[2])
+    return total(first, second)
+
+
+def total(first, second):
+    width = first[0].shape[-1]
+    return call(total_kernel, [whole] * 8, [((2 * HALF, width), f32)])(*first, *second)[0]
 
 
 def split_low(value, count):
@@ -261,10 +284,10 @@
     result[base:] = gains.astype(bf16)
 
 
-def dense_split_kernel(info, a, b, c, d, own, away, own_out, away_out, out, extra):
+def dense_split_kernel(info, a, b, c, d, own, away, own_out, away_out, extra):
     shard = a.shape[1]
     rows = own.shape[0]
-    size = out.shape[0]
+    size = own_out.shape[0]
     core = info[0]
     for i, piece in enumerate((a, b, c, d)):
         place = info[4 + i]
@@ -280,9 +303,7 @@
             away[:, columns] = piece[:rows]
             away_out[:, columns] = piece[rows : rows + size]
 
-        columns = core_columns(place, shard)
-        out[:, columns] = piece[rows : rows + size]
-        extra[:, columns] = piece[rows + size :]
+        extra[:, core_columns(place, shard)] = piece[rows + size :]
 
 
 def slots_kernel(info, *refs):
@@ -365,15 +386,10 @@
             pieces[4 + iz][ix, :, half:] = marks[HALF:]
 
 
-def put_sums_kernel(info, chosen, own, came, *pieces):
-    place_x, place_z, sign = info[8], info[9], info[10]
-    for ix in range(SIDE):
-        for iz in range(SIDE):
-            place = ((place_x + sign * ix) % SIDE) * SIDE + (place_z + sign * iz) % SIDE
-            rows = read_slots(own, place, slice(None)).astype(f32) + read_slots(came, place, slice(None)).astype(f32)
-            rows = dot_nn(chosen[place], rows.astype(bf16)).astype(bf16)
-            pieces[ix][iz] = rows[:HALF]
-            pieces[4 + iz][ix] = rows[HALF:]
+def put_spans_kernel(chosen, own, came, result):
+    for place in range(SIDE * SIDE):
+        rows = read_slots(own, place, slice(None)).astype(f32) + read_slots(came, place, slice(None)).astype(f32)
+        result[place] = dot_nn(chosen[place], rows.astype(bf16)).astype(bf16)
 
 
 def span_of(info, ix, iz):
@@ -405,7 +421,7 @@
             cut = slice(j * HALF, (j + 1) * HALF)
             normed_out[span, part] = normed[cut]
             own_out[span, part] = own_rows[cut]
-            other_out[span, part] = other_rows[cut]
+            other_out[span, part] = other_rows[cut].astype(bf16)
 
 
 def turn(value, cosine, sine):
@@ -437,7 +453,7 @@
 
     def prepare(j, carry):
         rows = pl.ds(pl.multiple_of(j * span, span), span)
-        block = own[j] + came[j]
+        block = own[j] + came[j].astype(f32)
         raw[rows, :] = block[:, : 2 * size]
         cos_rows = cosine[rows, :]
         sin_rows = sine[rows, :]
@@ -469,13 +485,14 @@
 
 
 def attend_back_kernel(
-    grad_mixed, raw, queries, keys, values, log_totals, cosine, sine, gains, doc_rows, doc_columns, pads,
-    grads, gain_grads, grad_queries, grad_keys, grad_values,
+    own, came, raw, queries, keys, values, log_totals, cosine, sine, gains, doc_rows, doc_columns, pads,
+    grads, gain_grads, grad_mixed, grad_queries, grad_keys, grad_values,
 ):
     count = queries.shape[0]
     size = queries.shape[1]
     span = grads.shape[1]
     scale = size ** (-0.5)
+    grad_mixed[...] = (own[...] + came[...]).astype(bf16).reshape(count, size)
     grad_keys[...] = jnp.zeros_like(grad_keys)
     grad_values[...] = jnp.zeros_like(grad_values)
     real = real_count(pads, float(count))
@@ -527,45 +544,49 @@
         piece[...] = rows.astype(bf16).reshape(piece.shape)
 
 
-def heads_back_kernel(rows, weight, result):
-    for i in range(weight.shape[0]):
-        result[i] = dot_nt(rows[...], weight[i]).astype(bf16)
-
-
-def out_grad_kernel(mixed, came_mixed, rows, own_out, away_out):
-    size = mixed.shape[-1]
-    count = mixed.shape[0] * mixed.shape[1]
-    grads = rows[...].reshape(count, rows.shape[-1])
-    own_out[...] = dot_tn(mixed[...].reshape(count, size), grads).astype(bf16)
-    away_out[...] = dot_tn(came_mixed[...].reshape(count, size), grads).astype(bf16)
-
-
-def input_back_kernel(info, grads, came_grads, own, came, *refs):
-    tokens, mixture, pieces, gain_grad = refs[:8], refs[8:16], refs[16:24], refs[24]
-    half = own.shape[1]
-    count = SIDE * HALF
-    lanes = lax.broadcasted_iota(jnp.int32, (count, EXTRA), 1)
-    total = jnp.zeros((1, half), f32)
+def heads_back_kernel(info, own, came, *refs):
+    pieces, (own_out, other_out) = refs[:8], refs[8:]
+    for i, piece in enumerate(pieces):
+        rows = piece[...].reshape(SIDE * HALF, piece.shape[-1])
+        own_rows = dot_nt(rows, own[...])
+        other_rows = dot_nt(rows, came[...])
+        for j, span, part in piece_parts(info, i):
+            cut = slice(j * HALF, (j + 1) * HALF)
+            own_out[span, part] = own_rows[cut]
+            other_out[span, part] = other_rows[cut]
+
+
+def out_grad_kernel(info, mixed, came_mixed, *refs):
+    pieces, (own_out, away_out) = refs[:8], refs[8:]
+    own_total = away_total = 0.0
+    for i, piece in enumerate(pieces):
+        rows = piece[...].reshape(SIDE * HALF, piece.shape[-1])
+        parts = list(piece_parts(info, i))
+        own_total += dot_tn(join([mixed[span, part] for _, span, part in parts]), rows)
+        away_total += dot_tn(join([came_mixed[span, part] for _, span, part in parts]), rows)
+    own_out[...] = own_total.astype(bf16)
+    away_out[...] = away_total.astype(bf16)
+
+
+def input_back_kernel(info, grads, came_grads, own, came, *pieces):
     for i, piece in enumerate(pieces):
         parts = list(piece_parts(info, i))
         left = join([grads[span, part] for _, span, part in parts])
         right = join([came_grads[span, part] for _, span, part in parts])
         rows = dot_nn(left, own[...]) + dot_nn(right, came[...])
-        piece[:, :, :half] = rows.astype(bf16).reshape(SIDE, HALF, half)
-        piece[:, :, half:] = mixture[i][...]
-        source = tokens[i][...].reshape(count, half + EXTRA)
-        marks = jnp.where((lanes >= 9) & (lanes < 12), source[:, half:].astype(f32), 0.0)
-        inverse = jnp.sum(marks, axis=-1, keepdims=True)
-        total += jnp.sum(rows * (source[:, :half].astype(f32) * inverse), axis=0, keepdims=True)
-    gain_grad[...] = jnp.broadcast_to(total, gain_grad.shape)
-
-
-def project_grad_kernel(grads, came_grads, normed, own_out, away_out):
+        piece[...] = rows.astype(bf16).reshape(piece.shape)
+
+
+def project_grad_kernel(grads, came_grads, normed, own, came, gain, own_out, away_out, gain_grad):
     count = normed.shape[0] * normed.shape[1]
     wide = grads.shape[-1]
     rows = normed[...].reshape(count, normed.shape[-1])
-    own_out[...] = dot_tn(grads[...].reshape(count, wide), rows).astype(bf16)
-    away_out[...] = dot_tn(came_grads[...].reshape(count, wide), rows).astype(bf16)
+    total = 0.0
+    for source, weight, target in ((grads, own, own_out), (came_grads, came, away_out)):
+        result = dot_tn(source[...].reshape(count, wide), rows)
+        target[...] = result.astype(bf16)
+        total += jnp.sum(result * weight[...].astype(f32), axis=0, keepdims=True)
+    gain_grad[...] = jnp.broadcast_to(total / gain[...], gain_grad.shape)
 
 
 def halves(core, own, came):
@@ -613,7 +634,7 @@
 
 def router_back_kernel(
     info, own, came, residual_ref, inverse_ref, normed, probs_ref, gates_ref, total, ids, padding, cotangent, extra,
-    grad_low, grad_half, grad_out, rows_out,
+    first, second, grad_out, rows_out, scratch,
 ):
     core = info[0]
     half = cotangent.shape[1] // 2
@@ -633,8 +654,10 @@
     mean = jnp.mean(scaled * residual, axis=-1, keepdims=True)
     grad = cotangent[...].astype(f32) + inverse * scaled - residual * (inverse * inverse * inverse * mean)
     grad_out[...] = grad
-    grad_low[...] = grad.astype(bf16)
-    grad_half[...] = grad_low[:, core_columns(core, half)]
+    scratch[...] = grad.astype(bf16)
+    mine = scratch[:, core_columns(core, half)]
+    first[...] = mine[:HALF]
+    second[...] = mine[HALF:]
     gain_grad = jnp.sum(grad_normed * residual * inverse, axis=0, keepdims=True)
     rows_out[:experts] = dot_tn(grad_logits, normed[...]).astype(bf16)
     kept = 1.0 - padding[...].astype(f32)
@@ -663,16 +686,18 @@
     rows_out[experts:] = small.astype(bf16)
 
 
-def final_rows_kernel(info, own, came, tokens, inverse_ref, extra, grad_residual, residual, grad_input, result):
+def final_rows_kernel(info, own, came, tokens, inverse_ref, extra, grad_residual, grad_input):
     core = info[0]
-    half = own.shape[1] // 2
     base = extra.shape[0] - SMALL
     rows = tokens[...].astype(f32)
     inverse = inverse_ref[...]
-    scaled = halves(core, own[:, :half], came[:, :half]) * extra[base : base + 1, :].astype(f32)
+    scaled = halves(core, own[...], came[...]) * extra[base : base + 1, :].astype(f32)
     mean = jnp.mean(scaled * rows, axis=-1, keepdims=True)
     grad_input[...] = grad_residual[...] + inverse * scaled - rows * (inverse * inverse * inverse * mean)
-    result[...] = residual[...] + halves(core, own[:, half:], came[:, half:])
+
+
+def result_kernel(info, own, came, residual, result):
+    result[...] = residual[...] + halves(info[0], own[...].astype(f32), came[...].astype(f32))
 
 
 def expert_kernel(info, rows, marks, grads, pairs_w, downs_w, back_own, back_other, back_marks, hidden_out, pairs_out):
@@ -719,13 +744,12 @@
     back_marks[0] = (jnp.where(high_lane, high, 0.0) + jnp.where(low_lane, low, 0.0)).astype(bf16)
 
 
-def expert_grad_kernel(info, rows, pairs, *refs):
-    gate_grads, up_grads = refs[:4], refs[4:]
-    shard, units = gate_grads[0].shape[1:]
+def expert_grad_kernel(info, rows, pairs, gate_grads, up_grads):
+    shard, units = up_grads.shape[2:]
     for i in range(SIDE):
-        result = dot_tn(rows[0, :, core_columns(info[4 + i], shard)], pairs[0]).astype(bf16)
-        gate_grads[i][0] = result[:, :units]
-        up_grads[i][0] = result[:, units:]
+        result = dot_tn(rows[0, :, i * shard : (i + 1) * shard], pairs[0]).astype(bf16)
+        gate_grads[i, 0] = result[:, :units]
+        up_grads[i, 0] = result[:, units:]
 
 
 def expert_out_kernel(info, grads, hidden, downs_w, out_own, out_other, *down_grads):
@@ -768,33 +792,38 @@
     core = info[0]
     shard = pieces[0].shape[1]
     size = out.shape[0]
+    base = 2 * size + extra.shape[0]
     numbers = lax.broadcasted_iota(jnp.int32, (SMALL, shard), 0)
     both = heads[...] + heads_came[...]
     rest = jnp.zeros((1, shard - 2 * size), f32)
     head_row = join([both[0:1], both[1:2], rest], 1)
-    for i in range(SIDE):
+    for i, piece in enumerate(pieces):
         place = info[4 + i]
         columns = core_columns(place % 2, shard)
         near = place // 2 == core
         block = jnp.where(near, own[:, columns], came[:, columns])
-        pieces[i][:size] = block[:size]
-        pieces[SIDE + i][...] = block[size:]
+        piece[:size] = block[:size]
+        piece[size : 2 * size] = jnp.where(near, out[:, columns], out_came[:, columns])
+        piece[2 * size : base] = extra[:, core_columns(place, shard)]
         gain_row = jnp.where(near, gain[0:1, columns], gain_came[0:1, columns])
         small = jnp.where(numbers == 0, gain_row, jnp.where(numbers == 1, head_row, 0.0))
-        pieces[i][size : 2 * size] = jnp.where(near, out[:, columns], out_came[:, columns])
-        pieces[i][2 * size : 2 * size + extra.shape[0]] = extra[:, core_columns(place, shard)]
-        pieces[i][2 * size + extra.shape[0] :] = small.astype(bf16)
-
-
-def project_final_kernel(info, parts, query, out_grad, router, gain1, gain2, head_gains, load, loss, total):
+        piece[base : base + SMALL] = small.astype(bf16)
+        piece[base + SMALL :] = block[size:]
+
+
+def project_final_kernel(
+    info, parts, query, out_grad, key, value, router, gain1, gain2, head_gains, load, loss, total, key_value
+):
     step = pl.program_id(0)
     size = out_grad.shape[0] // parts.shape[0]
-    rest = 0.0
+    base = 2 * size + total.shape[0]
+    rest = pair = 0.0
     for i in range(parts.shape[0]):
         block = parts[i].astype(f32)
         query[:, i * size : (i + 1) * size] = block[:size].T
         out_grad[i * size : (i + 1) * size] = block[size : 2 * size]
-        rest += block[2 * size :]
+        rest += block[2 * size : base]
+        pair += block[base:]
 
     @pl.when(step == 0)
     def _():
@@ -803,6 +832,16 @@
     @pl.when(step > 0)
     def _():
         total[...] += rest
+
+    @pl.when(step % 2 == 0)
+    def _():
+        key_value[...] = pair
+
+    @pl.when(step % 2 == 1)
+    def _():
+        both = key_value[...] + pair
+        key[...] = both[:size].T
+        value[...] = both[size:].T
 
     @pl.when(step == pl.num_programs(0) - 1)
     def _():
@@ -825,15 +864,6 @@
             sums = row(SMALL + 1)[:, part * size : (part + 1) * size]
             sums = pltpu.roll(jnp.broadcast_to(sums, (8, size)), (size - info[2] * count) % size, 1)
             head_gains[part : part + 1] = sums[:1, :count]
-
-
-def key_value_kernel(info, mine, other, key, value):
-    size = key.shape[1] // 2
-    for group in range(2):
-        cut = slice(group * size, (group + 1) * size)
-        block = jnp.where(info[11] == group, mine[...].astype(f32), other[...].astype(f32))
-        key[:, cut] = block[:size].T
-        value[:, cut] = block[size:].T
 
 
 def body(
@@ -919,12 +949,13 @@
         norm1_gain[None], norm2_gain[None], q_gain[None], k_gain[None],
     )[0]
     dense_pieces = ring_gather(dense, moves_y())
+    first_near, second_near = two_gathers(
+        first, second, moves_z(), moves_x(), (dense_pieces[3],), (dense_pieces[1],)
+    )
+    pairs = join([w_gate, after(w_up, first_near[2])], 2)
     cot_half = lax.dynamic_slice_in_dim(cot_rows, core * half, half, axis=1)
     cot_all = lax.all_gather(cot_half, "context", axis=0)
-    pairs_all = lax.all_gather(after(join([w_gate, w_up], 2), first), "fsdp", axis=0)
-    first_near, second_near = two_gathers(
-        first, second, moves_z(), moves_x(), (dense_pieces[3],), (dense_pieces[1],)
-    )
+    pairs_all = lax.all_gather(pairs, "fsdp", axis=0)
     first_pieces, second_pieces = two_gathers(
         stack(first_near),
         stack(second_near),
@@ -934,7 +965,7 @@
     )
     token_pieces = first_pieces + second_pieces
     extra_rows = expert_count + SMALL
-    dense_own, dense_away, out_own_rows, out_away_rows, dense_out, extra = call(
+    dense_own, dense_away, out_own_rows, out_away_rows, extra = call(
         dense_split_kernel,
         [scalars] + [whole] * 4,
         [
@@ -942,7 +973,6 @@
             ((3 * size, half), bf16),
             ((size, half), bf16),
             ((size, half), bf16),
-            ((size, width), bf16),
             ((extra_rows, width), bf16),
         ],
     )(info, *dense_pieces)
@@ -965,11 +995,11 @@
     own_part, away_part, normed1 = call(
         project_kernel,
         [scalars] + [whole] * 11,
-        [((spans, span, 3 * size), f32), ((spans, span, 3 * size), f32), ((spans, span, half), bf16)],
+        [((spans, span, 3 * size), f32), ((spans, span, 3 * size), bf16), ((spans, span, half), bf16)],
         flops=4 * count * half * 3 * size,
         moved=2 * 10**7,
     )(info, gain1, after(dense_own, cot_all), dense_came, *token_pieces)
-    down_all = lax.all_gather(after(w_down, token_pieces[0]), "fsdp", axis=0)
+    down_all = lax.all_gather(after(w_down, own_part), "fsdp", axis=0)
     mixed, raw, queries, keys, values, log_totals = call(
         attend_kernel,
         [whole] * 8,
@@ -1029,7 +1059,7 @@
     expert_flops = 2 * local_experts * slot_count * width * hidden_units
     slot_half = (local_experts, slot_count, half)
     slot_hidden = (local_experts, slot_count, hidden_units)
-    back_own, back_other, back_marks, hidden, pairs = per_expert(
+    back_own, back_other, back_marks, hidden, pair_grads = per_expert(
         expert_kernel,
         info,
         [slot_rows, slot_marks, slot_grads, pairs_all, down_all],
@@ -1038,23 +1068,21 @@
         5 * 10**7,
     )
     back_came = other_core(back_other)
-    expert_grads = per_expert(
+    gate_grads, up_grads = per_expert(
         expert_grad_kernel,
         info,
-        [slot_rows, pairs],
-        [(local_experts, shard, hidden_units)] * 8,
+        [slot_rows, pair_grads],
+        [(SIDE, local_experts, shard, hidden_units)] * 2,
         2 * expert_flops,
         3 * 10**7,
     )
-    gate_grads, up_grads = expert_grads[:4], expert_grads[4:]
-    out_all = lax.all_gather(after(dense_out, slot_rows), "context", axis=0)
     grad_pieces = call(
         put_rows_kernel,
         [scalars] + [whole] * 4,
         [((SIDE, HALF, half + EXTRA), bf16)] * 8,
         flops=2 * 10**9,
         moved=2 * 10**7,
-    )(info, chosen, back_own, after(back_came, gate_grads[0]), back_marks)
+    )(info, chosen, back_own, after(back_came, gate_grads), back_marks)
     out_own, out_other, *down_grads = per_expert(
         expert_out_kernel,
         info,
@@ -1063,117 +1091,112 @@
         2 * expert_flops,
         3 * 10**7,
     )
-    mixture_pieces = call(
-        put_sums_kernel,
-        [scalars] + [whole] * 3,
-        [(piece_shape, bf16)] * 8,
+    mixture_spans = call(
+        put_spans_kernel,
+        [whole] * 3,
+        [((spans, span, half), bf16)],
         flops=2 * 10**9,
         moved=2 * 10**7,
-    )(info, chosen, out_own, other_core(out_other))
-    gate_steps, up_steps, down_steps = scatter_chain([gate_grads, up_grads, down_grads], moves_y())
-    grad_message = plane_scatter(grad_pieces, ((out_own, *gate_steps[:2]), (), (), (gate_steps[2], up_steps[0], mixture_pieces[0])))
-
-    grad_low, grad_half, grad_residual2, router_rows = call(
+    )(chosen, out_own, other_core(out_other))[0]
+    gate_mine = lax.psum_scatter(gate_grads, "fsdp", scatter_dimension=0, tiled=False)
+    grad_message = plane_scatter(grad_pieces, ((out_own,), (), ()))
+    up_mine = lax.psum_scatter(up_grads, "fsdp", scatter_dimension=0, tiled=False)
+
+    first, second, grad_residual2, router_rows = call(
         router_back_kernel,
         [scalars] + [whole] * 12,
         [
-            ((span, width), bf16),
-            ((span, half), bf16),
+            ((HALF, half), bf16),
+            ((HALF, half), bf16),
             ((span, width), f32),
             ((extra_rows, width), bf16),
         ],
+        scratch_shapes=[pltpu.VMEM((span, width), bf16)],
     )(
         info, grad_message, other_core(grad_message), residual2, inverse2, normed2, probs, gates, picked_total,
         ids, pad_column, cot_rows, extra,
     )
 
-    four_heads = pl.BlockSpec((SIDE, span, size), lambda i: (i, 0, 0))
-    four_weights = pl.BlockSpec((SIDE, size, width), lambda i: (i, 0, 0))
-    out_grads_all = lax.all_gather(grad_half, "context", axis=0)
-    heads_back = call(
+    out_pieces = plane_gather(first, second, ((), (), (), (mixture_spans,)))
+    heads_own, heads_away = call(
         heads_back_kernel,
-        [whole, four_weights],
-        [(head_shape, bf16)],
-        flops=2 * span * width * width,
+        [scalars] + [whole] * 10,
+        [((spans, span, size), f32)] * 2,
+        flops=4 * count * size * half,
         moved=10**7,
-        grid=(SIDE,),
-        out_specs=[four_heads],
-    )(grad_low, out_all)[0]
-    heads_grad = lax.all_to_all(heads_back, "context", split_axis=0, concat_axis=0, tiled=True)
+    )(info, out_own_rows, out_came_rows, *out_pieces)
+    mixture = lax.psum_scatter(mixture_spans, "context", scatter_dimension=0, tiled=False)
+    result = call(result_kernel, [scalars] + [whole] * 3, [((span, width), f32)])(
+        info, mixture, other_core(mixture), residual2
+    )[0]
+    heads_came, gate_mine, up_mine = together(other_core(heads_away), gate_mine, up_mine)
     grads, gain_grads = call(
         attend_back_kernel,
-        [whole] * 12,
+        [whole] * 13,
         [((spans, span, 3 * size), bf16), ((8, size), f32)],
         flops=8 * 10**9,
         moved=3 * 10**7,
-        scratch_shapes=[pltpu.VMEM((count, size), f32)] * 3,
+        scratch_shapes=[pltpu.VMEM((count, size), bf16)] + [pltpu.VMEM((count, size), f32)] * 3,
     )(
-        heads_grad.reshape(count, size), raw, queries, keys, values, log_totals,
+        heads_own, heads_came, raw, queries, keys, values, log_totals,
         cosine, sine, head_gains, doc_rows, doc_columns, pads,
     )
     grads_came = other_core(grads)
-    project_own, project_away = call(
+    down_passing = moves_y()[0](down_grads[2])
+    down_ahead = moves_y()[1](after(down_grads[3], down_passing))
+    project_own, project_away, gain1_part = call(
         project_grad_kernel,
-        [whole] * 3,
-        [((3 * size, half), bf16)] * 2,
+        [whole] * 6,
+        [((3 * size, half), bf16)] * 2 + [((8, half), f32)],
         flops=4 * count * half * 3 * size,
         moved=2 * 10**7,
-    )(grads, grads_came, normed1)
+    )(grads, after(grads_came, down_passing), normed1, dense_own, dense_came, gain1)
     out_grad_own, out_grad_away = call(
-        out_grad_kernel, [whole] * 3, [((size, half), bf16)] * 2, flops=4 * count * size * half, moved=10**7
-    )(after(mixed, project_own), mixed_came, out_grads_all)
+        out_grad_kernel,
+        [scalars] + [whole] * 10,
+        [((size, half), bf16)] * 2,
+        flops=4 * count * size * half,
+        moved=10**7,
+    )(info, after(mixed, heads_own), mixed_came, *out_pieces)
     project_came = other_core(project_away)
-    *input_pieces, gain1_part = call(
+    message_shape = (4 * size + SMALL + extra_rows, shard)
+    project_pieces = call(
+        project_chunk_kernel, [scalars] + [whole] * 9, [(message_shape, bf16)] * 4
+    )(
+        info, project_own, project_came, gain1_part, other_core(gain1_part), gain_grads, other_core(gain_grads),
+        out_grad_own, after(other_core(out_grad_away), down_ahead), router_rows,
+    )
+    passing = moves_y()[0](project_pieces[2])
+    from_ahead = moves_y()[1](project_pieces[3])
+    input_pieces = call(
         input_back_kernel,
-        [scalars] + [whole] * 20,
-        [((SIDE, HALF, width), bf16)] * 8 + [((8, half), f32)],
+        [scalars] + [whole] * 4,
+        [(piece_shape, bf16)] * 8,
         flops=4 * count * half * 3 * size,
         moved=3 * 10**7,
-    )(info, grads, after(grads_came, project_own, up_steps[1], up_steps[2]), dense_own, dense_came, *token_pieces, *mixture_pieces)
-
-    query_shape = (2 * size + SMALL + extra_rows, shard)
-    key_value_shape = (2 * size, shard)
-    project_pieces = call(
-        project_chunk_kernel, [scalars] + [whole] * 9, [(query_shape, bf16)] * 4 + [(key_value_shape, bf16)] * 4
-    )(
-        info, project_own, project_came, gain1_part, other_core(gain1_part), gain_grads, other_core(gain_grads),
-        out_grad_own, other_core(out_grad_away), router_rows,
-    )
-    query_terms = ring_scatter(project_pieces[:4], moves_y())
-    key_passing = moves_y()[0](project_pieces[6])
-    key_ahead = moves_y()[1](project_pieces[7])
-    first, second, (key_passing, key_ahead, *query_terms), (key_ahead,) = two_scatters(
-        input_pieces[:4],
-        input_pieces[4:],
-        moves_x(),
-        moves_z(),
-        (key_passing, key_ahead, *query_terms, *down_steps[:2]),
-        (key_ahead,),
-    )
-    query_mine = low_sum(query_terms[:3])
-    query_all = lax.all_gather(query_mine, "context", axis=0)
-    key_behind = moves_y()[0](add_low(project_pieces[5], key_passing))
-    first, second, (key_behind,), key_terms = two_scatters(
-        unstack(first), unstack(second), moves_z(), moves_x(), (key_behind,), (down_steps[2],)
-    )
-    key_value = low_sum((project_pieces[4], key_behind, key_ahead))
-    key_value = low_sum([key_value] + [along_z(key_value, step) for step in range(1, SIDE)])
-    final_rows = call(total_kernel, [whole] * 6, [((span, width), f32)])(*first, *second)[0]
-    key_value = low_sum([key_value, across(key_value, 1)])
-    final_key, final_value = call(
-        key_value_kernel, [scalars] + [whole] * 2, [((shard, 2 * size), f32)] * 2
-    )(info, key_value, across(key_value, 2))
-    grad_input, result = call(final_rows_kernel, [scalars] + [whole] * 7, [((span, width), f32)] * 2)(
-        info, final_rows, other_core(final_rows), token_rows, inverse1, extra, grad_residual2, residual2
-    )
+    )(info, grads, after(grads_came, project_pieces[0]), dense_own, dense_came)
+    from_behind = moves_y()[0](add_low(project_pieces[1], after(passing, input_pieces[0])))
+    message = after(low_sum((project_pieces[0], from_behind, from_ahead)), result)
+    message_all = lax.all_gather(message, "context", axis=0)
+    down_behind = moves_y()[0](add_low(down_grads[1], down_passing))
+    final_rows = plane_scatter(input_pieces, ((), (down_behind,), ()))
+    grad_input = call(final_rows_kernel, [scalars] + [whole] * 6, [((span, width), f32)])(
+        info, final_rows, other_core(final_rows), token_rows, inverse1, extra, grad_residual2
+    )[0]
+    final_gate = gate_mine.astype(f32)
+    final_up = up_mine.astype(f32)
+    final_down = down_grads[0].astype(f32) + down_ahead.astype(f32) + down_behind.astype(f32)
     (
-        final_query, final_out, final_router, final_gain1, final_gain2, final_head_gains, expert_load, balance_loss
+        final_query, final_out, final_key, final_value, final_router, final_gain1, final_gain2, final_head_gains,
+        expert_load, balance_loss,
     ) = call(
         project_final_kernel,
-        [scalars, pl.BlockSpec((SIDE,) + query_shape, lambda i: (i, 0, 0))],
+        [scalars, pl.BlockSpec((SIDE,) + message_shape, lambda i: (i, 0, 0))],
         [
             ((shard, spans * size), f32),
             ((spans * size, shard), f32),
+            ((shard, 2 * size), f32),
+            ((shard, 2 * size), f32),
             ((expert_count, shard), f32),
             ((1, shard), f32),
             ((1, shard), f32),
@@ -1185,17 +1208,12 @@
         out_specs=[
             pl.BlockSpec((shard, SIDE * size), lambda i: (0, i)),
             pl.BlockSpec((SIDE * size, shard), lambda i: (i, 0)),
+            pl.BlockSpec((shard, size), lambda i: (0, i // 2)),
+            pl.BlockSpec((shard, size), lambda i: (0, i // 2)),
         ]
         + [whole] * 6,
-        scratch_shapes=[pltpu.VMEM((SMALL + extra_rows, shard), f32)],
-    )(info, after(query_all, grad_input))
-
-    def finished(parts, steps):
-        return parts[0].astype(f32) + steps[1].astype(f32) + steps[2].astype(f32)
-
-    final_gate = finished(gate_grads, gate_steps)
-    final_up = finished(up_grads, up_steps)
-    final_down = finished(down_grads, down_steps)
+        scratch_shapes=[pltpu.VMEM((SMALL + extra_rows, shard), f32), pltpu.VMEM((2 * size, shard), f32)],
+    )(info, after(message_all, grad_input, final_gate, final_up, final_down))
 
     return (
         result[None],

time: 671 us -> 659 us (0.982)
  other arithmetic: 43 us -> 23.4 us
  starting transfers between devices: 128 us -> 137 us
    ppermute x23 -> x25, starting transfers between devices: 14 us -> 35.3 us  [other_core(): return lax.ppermute(value, 'tensor', [(0, 1), (1, 0)])]
    ppermute x78 -> x71, starting transfers between devices: 101 us -> 85.4 us  [move(): return lambda value: lax.ppermute(value, (axis, 'tensor'), pairs)]
    convert_element_type x17 -> x8, other arithmetic: 17.7 us -> 4.8 us  [add_low(): return (left.astype(f32) + right.astype(f32)).astype(bf16)]
    ppermute x23 -> x25, waiting for transfers between devices: 10.6 us -> 21.3 us  [other_core(): return lax.ppermute(value, 'tensor', [(0, 1), (1, 0)])]
    ppermute x3 -> x5, waiting for transfers between devices: 15.7 us -> 5.37 us  [along_z(): return lax.ppermute(value, 'context', pairs)]
    ppermute x78 -> x71, waiting for transfers between devices: 170 us -> 161 us  [move(): return lambda value: lax.ppermute(value, (axis, 'tensor'), pairs)]
    add x3 -> x1, other arithmetic: 11 us -> 2.34 us  [body(): down_grads[0].astype(f32) + down_ahead.astype(f32) + down_behind.astype(f32)]
    ppermute x2 -> x5, starting transfers between devices: 1.79 us -> 10.3 us  [along_x(): return lax.ppermute(value, 'context', pairs)]
  transfers between devices with their start and end apart: 113 -> 113, of which waited for: 63 -> 59; matrix products, arithmetic and copies ran while one was open for 7% -> 5% of each run, Pallas kernels for 35% -> 28%
where the time goes in v2:
time: 659 us; the launch traced here: 649 us
  Pallas kernels  238 us (36%)
  waiting for transfers between devices  203 us (31%)
  starting transfers between devices  137 us (21%)
  local copies, waits for them, and re-layouts  32.2 us (5%)
  other arithmetic  23.4 us (4%)
  between operations  15.4 us (2%)
    ppermute x71, waiting for transfers between devices, move(): return lambda value: lax.ppermute(value, (axis, 'tensor'), pairs)  161 us
    ppermute x71, starting transfers between devices, move(): return lambda value: lax.ppermute(value, (axis, 'tensor'), pairs)  85.4 us
    pallas_call x3, Pallas kernels, per_expert(): call(kernel, [scalars] + [by_expert(array.shape) for array in arrays], [(...  58.8 us
    ppermute x25, starting transfers between devices, other_core(): return lax.ppermute(value, 'tensor', [(0, 1), (1, 0)])  35.3 us
    unnamed x233, local copies, waits for them, and re-layouts  22.6 us
    ppermute x25, waiting for transfers between devices, other_core(): return lax.ppermute(value, 'tensor', [(0, 1), (1, 0)])  21.3 us
    pallas_call x1, Pallas kernels, body(): call(attend_back_kernel, [whole] * 13, [((spans, span, 3 * size), bf16),...  17.2 us
    pallas_call x6, Pallas kernels, unstack(): return call(unstack_kernel, [whole] * 3, [(shape, bf16)] * 4)(*terms)  14.5 us
  transfers between devices with their start and end apart: 113, of which 59 were waited for; matrix products, arithmetic and copies ran while one was open for 5% of the time, Pallas kernels for 28%

profile of v2, /device:TPU:1, one launch (start us, length us, event | category | flops | bytes accessed | tf_op | source)
XLA Modules:
  0.0 649.1 jit_solution(2307311008115804942)
XLA Ops:
  71.3 7.2 %collective-permute-done.9.refs_1_ = bf16[4,64,1152]{2,1,0:T(8,128)(2,1)S(1)} collective-permute-done((bf16[4,64,1152]{2,1,0:T(8,128)(2,1)}, bf16[4,64,1152]{2,1,0:T(8,128)(2,1)S(1)}, u32[]{:S(2)}, u32[]{:S(2)}) %collective-permute-start.9) | collective-permute-done | bytes 589856 | tf_op jit(solution)/shard_map/ppermute | solution.py:64
  91.1 12.1 %shard_map.294 = (f32[16,128,384]{2,1,0:T(8,128)}, bf16[16,128,384]{2,1,0:T(8,128)(2,1)}, bf16[16,128,1024]{2,1,0:T(8,128)(2,1)}) custom-call(s32[12]{0:T(128)} %stack.51.info, f32[1,1024]{1,0:T(1,128)} %dynamic-slice_convert_fusion.gain, bf16[384,1024]{1,0:T(8,128)(2,1)} %get-tuple-element.241.own, bf16[384,1024]{1,0:T(8,128)(2,1)} %collective-permute-done.15.came, ...), custom_call_target="tpu_custom_call" | custom-call | flops 3221225472 | bytes 20000000 | tf_op jit(solution)/shard_map/pallas_call | solution.py:995
  112.4 12.9 %shard_map.295 = (bf16[16,128,128]{2,1,0:T(8,128)(2,1)}, f32[2048,256]{1,0:T(8,128)}, bf16[2048,128]{1,0:T(8,128)(2,1)}, bf16[2048,128]{1,0:T(8,128)(2,1)}, bf16...) custom-call(f32[16,128,384]{2,1,0:T(8,128)} %get-tuple-element.243.own, bf16[16,128,384]{2,1,0:T(8,128)(2,1)} %copy-done.97, ...), custom_call_target="tpu_custom_call" | custom-call | flops 4000000000 | bytes 30000000 | tf_op jit(solution)/shard_map/pallas_call | solution.py:1003
  128.6 5.2 shard_map.296
  137.0 8.9 %collective-permute-done.19 = bf16[4,64,1024]{2,1,0:T(8,128)(2,1)S(1)} collective-permute-done((bf16[4,64,1024]{2,1,0:T(8,128)(2,1)}, bf16[4,64,1024]{2,1,0:T(8,128)(2,1)S(1)}, u32[]{:S(2)}, u32[]{:S(2)}) %collective-permute-start.19) | collective-permute-done | bytes 524320 | tf_op jit(solution)/shard_map/ppermute | solution.py:64
  156.7 5.1 collective-permute-done.24.b
  219.0 4.7 collective-permute-done.42.refs_5_
  225.9 5.0 collective-permute-done.40.refs_1_
  235.0 9.3 %shard_map.301.grads = bf16[4,512,2048]{2,1,0:T(8,128)(2,1)} custom-call(s32[12]{0:T(128)} %stack.51.info, bf16[16,128,128]{2,1,0:T(8,128)(2,1)} %get-tuple-element.238.chosen, bf16[16,128,1024]{2,1,0:T(8,128)(2,1)} %all-gather.8.cloned.1.call-done.own, bf16[16,128,1024]{2,1,0:T(8,128)(2,1)} %collective-permute-done.32.other), custom_call_target="tpu_custom_call" | custom-call | flops 4000000000 | bytes 20000000 | tf_op jit(solution)/shard_map/pallas_call | solution.py:1040
  250.8 9.7 %shard_map.304 = (bf16[4,512,2048]{2,1,0:T(8,128)(2,1)}, bf16[4,512,128]{2,1,0:T(8,128)(2,1)}) custom-call(s32[12]{0:T(128)} %stack.51.info, bf16[16,128,128]{2,1,0:T(8,128)(2,1)} %get-tuple-element.238.chosen, bf16[4,64,1152]{2,1,0:T(8,128)(2,1)} %shard_map.302.refs_0_, bf16[4,64,1152]{2,1,0:T(8,128)(2,1)} %copy-done.101, bf16[4,64,1152]{2,1,0:T(8,128)(2,1)} %copy-done.103, ...), custom_call_target="tpu_custom_call" | custom-call | flops 4000000000 | bytes 20000000 | tf_op jit(solution)/shard_map/pallas_call | solution.py:1052
  260.6 6.5 %all-gather.12.cloned.1.call-done = bf16[16,384,512]{2,1,0:T(8,128)(2,1)} async-done(((bf16[4,384,512]{2,1,0:T(8,128)(2,1)}), bf16[16,384,512]{2,1,0:T(8,128)(2,1)}) %all-gather.12.cloned.1.call-update) | async-done | bytes 6291472 | tf_op jit(solution)/shard_map/all_gather | solution.py:1002
  267.1 30.1 %shard_map.305 = (bf16[4,512,1024]{2,1,0:T(8,128)(2,1)}, bf16[4,512,1024]{2,1,0:T(8,128)(2,1)}, bf16[4,512,128]{2,1,0:T(8,128)(2,1)}, bf16[4,512,384]{2,1,0:T(8,128)(2,1)}, bf16[4,512,768]{2,1,0:T(8,128)(2,1)}) custom-call(s32[12]{0:T(128)} %stack.51.info, bf16[4,512,2048]{2,1,0:T(8,128)(2,1)} %get-tuple-element.293.rows, ...), custom_call_target="tpu_custom_call" | custom-call | flops 16106127360 | bytes 50000000 | tf_op jit(solution)/shard_map/pallas_call | solution.py:780
  297.2 12.2 %shard_map.306 = (bf16[4,4,512,384]{3,2,1,0:T(8,128)(2,1)}, bf16[4,4,512,384]{3,2,1,0:T(8,128)(2,1)}) custom-call(s32[12]{0:T(128)} %stack.51.info, bf16[4,512,2048]{2,1,0:T(8,128)(2,1)} %get-tuple-element.293.rows, bf16[4,512,768]{2,1,0:T(8,128)(2,1)} %get-tuple-element.299.pairs), custom_call_target="tpu_custom_call" | custom-call | flops 6442450944 | bytes 30000000 | tf_op jit(solution)/shard_map/pallas_call | solution.py:780
  311.0 7.0 %collective-permute-done.53.came = bf16[4,512,1024]{2,1,0:T(8,128)(2,1)S(1)} collective-permute-done((bf16[4,512,1024]{2,1,0:T(8,128)(2,1)}, bf16[4,512,1024]{2,1,0:T(8,128)(2,1)S(1)}, u32[]{:S(2)}, u32[]{:S(2)}) %collective-permute-start.53) | collective-permute-done | bytes 4194336 | tf_op jit(solution)/shard_map/ppermute | solution.py:82
  320.6 7.2 %shard_map.307 = (bf16[4,64,1152]{2,1,0:T(8,128)(2,1)}, bf16[4,64,1152]{2,1,0:T(8,128)(2,1)}, bf16[4,64,1152]{2,1,0:T(8,128)(2,1)}, bf16[4,64,1152]{2,1,0:T(8,12...) custom-call(s32[12]{0:T(128)} %stack.51.info, ...), custom_call_target="tpu_custom_call" | custom-call | flops 2000000000 | bytes 20000000 | tf_op jit(solution)/shard_map/pallas_call | solution.py:1079
  327.8 16.5 %shard_map.308 = (bf16[4,512,1024]{2,1,0:T(8,128)(2,1)}, bf16[4,512,1024]{2,1,0:T(8,128)(2,1)}, bf16[4,384,512]{2,1,0:T(8,128)(2,1)}, bf16[4,384,512]{2,1,0:T(8,...) custom-call(s32[12]{0:T(128)} %stack.51.info, bf16[4,512,2048]{2,1,0:T(8,128)(2,1)} %shard_map.301.grads, ...), custom_call_target="tpu_custom_call" | custom-call | flops 6442450944 | bytes 30000000 | tf_op jit(solution)/shard_map/pallas_call | solution.py:780
  349.8 9.7 %collective-permute-done.56 = bf16[4,64,1152]{2,1,0:T(8,128)(2,1)S(1)} collective-permute-done((bf16[4,64,1152]{2,1,0:T(8,128)(2,1)}, bf16[4,64,1152]{2,1,0:T(8,128)(2,1)S(1)}, u32[]{:S(2)}, u32[]{:S(2)}) %collective-permute-start.56) | collective-permute-done | bytes 589856 | tf_op jit(solution)/shard_map/ppermute | solution.py:64
  371.4 7.4 %shard_map.309 = bf16[16,128,1024]{2,1,0:T(8,128)(2,1)} custom-call(bf16[16,128,128]{2,1,0:T(8,128)(2,1)} %get-tuple-element.238.chosen, bf16[4,512,1024]{2,1,0:T(8,128)(2,1)} %get-tuple-element.305.own, bf16[4,512,1024]{2,1,0:T(8,128)(2,1)} %copy-done), custom_call_target="tpu_custom_call" | custom-call | flops 2000000000 | bytes 20000000 | tf_op jit(solution)/shard_map/pallas_call | solution.py:1094
  392.2 5.4 collective-permute-done.62.refs_1_
  404.2 4.8 shard_map.314
  432.7 6.2 collective-permute-done.78.refs_5_
  448.4 6.7 %collective-permute-done.79.refs_2_ = bf16[4,64,1024]{2,1,0:T(8,128)(2,1)S(1)} collective-permute-done((bf16[4,64,1024]{2,1,0:T(8,128)(2,1)S(1)}, bf16[4,64,1024]{2,1,0:T(8,128)(2,1)S(1)}, u32[]{:S(2)}, u32[]{:S(2)}) %collective-permute-start.79) | collective-permute-done | bytes 524320 | tf_op jit(solution)/shard_map/ppermute | solution.py:64
  458.3 6.0 shard_map.317
  468.1 17.2 %shard_map.318 = (bf16[16,128,384]{2,1,0:T(8,128)(2,1)}, f32[8,128]{1,0:T(8,128)}) custom-call(f32[16,128,128]{2,1,0:T(8,128)} %get-tuple-element.354.own, f32[16,128,128]{2,1,0:T(8,128)} %copy-done.98, f32[2048,256]{1,0:T(8,128)} %get-tuple-element.358.raw, bf16[2048,128]{1,0:T(8,128)(2,1)} %get-tuple-element.359.queries, ...), custom_call_target="tpu_custom_call" | custom-call | flops 8000000000 | bytes 30000000 | tf_op jit(solution)/shard_map/pallas_call | solution.py:1133
  490.1 7.9 %shard_map.319 = (bf16[384,1024]{1,0:T(8,128)(2,1)}, bf16[384,1024]{1,0:T(8,128)(2,1)}, f32[8,1024]{1,0:T(8,128)}) custom-call(bf16[16,128,384]{2,1,0:T(8,128)(2,1)} %get-tuple-element.363.grads, bf16[16,128,384]{2,1,0:T(8,128)(2,1)} %copy-done.96, bf16[16,128,1024]{2,1,0:T(8,128)(2,1)} %get-tuple-element.366.normed, ...), custom_call_target="tpu_custom_call" | custom-call | flops 3221225472 | bytes 20000000 | tf_op jit(solution)/shard_map/pallas_call | solution.py:1147
  512.0 8.2 %shard_map.322 = (bf16[4,64,1024]{2,1,0:T(8,128)(2,1)}, bf16[4,64,1024]{2,1,0:T(8,128)(2,1)}, bf16[4,64,1024]{2,1,0:T(8,128)(2,1)}, bf16[4,64,1024]{2,1,0:T(8,12...) custom-call(s32[12]{0:T(128)} %stack.51.info, ...), custom_call_target="tpu_custom_call" | custom-call | flops 3221225472 | bytes 30000000 | tf_op jit(solution)/shard_map/pallas_call | solution.py:1171
  529.9 5.5 collective-permute-done.90
  549.9 5.2 collective-permute-done.93.c
  556.6 8.4 %collective-permute-done.98 = bf16[4,384,512]{2,1,0:T(8,128)(2,1)S(1)} collective-permute-done((bf16[4,384,512]{2,1,0:T(8,128)(2,1)S(1)}, bf16[4,384,512]{2,1,0:T(8,128)(2,1)S(1)}, u32[]{:S(2)}, u32[]{:S(2)}) %collective-permute-start.98) | collective-permute-done | bytes 1572896 | tf_op jit(solution)/shard_map/ppermute | solution.py:64
  565.1 10.2 %collective-permute-done.97.b = bf16[4,64,1024]{2,1,0:T(8,128)(2,1)S(1)} collective-permute-done((bf16[4,64,1024]{2,1,0:T(8,128)(2,1)S(1)}, bf16[4,64,1024]{2,1,0:T(8,128)(2,1)S(1)}, u32[]{:S(2)}, u32[]{:S(2)}) %collective-permute-start.97) | collective-permute-done | bytes 524320 | tf_op jit(solution)/shard_map/ppermute | solution.py:64
  601.5 20.1 %collective-permute-start.105 = (f32[128,1024]{1,0:T(8,128)}, f32[128,1024]{1,0:T(8,128)S(1)}, u32[]{:S(2)}, u32[]{:S(2)}) collective-permute-start(f32[128,1024]{1,0:T(8,128)} %shard_map.325.own), channel_id=1, source_target_pairs={{0,1},{1,0},{2,3},{3,2},{4,5},{5,4},{6,7},{7,6},{8,9},{9,8},{10,11... | collective-permute-start | bytes 1572872 | tf_op jit(solution)/shard_map/ppermute | solution.py:82
  631.9 8.9 %shard_map.327 = (f32[512,2048]{1,0:T(8,128)}, f32[2048,512]{1,0:T(8,128)}, f32[512,256]{1,0:T(8,128)}, f32[512,256]{1,0:T(8,128)}, f32[64,512]{1,0:T(8,128)}, /...) custom-call(s32[12]{0:T(128)} %stack.51.info, ...), custom_call_target="tpu_custom_call" | custom-call | flops 1000000 | bytes 1000000 | tf_op jit(solution)/shard_map/pallas_call | solution.py:1192
  (506 shorter events, 336.6 us)
Async XLA Ops:
  7.2 83.1 %all-gather.8.cloned.1.call-start = ((), (), s32[]{:S(2)}) async-start(), calls=%async_computation.3 | async-start | bytes 4456448 | tf_op jit(solution)/shard_map/all_gather | solution.py:957
  8.9 222.2 %all-gather.10.cloned.1.call-start = ((), (), s32[]{:S(2)}) async-start(), calls=%async_computation.6 | async-start | bytes 15728640 | tf_op jit(solution)/shard_map/all_gather | solution.py:958
  20.3 17.1 %collective-permute-start.4 = (bf16[592,512]{1,0:T(8,128)(2,1)}, bf16[592,512]{1,0:T(8,128)(2,1)S(1)}, u32[]{:S(2)}, u32[]{:S(2)}) collective-permute-start(bf16[592,512]{1,0:T(8,128)(2,1)} %shard_map.289.a), channel_id=1, source_target_pairs={{0,32},{1,97},{32,64},{33,1},{64,96},{65,33},{96,0},{97,65},{2,34}... | collective-permute-start | bytes 1818632 | tf_op jit(solution)/shard_map/ppermute | solution.py:64
  23.9 19.2 %collective-permute-start.7 = (bf16[592,512]{1,0:T(8,128)(2,1)}, bf16[592,512]{1,0:T(8,128)(2,1)S(1)}, u32[]{:S(2)}, u32[]{:S(2)}) collective-permute-start(bf16[592,512]{1,0:T(8,128)(2,1)} %shard_map.289.a), channel_id=1, source_target_pairs={{0,96},{1,33},{32,0},{33,65},{64,32},{65,97},{96,64},{97,1},{2,98}... | collective-permute-start | bytes 1818632 | tf_op jit(solution)/shard_map/ppermute | solution.py:64
  47.2 219.9 %all-gather.12.cloned.1.call-start = ((), (), s32[]{:S(2)}) async-start(), calls=%async_computation.7 | async-start | bytes 7864320 | tf_op jit(solution)/shard_map/all_gather | solution.py:1002
  48.7 16.6 %collective-permute-start.12 = (bf16[592,512]{1,0:T(8,128)(2,1)S(1)}, bf16[592,512]{1,0:T(8,128)(2,1)S(1)}, u32[]{:S(2)}, u32[]{:S(2)}) collective-permute-start(bf16[592,512]{1,0:T(8,128)(2,1)S(1)} %collective-permute-done.4.d), channel_id=1, source_target_pairs={{0,32},{1,97},{32,64},{33,1},{64,96},{65,33},{96,0},{97,65},{2,34}... | collective-permute-start | bytes 1818632 | tf_op jit(solution)/shard_map/ppermute | solution.py:64
  53.5 25.0 %collective-permute-start.9 = (bf16[4,64,1152]{2,1,0:T(8,128)(2,1)}, bf16[4,64,1152]{2,1,0:T(8,128)(2,1)S(1)}, u32[]{:S(2)}, u32[]{:S(2)}) collective-permute-start(bf16[4,64,1152]{2,1,0:T(8,128)(2,1)} %shard_map.290.refs_0_), channel_id=1, source_target_pairs={{0,24},{1,9},{2,26},{3,11},{4,28},{5,13},{6,30},{7,15},{8,0},{9,17... | collective-permute-start | bytes 1769480 | tf_op jit(solution)/shard_map/ppermute | solution.py:64
  54.4 24.1 %collective-permute-start.8 = (bf16[4,64,1152]{2,1,0:T(8,128)(2,1)}, bf16[4,64,1152]{2,1,0:T(8,128)(2,1)S(1)}, u32[]{:S(2)}, u32[]{:S(2)}) collective-permute-start(bf16[4,64,1152]{2,1,0:T(8,128)(2,1)} %shard_map.290.refs_0_), channel_id=1, source_target_pairs={{0,8},{1,25},{2,10},{3,27},{4,12},{5,29},{6,14},{7,31},{8,16},{9,1... | collective-permute-start | bytes 1769480 | tf_op jit(solution)/shard_map/ppermute | solution.py:64
  58.9 19.7 %collective-permute-start.11 = (bf16[4,64,1152]{2,1,0:T(8,128)(2,1)}, bf16[4,64,1152]{2,1,0:T(8,128)(2,1)S(1)}, u32[]{:S(2)}, u32[]{:S(2)}) collective-permute-start(bf16[4,64,1152]{2,1,0:T(8,128)(2,1)} %shard_map.291.refs_4_), channel_id=1, source_target_pairs={{0,6},{1,3},{2,0},{3,5},{4,2},{5,7},{6,4},{7,1},{8,14},{9,11},{10,... | collective-permute-start | bytes 1769480 | tf_op jit(solution)/shard_map/ppermute | solution.py:64
  58.9 19.7 %collective-permute-start.10 = (bf16[4,64,1152]{2,1,0:T(8,128)(2,1)}, bf16[4,64,1152]{2,1,0:T(8,128)(2,1)S(1)}, u32[]{:S(2)}, u32[]{:S(2)}) collective-permute-start(bf16[4,64,1152]{2,1,0:T(8,128)(2,1)} %shard_map.291.refs_4_), channel_id=1, source_target_pairs={{0,2},{1,7},{2,4},{3,1},{4,6},{5,3},{6,0},{7,5},{8,10},{9,15},{10,... | collective-permute-start | bytes 1769480 | tf_op jit(solution)/shard_map/ppermute | solution.py:64
  69.3 20.9 %collective-permute-start.15 = (bf16[384,1024]{1,0:T(8,128)(2,1)}, bf16[384,1024]{1,0:T(8,128)(2,1)}, u32[]{:S(2)}, u32[]{:S(2)}) collective-permute-start(bf16[384,1024]{1,0:T(8,128)(2,1)} %get-tuple-element.242), channel_id=1, source_target_pairs={{0,1},{1,0},{2,3},{3,2},{4,5},{5,4},{6,7},{7,6},{8,9},{9,8},{10,11... | collective-permute-start | bytes 2359304 | tf_op jit(solution)/shard_map/ppermute | solution.py:82
  105.1 362.1 %reduce-scatter.8.cloned.1.call-start = ((), (), s32[]{:S(2)}) async-start(), calls=%async_computation.5 | async-start | bytes 7864320 | tf_op jit(solution)/shard_map/reduce_scatter | solution.py:1103
  137.0 14.9 %collective-permute-start.22 = (bf16[4,64,1024]{2,1,0:T(8,128)(2,1)}, bf16[4,64,1024]{2,1,0:T(8,128)(2,1)S(1)}, u32[]{:S(2)}, u32[]{:S(2)}) collective-permute-start(bf16[4,64,1024]{2,1,0:T(8,128)(2,1)} %get-tuple-element.254), channel_id=1, source_target_pairs={{0,6},{1,3},{2,0},{3,5},{4,2},{5,7},{6,4},{7,1},{8,14},{9,11},{10,... | collective-permute-start | bytes 1572872 | tf_op jit(solution)/shard_map/ppermute | solution.py:64
  192.3 42.7 %collective-permute-start.32 = (bf16[16,128,1024]{2,1,0:T(8,128)(2,1)}, bf16[16,128,1024]{2,1,0:T(8,128)(2,1)}, u32[]{:S(2)}, u32[]{:S(2)}) collective-permute-start(bf16[16,128,1024]{2,1,0:T(8,128)(2,1)} %all-gather.8.cloned.1.call-done.own), channel_id=1, source_target_pairs={{0,1},{1,0},{2,3},{3,2},{4,5},{5,4},{6,7},{7,6},{8,9},{9,8},{10,11... | collective-permute-start | bytes 12582920 | tf_op jit(solution)/shard_map/ppermute | solution.py:82
  211.3 14.6 %collective-permute-start.41 = (bf16[4,64,1152]{2,1,0:T(8,128)(2,1)}, bf16[4,64,1152]{2,1,0:T(8,128)(2,1)S(1)}, u32[]{:S(2)}, u32[]{:S(2)}) collective-permute-start(bf16[4,64,1152]{2,1,0:T(8,128)(2,1)} %shard_map.303.refs_4_), channel_id=1, source_target_pairs={{0,2},{1,7},{2,4},{3,1},{4,6},{5,3},{6,0},{7,5},{8,10},{9,15},{10,... | collective-permute-start | bytes 1769480 | tf_op jit(solution)/shard_map/ppermute | solution.py:64
  216.1 14.8 %collective-permute-start.40 = (bf16[4,64,1152]{2,1,0:T(8,128)(2,1)}, bf16[4,64,1152]{2,1,0:T(8,128)(2,1)S(1)}, u32[]{:S(2)}, u32[]{:S(2)}) collective-permute-start(bf16[4,64,1152]{2,1,0:T(8,128)(2,1)} %shard_map.302.refs_0_), channel_id=1, source_target_pairs={{0,24},{1,9},{2,26},{3,11},{4,28},{5,13},{6,30},{7,15},{8,0},{9,17... | collective-permute-start | bytes 1769480 | tf_op jit(solution)/shard_map/ppermute | solution.py:64
  216.1 15.0 %collective-permute-start.39 = (bf16[4,64,1152]{2,1,0:T(8,128)(2,1)}, bf16[4,64,1152]{2,1,0:T(8,128)(2,1)S(1)}, u32[]{:S(2)}, u32[]{:S(2)}) collective-permute-start(bf16[4,64,1152]{2,1,0:T(8,128)(2,1)} %shard_map.302.refs_0_), channel_id=1, source_target_pairs={{0,8},{1,25},{2,10},{3,27},{4,12},{5,29},{6,14},{7,31},{8,16},{9,1... | collective-permute-start | bytes 1769480 | tf_op jit(solution)/shard_map/ppermute | solution.py:64
  309.4 157.7 %reduce-scatter.6.cloned.1.call-start = ((), (), s32[]{:S(2)}) async-start(), calls=%async_computation.4 | async-start | bytes 7864320 | tf_op jit(solution)/shard_map/reduce_scatter | solution.py:1101
  310.0 215.7 %reduce-scatter.10.cloned.1.call-start = ((), (), s32[]{:S(2)}) async-start(), calls=%async_computation.9 | async-start | bytes 4456448
  344.2 25.2 %collective-permute-start.54 = (bf16[4,512,1024]{2,1,0:T(8,128)(2,1)}, bf16[4,512,1024]{2,1,0:T(8,128)(2,1)S(1)}, u32[]{:S(2)}, u32[]{:S(2)}) collective-permute-start(bf16[4,512,1024]{2,1,0:T(8,128)(2,1)} %get-tuple-element.306), channel_id=1, source_target_pairs={{0,1},{1,0},{2,3},{3,2},{4,5},{5,4},{6,7},{7,6},{8,9},{9,8},{10,11... | collective-permute-start | bytes 12582920 | tf_op jit(solution)/shard_map/ppermute | solution.py:82
  344.7 14.8 %collective-permute-start.56 = (bf16[4,64,1152]{2,1,0:T(8,128)(2,1)}, bf16[4,64,1152]{2,1,0:T(8,128)(2,1)S(1)}, u32[]{:S(2)}, u32[]{:S(2)}) collective-permute-start(bf16[4,64,1152]{2,1,0:T(8,128)(2,1)} %get-tuple-element.309), channel_id=1, source_target_pairs={{0,8},{1,25},{2,10},{3,27},{4,12},{5,29},{6,14},{7,31},{8,16},{9,1... | collective-permute-start | bytes 1769480 | tf_op jit(solution)/shard_map/ppermute | solution.py:64
  347.1 15.0 %collective-permute-start.57 = (bf16[4,64,1152]{2,1,0:T(8,128)(2,1)}, bf16[4,64,1152]{2,1,0:T(8,128)(2,1)S(1)}, u32[]{:S(2)}, u32[]{:S(2)}) collective-permute-start(bf16[4,64,1152]{2,1,0:T(8,128)(2,1)} %get-tuple-element.310), channel_id=1, source_target_pairs={{0,24},{1,9},{2,26},{3,11},{4,28},{5,13},{6,30},{7,15},{8,0},{9,17... | collective-permute-start | bytes 1769480 | tf_op jit(solution)/shard_map/ppermute | solution.py:64
  347.1 15.0 %collective-permute-start.58 = (bf16[4,64,1152]{2,1,0:T(8,128)(2,1)S(1)}, bf16[4,64,1152]{2,1,0:T(8,128)(2,1)S(1)}, u32[]{:S(2)}, u32[]{:S(2)}) collective-permute-start(bf16[4,64,1152]{2,1,0:T(8,128)(2,1)S(1)} %copy-done.111), channel_id=1, source_target_pairs={{0,2},{1,7},{2,4},{3,1},{4,6},{5,3},{6,0},{7,5},{8,10},{9,15},{10,... | collective-permute-start | bytes 1769480 | tf_op jit(solution)/shard_map/ppermute | solution.py:64
  349.8 15.4 %collective-permute-start.59 = (bf16[4,64,1152]{2,1,0:T(8,128)(2,1)S(1)}, bf16[4,64,1152]{2,1,0:T(8,128)(2,1)S(1)}, u32[]{:S(2)}, u32[]{:S(2)}) collective-permute-start(bf16[4,64,1152]{2,1,0:T(8,128)(2,1)S(1)} %copy-done.110), channel_id=1, source_target_pairs={{0,6},{1,3},{2,0},{3,5},{4,2},{5,7},{6,4},{7,1},{8,14},{9,11},{10,... | collective-permute-start | bytes 1769480 | tf_op jit(solution)/shard_map/ppermute | solution.py:64
  378.8 253.1 %all-gather.14.cloned.1.call-start = ((), (), s32[]{:S(2)}) async-start(), calls=%async_computation.8 | async-start | bytes 10584064 | tf_op jit(solution)/shard_map/all_gather | solution.py:1180
  464.3 21.2 %collective-permute-start.83 = (bf16[4,384,512]{2,1,0:T(8,128)(2,1)}, bf16[4,384,512]{2,1,0:T(8,128)(2,1)S(1)}, u32[]{:S(2)}, u32[]{:S(2)}) collective-permute-start(bf16[4,384,512]{2,1,0:T(8,128)(2,1)} %get-tuple-element.364), channel_id=1, source_target_pairs={{0,32},{1,97},{32,64},{33,1},{64,96},{65,33},{96,0},{97,65},{2,34}... | collective-permute-start | bytes 4718600 | tf_op jit(solution)/shard_map/ppermute | solution.py:64
  485.5 20.5 %collective-permute-start.88 = (bf16[4,384,512]{2,1,0:T(8,128)(2,1)S(1)}, bf16[4,384,512]{2,1,0:T(8,128)(2,1)S(1)}, u32[]{:S(2)}, u32[]{:S(2)}) collective-permute-start(bf16[4,384,512]{2,1,0:T(8,128)(2,1)S(1)} %copy-done.95), channel_id=1, source_target_pairs={{0,96},{1,33},{32,0},{33,65},{64,32},{65,97},{96,64},{97,1},{2,98}... | collective-permute-start | bytes 4718600 | tf_op jit(solution)/shard_map/ppermute | solution.py:64
  510.5 19.4 %collective-permute-start.91 = (bf16[608,512]{1,0:T(8,128)(2,1)}, bf16[608,512]{1,0:T(8,128)(2,1)S(1)}, u32[]{:S(2)}, u32[]{:S(2)}) collective-permute-start(bf16[608,512]{1,0:T(8,128)(2,1)} %get-tuple-element.384), channel_id=1, source_target_pairs={{0,96},{1,33},{32,0},{33,65},{64,32},{65,97},{96,64},{97,1},{2,98}... | collective-permute-start | bytes 1867784 | tf_op jit(solution)/shard_map/ppermute | solution.py:64
  545.4 19.7 %collective-permute-start.98 = (bf16[4,384,512]{2,1,0:T(8,128)(2,1)S(1)}, bf16[4,384,512]{2,1,0:T(8,128)(2,1)S(1)}, u32[]{:S(2)}, u32[]{:S(2)}) collective-permute-start(bf16[4,384,512]{2,1,0:T(8,128)(2,1)S(1)} %add_convert_fusion), channel_id=1, source_target_pairs={{0,32},{1,97},{32,64},{33,1},{64,96},{65,33},{96,0},{97,65},{2,34}... | collective-permute-start | bytes 4718600 | tf_op jit(solution)/shard_map/ppermute | solution.py:64
  555.3 20.0 %collective-permute-start.97 = (bf16[4,64,1024]{2,1,0:T(8,128)(2,1)S(1)}, bf16[4,64,1024]{2,1,0:T(8,128)(2,1)S(1)}, u32[]{:S(2)}, u32[]{:S(2)}) collective-permute-start(bf16[4,64,1024]{2,1,0:T(8,128)(2,1)S(1)} %add_convert_fusion.5), channel_id=1, source_target_pairs={{0,2},{1,7},{2,4},{3,1},{4,6},{5,3},{6,0},{7,5},{8,10},{9,15},{10,... | collective-permute-start | bytes 1572872 | tf_op jit(solution)/shard_map/ppermute | solution.py:64
  555.6 19.7 %collective-permute-start.96 = (bf16[4,64,1024]{2,1,0:T(8,128)(2,1)S(1)}, bf16[4,64,1024]{2,1,0:T(8,128)(2,1)S(1)}, u32[]{:S(2)}, u32[]{:S(2)}) collective-permute-start(bf16[4,64,1024]{2,1,0:T(8,128)(2,1)S(1)} %add_convert_fusion.6), channel_id=1, source_target_pairs={{0,8},{1,25},{2,10},{3,27},{4,12},{5,29},{6,14},{7,31},{8,16},{9,1... | collective-permute-start | bytes 1572872 | tf_op jit(solution)/shard_map/ppermute | solution.py:64
  601.5 26.3 %collective-permute-start.105 = (f32[128,1024]{1,0:T(8,128)}, f32[128,1024]{1,0:T(8,128)S(1)}, u32[]{:S(2)}, u32[]{:S(2)}) collective-permute-start(f32[128,1024]{1,0:T(8,128)} %shard_map.325.own), channel_id=1, source_target_pairs={{0,1},{1,0},{2,3},{3,2},{4,5},{5,4},{6,7},{7,6},{8,9},{9,8},{10,11... | collective-permute-start | bytes 1572872 | tf_op jit(solution)/shard_map/ppermute | solution.py:82
  (197 other events, 1692.3 us)
Sparse Core Ops, SparseCore 0:
  10.7 63.0 all-gather.7
  76.1 122.5 all-gather.9
  200.4 66.6 all-gather.11
  309.6 64.6 reduce-scatter.7
  376.5 63.6 reduce-scatter.5
  443.4 75.8 reduce-scatter.9
  540.9 90.6 all-gather.13

commit v3 on v2

--- a/solution.py
+++ b/solution.py
@@ -429,13 +429,30 @@
 
 
 def block_mask(doc_rows, doc_columns, real, query_start, key_start, query_count, key_count):
-    rows = lax.broadcasted_iota(jnp.int32, (query_count, key_count), 0)
-    columns = lax.broadcasted_iota(jnp.int32, (query_count, key_count), 1)
-    distance = rows - columns + (query_start - key_start)
     positions = lax.broadcasted_iota(jnp.int32, (1, key_count), 1) + key_start
     doc_columns = jnp.where(positions < real, doc_columns, -1)
-    inside = (distance >= 0) & (distance < WINDOW) & (doc_rows == doc_columns)
-    return inside | (distance == 0)
+    offsets = lax.broadcasted_iota(jnp.int32, (query_count, query_count), 0) - lax.broadcasted_iota(
+        jnp.int32, (query_count, query_count), 1
+    )
+    same = doc_rows == doc_columns[:, key_count - query_count :]
+    parts = [((offsets >= 0) & same) | (offsets == 0)]
+    begin = 0
+    if query_start - key_start == WINDOW:
+        begin = query_count
+        parts.insert(0, (offsets < 0) & (doc_rows == doc_columns[:, :begin]))
+    if begin < key_count - query_count:
+        parts.insert(-1, doc_rows == doc_columns[:, begin : key_count - query_count])
+    return parts
+
+
+def keep(parts, values, other):
+    result = []
+    begin = 0
+    for part in parts:
+        end = begin + part.shape[1]
+        result.append(jnp.where(part, values[:, begin:end], other))
+        begin = end
+    return result[0] if len(result) == 1 else join(result, 1)
 
 
 def real_count(pads, count):
@@ -474,7 +491,7 @@
         allowed = block_mask(
             doc_rows[start:high, :], doc_columns[:, low:high], real, start, low, QUERY_BLOCK, high - low
         )
-        scores = jnp.where(allowed, scores, negative)
+        scores = keep(allowed, scores, negative)
         peak = jnp.max(scores, axis=-1, keepdims=True)
         exponent = jnp.exp(scores - peak)
         total = jnp.sum(exponent, axis=-1, keepdims=True)
@@ -506,7 +523,7 @@
         allowed = block_mask(
             doc_rows[start:high, :], doc_columns[:, low:high], real, start, low, QUERY_BLOCK, high - low
         )
-        soft = jnp.where(allowed, jnp.exp(scores - log_totals[start:high, :]), 0.0)
+        soft = keep(allowed, jnp.exp(scores - log_totals[start:high, :]), 0.0)
         grad_soft = dot_nt(grad_rows, values[low:high, :])
         row_dot = jnp.sum(soft * grad_soft, axis=-1, keepdims=True)
         grad_scores = (soft * (grad_soft - row_dot)).astype(bf16)
@@ -1125,7 +1142,7 @@
         flops=4 * count * size * half,
         moved=10**7,
     )(info, out_own_rows, out_came_rows, *out_pieces)
-    mixture = lax.psum_scatter(mixture_spans, "context", scatter_dimension=0, tiled=False)
+    mixture = lax.psum_scatter(after(mixture_spans, heads_own), "context", scatter_dimension=0, tiled=False)
     result = call(result_kernel, [scalars] + [whole] * 3, [((span, width), f32)])(
         info, mixture, other_core(mixture), residual2
     )[0]
@@ -1176,7 +1193,7 @@
         moved=3 * 10**7,
     )(info, grads, after(grads_came, project_pieces[0]), dense_own, dense_came)
     from_behind = moves_y()[0](add_low(project_pieces[1], after(passing, input_pieces[0])))
-    message = after(low_sum((project_pieces[0], from_behind, from_ahead)), result)
+    message = low_sum((project_pieces[0], from_behind, from_ahead))
     message_all = lax.all_gather(message, "context", axis=0)
     down_behind = moves_y()[0](add_low(down_grads[1], down_passing))
     final_rows = plane_scatter(input_pieces, ((), (down_behind,), ()))
@@ -1213,7 +1230,7 @@
         ]
         + [whole] * 6,
         scratch_shapes=[pltpu.VMEM((SMALL + extra_rows, shard), f32), pltpu.VMEM((2 * size, shard), f32)],
-    )(info, after(message_all, grad_input, final_gate, final_up, final_down))
+    )(info, after(message_all, grad_input, final_gate, final_up, final_down, result))
 
     return (
         result[None],

time: 659 us -> 645 us (0.979)
  waiting for transfers between devices: 203 us -> 191 us
    ppermute x71, waiting for transfers between devices: 161 us -> 143 us  [move(): return lambda value: lax.ppermute(value, (axis, 'tensor'), pairs)]
    ppermute x25, starting transfers between devices: 35.3 us -> 22.1 us  [other_core(): return lax.ppermute(value, 'tensor', [(0, 1), (1, 0)])]
    all_gather x1, waiting for transfers between devices: 0.01 us -> 12 us  [body(): message_all = lax.all_gather(message, 'context', axis=0)]
    unnamed x233 -> x227, local copies, waits for them, and re-layouts: 22.6 us -> 22 us
  transfers between devices with their start and end apart: 113 -> 113, of which waited for: 59 -> 57; matrix products, arithmetic and copies ran while one was open for 5% -> 5% of each run, Pallas kernels for 28% -> 29%
where the time goes in v3:
time: 645 us; the launch traced here: 634 us
  Pallas kernels  237 us (37%)
  waiting for transfers between devices  191 us (30%)
  starting transfers between devices  136 us (21%)
  local copies, waits for them, and re-layouts  31.6 us (5%)
  other arithmetic  23 us (4%)
  between operations  15.3 us (2%)
    ppermute x71, waiting for transfers between devices, move(): return lambda value: lax.ppermute(value, (axis, 'tensor'), pairs)  143 us
    ppermute x71, starting transfers between devices, move(): return lambda value: lax.ppermute(value, (axis, 'tensor'), pairs)  89.1 us
    pallas_call x3, Pallas kernels, per_expert(): call(kernel, [scalars] + [by_expert(array.shape) for array in arrays], [(...  58.7 us
    ppermute x25, starting transfers between devices, other_core(): return lax.ppermute(value, 'tensor', [(0, 1), (1, 0)])  22.1 us
    unnamed x227, local copies, waits for them, and re-layouts  22 us
    ppermute x25, waiting for transfers between devices, other_core(): return lax.ppermute(value, 'tensor', [(0, 1), (1, 0)])  19.5 us
    pallas_call x1, Pallas kernels, body(): call(attend_back_kernel, [whole] * 13, [((spans, span, 3 * size), bf16),...  17.1 us
    ppermute x5, starting transfers between devices, along_x(): return lax.ppermute(value, 'context', pairs)  16.6 us
  transfers between devices with their start and end apart: 113, of which 57 were waited for; matrix products, arithmetic and copies ran while one was open for 5% of the time, Pallas kernels for 29%

profile of v3, /device:TPU:1, one launch (start us, length us, event | category | flops | bytes accessed | tf_op | source)
XLA Modules:
  0.0 633.9 jit_solution(12390307737321153321)
XLA Ops:
  71.3 7.2 %collective-permute-done.9.refs_1_ = bf16[4,64,1152]{2,1,0:T(8,128)(2,1)S(1)} collective-permute-done((bf16[4,64,1152]{2,1,0:T(8,128)(2,1)}, bf16[4,64,1152]{2,1,0:T(8,128)(2,1)S(1)}, u32[]{:S(2)}, u32[]{:S(2)}) %collective-permute-start.9) | collective-permute-done | bytes 589856 | tf_op jit(solution)/shard_map/ppermute | solution.py:64
  91.1 12.1 %shard_map.294 = (f32[16,128,384]{2,1,0:T(8,128)}, bf16[16,128,384]{2,1,0:T(8,128)(2,1)}, bf16[16,128,1024]{2,1,0:T(8,128)(2,1)}) custom-call(s32[12]{0:T(128)} %stack.51.info, f32[1,1024]{1,0:T(1,128)} %dynamic-slice_convert_fusion.gain, bf16[384,1024]{1,0:T(8,128)(2,1)} %get-tuple-element.241.own, bf16[384,1024]{1,0:T(8,128)(2,1)} %collective-permute-done.15.came, ...), custom_call_target="tpu_custom_call" | custom-call | flops 3221225472 | bytes 20000000 | tf_op jit(solution)/shard_map/pallas_call | solution.py:1012
  112.4 12.8 %shard_map.295 = (bf16[16,128,128]{2,1,0:T(8,128)(2,1)}, f32[2048,256]{1,0:T(8,128)}, bf16[2048,128]{1,0:T(8,128)(2,1)}, bf16[2048,128]{1,0:T(8,128)(2,1)}, bf16...) custom-call(f32[16,128,384]{2,1,0:T(8,128)} %get-tuple-element.243.own, bf16[16,128,384]{2,1,0:T(8,128)(2,1)} %copy-done.97, ...), custom_call_target="tpu_custom_call" | custom-call | flops 4000000000 | bytes 30000000 | tf_op jit(solution)/shard_map/pallas_call | solution.py:1020
  128.4 5.2 shard_map.296
  136.8 8.9 %collective-permute-done.19 = bf16[4,64,1024]{2,1,0:T(8,128)(2,1)S(1)} collective-permute-done((bf16[4,64,1024]{2,1,0:T(8,128)(2,1)}, bf16[4,64,1024]{2,1,0:T(8,128)(2,1)S(1)}, u32[]{:S(2)}, u32[]{:S(2)}) %collective-permute-start.19) | collective-permute-done | bytes 524320 | tf_op jit(solution)/shard_map/ppermute | solution.py:64
  156.5 5.1 collective-permute-done.24.b
  225.8 4.8 collective-permute-done.40.refs_1_
  235.1 9.3 %shard_map.301.grads = bf16[4,512,2048]{2,1,0:T(8,128)(2,1)} custom-call(s32[12]{0:T(128)} %stack.51.info, bf16[16,128,128]{2,1,0:T(8,128)(2,1)} %get-tuple-element.238.chosen, bf16[16,128,1024]{2,1,0:T(8,128)(2,1)} %all-gather.8.cloned.1.call-done.own, bf16[16,128,1024]{2,1,0:T(8,128)(2,1)} %collective-permute-done.32.other), custom_call_target="tpu_custom_call" | custom-call | flops 4000000000 | bytes 20000000 | tf_op jit(solution)/shard_map/pallas_call | solution.py:1057
  250.9 9.8 %shard_map.304 = (bf16[4,512,2048]{2,1,0:T(8,128)(2,1)}, bf16[4,512,128]{2,1,0:T(8,128)(2,1)}) custom-call(s32[12]{0:T(128)} %stack.51.info, bf16[16,128,128]{2,1,0:T(8,128)(2,1)} %get-tuple-element.238.chosen, bf16[4,64,1152]{2,1,0:T(8,128)(2,1)} %shard_map.302.refs_0_, bf16[4,64,1152]{2,1,0:T(8,128)(2,1)} %copy-done.100, bf16[4,64,1152]{2,1,0:T(8,128)(2,1)} %copy-done.102, ...), custom_call_target="tpu_custom_call" | custom-call | flops 4000000000 | bytes 20000000 | tf_op jit(solution)/shard_map/pallas_call | solution.py:1069
  260.6 6.5 %all-gather.12.cloned.1.call-done = bf16[16,384,512]{2,1,0:T(8,128)(2,1)} async-done(((bf16[4,384,512]{2,1,0:T(8,128)(2,1)}), bf16[16,384,512]{2,1,0:T(8,128)(2,1)}) %all-gather.12.cloned.1.call-update) | async-done | bytes 6291472 | tf_op jit(solution)/shard_map/all_gather | solution.py:1019
  267.1 30.1 %shard_map.305 = (bf16[4,512,1024]{2,1,0:T(8,128)(2,1)}, bf16[4,512,1024]{2,1,0:T(8,128)(2,1)}, bf16[4,512,128]{2,1,0:T(8,128)(2,1)}, bf16[4,512,384]{2,1,0:T(8,128)(2,1)}, bf16[4,512,768]{2,1,0:T(8,128)(2,1)}) custom-call(s32[12]{0:T(128)} %stack.51.info, bf16[4,512,2048]{2,1,0:T(8,128)(2,1)} %get-tuple-element.293.rows, ...), custom_call_target="tpu_custom_call" | custom-call | flops 16106127360 | bytes 50000000 | tf_op jit(solution)/shard_map/pallas_call | solution.py:797
  297.2 12.3 %shard_map.306 = (bf16[4,4,512,384]{3,2,1,0:T(8,128)(2,1)}, bf16[4,4,512,384]{3,2,1,0:T(8,128)(2,1)}) custom-call(s32[12]{0:T(128)} %stack.51.info, bf16[4,512,2048]{2,1,0:T(8,128)(2,1)} %get-tuple-element.293.rows, bf16[4,512,768]{2,1,0:T(8,128)(2,1)} %get-tuple-element.299.pairs), custom_call_target="tpu_custom_call" | custom-call | flops 6442450944 | bytes 30000000 | tf_op jit(solution)/shard_map/pallas_call | solution.py:797
  310.9 7.0 %collective-permute-done.53.came = bf16[4,512,1024]{2,1,0:T(8,128)(2,1)S(1)} collective-permute-done((bf16[4,512,1024]{2,1,0:T(8,128)(2,1)}, bf16[4,512,1024]{2,1,0:T(8,128)(2,1)S(1)}, u32[]{:S(2)}, u32[]{:S(2)}) %collective-permute-start.53) | collective-permute-done | bytes 4194336 | tf_op jit(solution)/shard_map/ppermute | solution.py:82
  320.4 7.2 %shard_map.307 = (bf16[4,64,1152]{2,1,0:T(8,128)(2,1)}, bf16[4,64,1152]{2,1,0:T(8,128)(2,1)}, bf16[4,64,1152]{2,1,0:T(8,128)(2,1)}, bf16[4,64,1152]{2,1,0:T(8,12...) custom-call(s32[12]{0:T(128)} %stack.51.info, ...), custom_call_target="tpu_custom_call" | custom-call | flops 2000000000 | bytes 20000000 | tf_op jit(solution)/shard_map/pallas_call | solution.py:1096
  332.9 16.3 %shard_map.308 = (bf16[4,512,1024]{2,1,0:T(8,128)(2,1)}, bf16[4,512,1024]{2,1,0:T(8,128)(2,1)}, bf16[4,384,512]{2,1,0:T(8,128)(2,1)}, bf16[4,384,512]{2,1,0:T(8,...) custom-call(s32[12]{0:T(128)} %stack.51.info, bf16[4,512,2048]{2,1,0:T(8,128)(2,1)} %shard_map.301.grads, ...), custom_call_target="tpu_custom_call" | custom-call | flops 6442450944 | bytes 30000000 | tf_op jit(solution)/shard_map/pallas_call | solution.py:797
  355.2 5.3 collective-permute-done.60.b
  388.1 4.8 shard_map.313
  397.6 4.9 collective-permute-start.72
  419.5 5.8 collective-permute-done.77.refs_5_
  436.7 7.3 %shard_map.309 = bf16[16,128,1024]{2,1,0:T(8,128)(2,1)} custom-call(bf16[16,128,128]{2,1,0:T(8,128)(2,1)} %get-tuple-element.238.chosen, bf16[4,512,1024]{2,1,0:T(8,128)(2,1)} %get-tuple-element.305.own, bf16[4,512,1024]{2,1,0:T(8,128)(2,1)} %copy-done), custom_call_target="tpu_custom_call" | custom-call | flops 2000000000 | bytes 20000000 | tf_op jit(solution)/shard_map/pallas_call | solution.py:1111
  445.6 6.0 shard_map.316
  457.0 17.1 %shard_map.318 = (bf16[16,128,384]{2,1,0:T(8,128)(2,1)}, f32[8,128]{1,0:T(8,128)}) custom-call(f32[16,128,128]{2,1,0:T(8,128)} %get-tuple-element.354.own, f32[16,128,128]{2,1,0:T(8,128)} %collective-permute-done.81.came, f32[2048,256]{1,0:T(8,128)} %get-tuple-element.359.raw, bf16[2048,128]{1,0:T(8,128)(2,1)} %get-tuple-element.360.queries, ...), custom_call_target="tpu_custom_call" | custom-call | flops 8000000000 | bytes 30000000 | tf_op jit(solution)/shard_map/pallas_call | solution.py:1150
  477.8 7.9 %shard_map.319 = (bf16[384,1024]{1,0:T(8,128)(2,1)}, bf16[384,1024]{1,0:T(8,128)(2,1)}, f32[8,1024]{1,0:T(8,128)}) custom-call(bf16[16,128,384]{2,1,0:T(8,128)(2,1)} %get-tuple-element.364.grads, bf16[16,128,384]{2,1,0:T(8,128)(2,1)} %collective-permute-done.82.came_grads, bf16[16,128,1024]{2,1,0:T(8,128)(2,1)} %get-tuple-element.367.normed, ...), custom_call_target="tpu_custom_call" | custom-call | flops 3221225472 | bytes 20000000 | tf_op jit(solution)/shard_map/pallas_call | solution.py:1164
  501.6 8.2 %shard_map.322 = (bf16[4,64,1024]{2,1,0:T(8,128)(2,1)}, bf16[4,64,1024]{2,1,0:T(8,128)(2,1)}, bf16[4,64,1024]{2,1,0:T(8,128)(2,1)}, bf16[4,64,1024]{2,1,0:T(8,12...) custom-call(s32[12]{0:T(128)} %stack.51.info, ...), custom_call_target="tpu_custom_call" | custom-call | flops 3221225472 | bytes 30000000 | tf_op jit(solution)/shard_map/pallas_call | solution.py:1188
  509.8 6.0 collective-permute-done.89
  517.5 8.0 %collective-permute-done.90 = bf16[608,512]{1,0:T(8,128)(2,1)S(1)} collective-permute-done((bf16[608,512]{1,0:T(8,128)(2,1)S(1)}, bf16[608,512]{1,0:T(8,128)(2,1)S(1)}, u32[]{:S(2)}, u32[]{:S(2)}) %collective-permute-start.90) | collective-permute-done | bytes 622624 | tf_op jit(solution)/shard_map/ppermute | solution.py:64
  540.0 10.1 %collective-permute-done.98 = bf16[4,384,512]{2,1,0:T(8,128)(2,1)S(1)} collective-permute-done((bf16[4,384,512]{2,1,0:T(8,128)(2,1)S(1)}, bf16[4,384,512]{2,1,0:T(8,128)(2,1)S(1)}, u32[]{:S(2)}, u32[]{:S(2)}) %collective-permute-start.98) | collective-permute-done | bytes 1572896 | tf_op jit(solution)/shard_map/ppermute | solution.py:64
  558.8 4.7 collective-permute-start.100
  572.7 5.0 collective-permute-done.104.refs_7_
  580.7 9.6 %collective-permute-start.105 = (f32[128,1024]{1,0:T(8,128)}, f32[128,1024]{1,0:T(8,128)}, u32[]{:S(2)}, u32[]{:S(2)}) collective-permute-start(f32[128,1024]{1,0:T(8,128)} %shard_map.325.own), channel_id=1, source_target_pairs={{0,1},{1,0},{2,3},{3,2},{4,5},{5,4},{6,7},{7,6},{8,9},{9,8},{10,11... | collective-permute-start | bytes 1572872 | tf_op jit(solution)/shard_map/ppermute | solution.py:82
  604.6 12.0 %all-gather.14.cloned.1.call-done = bf16[9728,512]{1,0:T(8,128)(2,1)} async-done(((bf16[608,512]{1,0:T(8,128)(2,1)}), bf16[9728,512]{1,0:T(8,128)(2,1)}) %all-gather.14.cloned.1.call-update) | async-done | bytes 9961488 | tf_op jit(solution)/shard_map/all_gather | solution.py:1197
  616.7 8.9 %shard_map.327 = (f32[512,2048]{1,0:T(8,128)}, f32[2048,512]{1,0:T(8,128)}, f32[512,256]{1,0:T(8,128)}, f32[512,256]{1,0:T(8,128)}, f32[64,512]{1,0:T(8,128)}, /...) custom-call(s32[12]{0:T(128)} %stack.51.info, ...), custom_call_target="tpu_custom_call" | custom-call | flops 1000000 | bytes 1000000 | tf_op jit(solution)/shard_map/pallas_call | solution.py:1209
  (500 shorter events, 332.6 us)
Async XLA Ops:
  7.2 83.1 %all-gather.8.cloned.1.call-start = ((), (), s32[]{:S(2)}) async-start(), calls=%async_computation.3 | async-start | bytes 4456448 | tf_op jit(solution)/shard_map/all_gather | solution.py:974
  8.9 222.1 %all-gather.10.cloned.1.call-start = ((), (), s32[]{:S(2)}) async-start(), calls=%async_computation.6 | async-start | bytes 15728640 | tf_op jit(solution)/shard_map/all_gather | solution.py:975
  20.3 17.2 %collective-permute-start.4 = (bf16[592,512]{1,0:T(8,128)(2,1)}, bf16[592,512]{1,0:T(8,128)(2,1)S(1)}, u32[]{:S(2)}, u32[]{:S(2)}) collective-permute-start(bf16[592,512]{1,0:T(8,128)(2,1)} %shard_map.289.a), channel_id=1, source_target_pairs={{0,32},{1,97},{32,64},{33,1},{64,96},{65,33},{96,0},{97,65},{2,34}... | collective-permute-start | bytes 1818632 | tf_op jit(solution)/shard_map/ppermute | solution.py:64
  23.9 19.2 %collective-permute-start.7 = (bf16[592,512]{1,0:T(8,128)(2,1)}, bf16[592,512]{1,0:T(8,128)(2,1)S(1)}, u32[]{:S(2)}, u32[]{:S(2)}) collective-permute-start(bf16[592,512]{1,0:T(8,128)(2,1)} %shard_map.289.a), channel_id=1, source_target_pairs={{0,96},{1,33},{32,0},{33,65},{64,32},{65,97},{96,64},{97,1},{2,98}... | collective-permute-start | bytes 1818632 | tf_op jit(solution)/shard_map/ppermute | solution.py:64
  47.3 219.8 %all-gather.12.cloned.1.call-start = ((), (), s32[]{:S(2)}) async-start(), calls=%async_computation.7 | async-start | bytes 7864320 | tf_op jit(solution)/shard_map/all_gather | solution.py:1019
  48.8 16.4 %collective-permute-start.12 = (bf16[592,512]{1,0:T(8,128)(2,1)S(1)}, bf16[592,512]{1,0:T(8,128)(2,1)S(1)}, u32[]{:S(2)}, u32[]{:S(2)}) collective-permute-start(bf16[592,512]{1,0:T(8,128)(2,1)S(1)} %collective-permute-done.4.d), channel_id=1, source_target_pairs={{0,32},{1,97},{32,64},{33,1},{64,96},{65,33},{96,0},{97,65},{2,34}... | collective-permute-start | bytes 1818632 | tf_op jit(solution)/shard_map/ppermute | solution.py:64
  53.5 25.0 %collective-permute-start.9 = (bf16[4,64,1152]{2,1,0:T(8,128)(2,1)}, bf16[4,64,1152]{2,1,0:T(8,128)(2,1)S(1)}, u32[]{:S(2)}, u32[]{:S(2)}) collective-permute-start(bf16[4,64,1152]{2,1,0:T(8,128)(2,1)} %shard_map.290.refs_0_), channel_id=1, source_target_pairs={{0,24},{1,9},{2,26},{3,11},{4,28},{5,13},{6,30},{7,15},{8,0},{9,17... | collective-permute-start | bytes 1769480 | tf_op jit(solution)/shard_map/ppermute | solution.py:64
  54.4 24.1 %collective-permute-start.8 = (bf16[4,64,1152]{2,1,0:T(8,128)(2,1)}, bf16[4,64,1152]{2,1,0:T(8,128)(2,1)S(1)}, u32[]{:S(2)}, u32[]{:S(2)}) collective-permute-start(bf16[4,64,1152]{2,1,0:T(8,128)(2,1)} %shard_map.290.refs_0_), channel_id=1, source_target_pairs={{0,8},{1,25},{2,10},{3,27},{4,12},{5,29},{6,14},{7,31},{8,16},{9,1... | collective-permute-start | bytes 1769480 | tf_op jit(solution)/shard_map/ppermute | solution.py:64
  58.9 19.7 %collective-permute-start.11 = (bf16[4,64,1152]{2,1,0:T(8,128)(2,1)}, bf16[4,64,1152]{2,1,0:T(8,128)(2,1)S(1)}, u32[]{:S(2)}, u32[]{:S(2)}) collective-permute-start(bf16[4,64,1152]{2,1,0:T(8,128)(2,1)} %shard_map.291.refs_4_), channel_id=1, source_target_pairs={{0,6},{1,3},{2,0},{3,5},{4,2},{5,7},{6,4},{7,1},{8,14},{9,11},{10,... | collective-permute-start | bytes 1769480 | tf_op jit(solution)/shard_map/ppermute | solution.py:64
  58.9 19.7 %collective-permute-start.10 = (bf16[4,64,1152]{2,1,0:T(8,128)(2,1)}, bf16[4,64,1152]{2,1,0:T(8,128)(2,1)S(1)}, u32[]{:S(2)}, u32[]{:S(2)}) collective-permute-start(bf16[4,64,1152]{2,1,0:T(8,128)(2,1)} %shard_map.291.refs_4_), channel_id=1, source_target_pairs={{0,2},{1,7},{2,4},{3,1},{4,6},{5,3},{6,0},{7,5},{8,10},{9,15},{10,... | collective-permute-start | bytes 1769480 | tf_op jit(solution)/shard_map/ppermute | solution.py:64
  69.3 20.9 %collective-permute-start.15 = (bf16[384,1024]{1,0:T(8,128)(2,1)}, bf16[384,1024]{1,0:T(8,128)(2,1)}, u32[]{:S(2)}, u32[]{:S(2)}) collective-permute-start(bf16[384,1024]{1,0:T(8,128)(2,1)} %get-tuple-element.242), channel_id=1, source_target_pairs={{0,1},{1,0},{2,3},{3,2},{4,5},{5,4},{6,7},{7,6},{8,9},{9,8},{10,11... | collective-permute-start | bytes 2359304 | tf_op jit(solution)/shard_map/ppermute | solution.py:82
  105.0 351.9 %reduce-scatter.8.cloned.1.call-start = ((), (), s32[]{:S(2)}) async-start(), calls=%async_computation.5 | async-start | bytes 7864320 | tf_op jit(solution)/shard_map/reduce_scatter | solution.py:1120
  136.8 14.9 %collective-permute-start.22 = (bf16[4,64,1024]{2,1,0:T(8,128)(2,1)}, bf16[4,64,1024]{2,1,0:T(8,128)(2,1)S(1)}, u32[]{:S(2)}, u32[]{:S(2)}) collective-permute-start(bf16[4,64,1024]{2,1,0:T(8,128)(2,1)} %get-tuple-element.254), channel_id=1, source_target_pairs={{0,6},{1,3},{2,0},{3,5},{4,2},{5,7},{6,4},{7,1},{8,14},{9,11},{10,... | collective-permute-start | bytes 1572872 | tf_op jit(solution)/shard_map/ppermute | solution.py:64
  192.2 42.8 %collective-permute-start.32 = (bf16[16,128,1024]{2,1,0:T(8,128)(2,1)}, bf16[16,128,1024]{2,1,0:T(8,128)(2,1)}, u32[]{:S(2)}, u32[]{:S(2)}) collective-permute-start(bf16[16,128,1024]{2,1,0:T(8,128)(2,1)} %all-gather.8.cloned.1.call-done.own), channel_id=1, source_target_pairs={{0,1},{1,0},{2,3},{3,2},{4,5},{5,4},{6,7},{7,6},{8,9},{9,8},{10,11... | collective-permute-start | bytes 12582920 | tf_op jit(solution)/shard_map/ppermute | solution.py:82
  216.0 14.6 %collective-permute-start.40 = (bf16[4,64,1152]{2,1,0:T(8,128)(2,1)}, bf16[4,64,1152]{2,1,0:T(8,128)(2,1)S(1)}, u32[]{:S(2)}, u32[]{:S(2)}) collective-permute-start(bf16[4,64,1152]{2,1,0:T(8,128)(2,1)} %shard_map.302.refs_0_), channel_id=1, source_target_pairs={{0,24},{1,9},{2,26},{3,11},{4,28},{5,13},{6,30},{7,15},{8,0},{9,17... | collective-permute-start | bytes 1769480 | tf_op jit(solution)/shard_map/ppermute | solution.py:64
  216.0 15.0 %collective-permute-start.39 = (bf16[4,64,1152]{2,1,0:T(8,128)(2,1)}, bf16[4,64,1152]{2,1,0:T(8,128)(2,1)S(1)}, u32[]{:S(2)}, u32[]{:S(2)}) collective-permute-start(bf16[4,64,1152]{2,1,0:T(8,128)(2,1)} %shard_map.302.refs_0_), channel_id=1, source_target_pairs={{0,8},{1,25},{2,10},{3,27},{4,12},{5,29},{6,14},{7,31},{8,16},{9,1... | collective-permute-start | bytes 1769480 | tf_op jit(solution)/shard_map/ppermute | solution.py:64
  309.5 147.4 %reduce-scatter.6.cloned.1.call-start = ((), (), s32[]{:S(2)}) async-start(), calls=%async_computation.4 | async-start | bytes 7864320 | tf_op jit(solution)/shard_map/reduce_scatter | solution.py:1118
  310.1 280.2 %reduce-scatter.10.cloned.1.call-start = ((), (), s32[]{:S(2)}) async-start(), calls=%async_computation.9 | async-start | bytes 4456448
  327.7 23.4 %collective-permute-start.55 = (bf16[4,64,1152]{2,1,0:T(8,128)(2,1)}, bf16[4,64,1152]{2,1,0:T(8,128)(2,1)S(1)}, u32[]{:S(2)}, u32[]{:S(2)}) collective-permute-start(bf16[4,64,1152]{2,1,0:T(8,128)(2,1)} %get-tuple-element.308), channel_id=1, source_target_pairs={{0,8},{1,25},{2,10},{3,27},{4,12},{5,29},{6,14},{7,31},{8,16},{9,1... | collective-permute-start | bytes 1769480 | tf_op jit(solution)/shard_map/ppermute | solution.py:64
  330.1 21.0 %collective-permute-start.56 = (bf16[4,64,1152]{2,1,0:T(8,128)(2,1)}, bf16[4,64,1152]{2,1,0:T(8,128)(2,1)S(1)}, u32[]{:S(2)}, u32[]{:S(2)}) collective-permute-start(bf16[4,64,1152]{2,1,0:T(8,128)(2,1)} %get-tuple-element.309), channel_id=1, source_target_pairs={{0,24},{1,9},{2,26},{3,11},{4,28},{5,13},{6,30},{7,15},{8,0},{9,17... | collective-permute-start | bytes 1769480 | tf_op jit(solution)/shard_map/ppermute | solution.py:64
  330.1 21.0 %collective-permute-start.57 = (bf16[4,64,1152]{2,1,0:T(8,128)(2,1)}, bf16[4,64,1152]{2,1,0:T(8,128)(2,1)S(1)}, u32[]{:S(2)}, u32[]{:S(2)}) collective-permute-start(bf16[4,64,1152]{2,1,0:T(8,128)(2,1)} %get-tuple-element.310), channel_id=1, source_target_pairs={{0,2},{1,7},{2,4},{3,1},{4,6},{5,3},{6,0},{7,5},{8,10},{9,15},{10,... | collective-permute-start | bytes 1769480 | tf_op jit(solution)/shard_map/ppermute | solution.py:64
  332.7 18.4 %collective-permute-start.58 = (bf16[4,64,1152]{2,1,0:T(8,128)(2,1)}, bf16[4,64,1152]{2,1,0:T(8,128)(2,1)S(1)}, u32[]{:S(2)}, u32[]{:S(2)}) collective-permute-start(bf16[4,64,1152]{2,1,0:T(8,128)(2,1)} %get-tuple-element.311), channel_id=1, source_target_pairs={{0,6},{1,3},{2,0},{3,5},{4,2},{5,7},{6,4},{7,1},{8,14},{9,11},{10,... | collective-permute-start | bytes 1769480 | tf_op jit(solution)/shard_map/ppermute | solution.py:64
  349.2 85.5 %collective-permute-start.54 = (bf16[4,512,1024]{2,1,0:T(8,128)(2,1)}, bf16[4,512,1024]{2,1,0:T(8,128)(2,1)S(1)}, u32[]{:S(2)}, u32[]{:S(2)}) collective-permute-start(bf16[4,512,1024]{2,1,0:T(8,128)(2,1)} %get-tuple-element.306), channel_id=1, source_target_pairs={{0,1},{1,0},{2,3},{3,2},{4,5},{5,4},{6,7},{7,6},{8,9},{9,8},{10,11... | collective-permute-start | bytes 12582920 | tf_op jit(solution)/shard_map/ppermute | solution.py:82
  451.6 165.1 %all-gather.14.cloned.1.call-start = ((), (), s32[]{:S(2)}) async-start(), calls=%async_computation.8 | async-start | bytes 10584064 | tf_op jit(solution)/shard_map/all_gather | solution.py:1197
  452.9 21.4 %collective-permute-start.83 = (bf16[4,384,512]{2,1,0:T(8,128)(2,1)S(1)}, bf16[4,384,512]{2,1,0:T(8,128)(2,1)S(1)}, u32[]{:S(2)}, u32[]{:S(2)}) collective-permute-start(bf16[4,384,512]{2,1,0:T(8,128)(2,1)S(1)} %copy-done.96), channel_id=1, source_target_pairs={{0,32},{1,97},{32,64},{33,1},{64,96},{65,33},{96,0},{97,65},{2,34}... | collective-permute-start | bytes 4718600 | tf_op jit(solution)/shard_map/ppermute | solution.py:64
  474.3 21.1 %collective-permute-start.88 = (bf16[4,384,512]{2,1,0:T(8,128)(2,1)S(1)}, bf16[4,384,512]{2,1,0:T(8,128)(2,1)S(1)}, u32[]{:S(2)}, u32[]{:S(2)}) collective-permute-start(bf16[4,384,512]{2,1,0:T(8,128)(2,1)S(1)} %copy-done.95), channel_id=1, source_target_pairs={{0,96},{1,33},{32,0},{33,65},{64,32},{65,97},{96,64},{97,1},{2,98}... | collective-permute-start | bytes 4718600 | tf_op jit(solution)/shard_map/ppermute | solution.py:64
  499.9 15.8 %collective-permute-start.89 = (bf16[608,512]{1,0:T(8,128)(2,1)}, bf16[608,512]{1,0:T(8,128)(2,1)S(1)}, u32[]{:S(2)}, u32[]{:S(2)}) collective-permute-start(bf16[608,512]{1,0:T(8,128)(2,1)} %get-tuple-element.381), channel_id=1, source_target_pairs={{0,32},{1,97},{32,64},{33,1},{64,96},{65,33},{96,0},{97,65},{2,34}... | collective-permute-start | bytes 1867784 | tf_op jit(solution)/shard_map/ppermute | solution.py:64
  501.6 15.9 %collective-permute-start.91 = (bf16[608,512]{1,0:T(8,128)(2,1)}, bf16[608,512]{1,0:T(8,128)(2,1)S(1)}, u32[]{:S(2)}, u32[]{:S(2)}) collective-permute-start(bf16[608,512]{1,0:T(8,128)(2,1)} %get-tuple-element.385), channel_id=1, source_target_pairs={{0,96},{1,33},{32,0},{33,65},{64,32},{65,97},{96,64},{97,1},{2,98}... | collective-permute-start | bytes 1867784 | tf_op jit(solution)/shard_map/ppermute | solution.py:64
  530.0 20.1 %collective-permute-start.98 = (bf16[4,384,512]{2,1,0:T(8,128)(2,1)S(1)}, bf16[4,384,512]{2,1,0:T(8,128)(2,1)S(1)}, u32[]{:S(2)}, u32[]{:S(2)}) collective-permute-start(bf16[4,384,512]{2,1,0:T(8,128)(2,1)S(1)} %add_convert_fusion), channel_id=1, source_target_pairs={{0,32},{1,97},{32,64},{33,1},{64,96},{65,33},{96,0},{97,65},{2,34}... | collective-permute-start | bytes 4718600 | tf_op jit(solution)/shard_map/ppermute | solution.py:64
  538.7 17.1 %collective-permute-start.97 = (bf16[4,64,1024]{2,1,0:T(8,128)(2,1)S(1)}, bf16[4,64,1024]{2,1,0:T(8,128)(2,1)S(1)}, u32[]{:S(2)}, u32[]{:S(2)}) collective-permute-start(bf16[4,64,1024]{2,1,0:T(8,128)(2,1)S(1)} %add_convert_fusion.5), channel_id=1, source_target_pairs={{0,2},{1,7},{2,4},{3,1},{4,6},{5,3},{6,0},{7,5},{8,10},{9,15},{10,... | collective-permute-start | bytes 1572872 | tf_op jit(solution)/shard_map/ppermute | solution.py:64
  539.1 16.7 %collective-permute-start.96 = (bf16[4,64,1024]{2,1,0:T(8,128)(2,1)S(1)}, bf16[4,64,1024]{2,1,0:T(8,128)(2,1)S(1)}, u32[]{:S(2)}, u32[]{:S(2)}) collective-permute-start(bf16[4,64,1024]{2,1,0:T(8,128)(2,1)S(1)} %add_convert_fusion.6), channel_id=1, source_target_pairs={{0,8},{1,25},{2,10},{3,27},{4,12},{5,29},{6,14},{7,31},{8,16},{9,1... | collective-permute-start | bytes 1572872 | tf_op jit(solution)/shard_map/ppermute | solution.py:64
  580.7 17.5 %collective-permute-start.105 = (f32[128,1024]{1,0:T(8,128)}, f32[128,1024]{1,0:T(8,128)}, u32[]{:S(2)}, u32[]{:S(2)}) collective-permute-start(f32[128,1024]{1,0:T(8,128)} %shard_map.325.own), channel_id=1, source_target_pairs={{0,1},{1,0},{2,3},{3,2},{4,5},{5,4},{6,7},{7,6},{8,9},{9,8},{10,11... | collective-permute-start | bytes 1572872 | tf_op jit(solution)/shard_map/ppermute | solution.py:82
  (194 other events, 1603.0 us)
Sparse Core Ops, SparseCore 0:
  10.7 63.0 all-gather.7
  76.1 122.5 all-gather.9
  200.4 66.6 all-gather.11
  309.7 64.6 reduce-scatter.7
  376.6 63.6 reduce-scatter.5
  451.7 75.9 reduce-scatter.9
  530.7 85.9 all-gather.13

commit v4 on v3

--- a/solution.py
+++ b/solution.py
@@ -1115,9 +1115,9 @@
         flops=2 * 10**9,
         moved=2 * 10**7,
     )(chosen, out_own, other_core(out_other))[0]
-    gate_mine = lax.psum_scatter(gate_grads, "fsdp", scatter_dimension=0, tiled=False)
+    gate_mine = lax.psum_scatter(after(gate_grads, grad_pieces[0]), "fsdp", scatter_dimension=0, tiled=False)
     grad_message = plane_scatter(grad_pieces, ((out_own,), (), ()))
-    up_mine = lax.psum_scatter(up_grads, "fsdp", scatter_dimension=0, tiled=False)
+    up_mine = lax.psum_scatter(after(up_grads, grad_pieces[0]), "fsdp", scatter_dimension=0, tiled=False)
 
     first, second, grad_residual2, router_rows = call(
         router_back_kernel,
@@ -1181,7 +1181,7 @@
         project_chunk_kernel, [scalars] + [whole] * 9, [(message_shape, bf16)] * 4
     )(
         info, project_own, project_came, gain1_part, other_core(gain1_part), gain_grads, other_core(gain_grads),
-        out_grad_own, after(other_core(out_grad_away), down_ahead), router_rows,
+        out_grad_own, other_core(out_grad_away), router_rows,
     )
     passing = moves_y()[0](project_pieces[2])
     from_ahead = moves_y()[1](project_pieces[3])
@@ -1192,7 +1192,7 @@
         flops=4 * count * half * 3 * size,
         moved=3 * 10**7,
     )(info, grads, after(grads_came, project_pieces[0]), dense_own, dense_came)
-    from_behind = moves_y()[0](add_low(project_pieces[1], after(passing, input_pieces[0])))
+    from_behind = moves_y()[0](add_low(project_pieces[1], after(passing, input_pieces[0], down_ahead)))
     message = low_sum((project_pieces[0], from_behind, from_ahead))
     message_all = lax.all_gather(message, "context", axis=0)
     down_behind = moves_y()[0](add_low(down_grads[1], down_passing))

time: 645 us -> 642 us (level)
    all_gather x1, waiting for transfers between devices: 12 us -> 23.5 us  [body(): message_all = lax.all_gather(message, 'context', axis=0)]
    ppermute x71, waiting for transfers between devices: 143 us -> 133 us  [move(): return lambda value: lax.ppermute(value, (axis, 'tensor'), pairs)]
    unnamed x227 -> x231, local copies, waits for them, and re-layouts: 22 us -> 20.5 us
  transfers between devices with their start and end apart: 113 -> 113, of which waited for: 57 -> 58; matrix products, arithmetic and copies ran while one was open for 5% -> 5% of each run, Pallas kernels for 29% -> 30%
where the time goes in v4:
time: 642 us; the launch traced here: 632 us
  Pallas kernels  237 us (37%)
  waiting for transfers between devices  193 us (30%)
  starting transfers between devices  134 us (21%)
  local copies, waits for them, and re-layouts  30.3 us (5%)
  other arithmetic  22.9 us (4%)
  between operations  15.3 us (2%)
    ppermute x71, waiting for transfers between devices, move(): return lambda value: lax.ppermute(value, (axis, 'tensor'), pairs)  133 us
    ppermute x71, starting transfers between devices, move(): return lambda value: lax.ppermute(value, (axis, 'tensor'), pairs)  92.6 us
    pallas_call x3, Pallas kernels, per_expert(): call(kernel, [scalars] + [by_expert(array.shape) for array in arrays], [(...  58.7 us
    all_gather x1, waiting for transfers between devices, body(): message_all = lax.all_gather(message, 'context', axis=0)  23.5 us
    ppermute x5, starting transfers between devices, along_x(): return lax.ppermute(value, 'context', pairs)  21 us
    unnamed x231, local copies, waits for them, and re-layouts  20.5 us
    ppermute x25, starting transfers between devices, other_core(): return lax.ppermute(value, 'tensor', [(0, 1), (1, 0)])  17.2 us
    pallas_call x1, Pallas kernels, body(): call(attend_back_kernel, [whole] * 13, [((spans, span, 3 * size), bf16),...  17 us
  transfers between devices with their start and end apart: 113, of which 58 were waited for; matrix products, arithmetic and copies ran while one was open for 5% of the time, Pallas kernels for 30%

profile of v4, /device:TPU:1, one launch (start us, length us, event | category | flops | bytes accessed | tf_op | source)
XLA Modules:
  0.0 631.9 jit_solution(13639337682823455830)
XLA Ops:
  71.4 7.2 %collective-permute-done.9.refs_1_ = bf16[4,64,1152]{2,1,0:T(8,128)(2,1)S(1)} collective-permute-done((bf16[4,64,1152]{2,1,0:T(8,128)(2,1)}, bf16[4,64,1152]{2,1,0:T(8,128)(2,1)S(1)}, u32[]{:S(2)}, u32[]{:S(2)}) %collective-permute-start.9) | collective-permute-done | bytes 589856 | tf_op jit(solution)/shard_map/ppermute | solution.py:64
  91.1 12.1 %shard_map.294 = (f32[16,128,384]{2,1,0:T(8,128)}, bf16[16,128,384]{2,1,0:T(8,128)(2,1)}, bf16[16,128,1024]{2,1,0:T(8,128)(2,1)}) custom-call(s32[12]{0:T(128)} %stack.51.info, f32[1,1024]{1,0:T(1,128)} %dynamic-slice_convert_fusion.gain, bf16[384,1024]{1,0:T(8,128)(2,1)} %get-tuple-element.242.own, bf16[384,1024]{1,0:T(8,128)(2,1)} %collective-permute-done.15.came, ...), custom_call_target="tpu_custom_call" | custom-call | flops 3221225472 | bytes 20000000 | tf_op jit(solution)/shard_map/pallas_call | solution.py:1012
  112.5 12.8 %shard_map.295 = (bf16[16,128,128]{2,1,0:T(8,128)(2,1)}, f32[2048,256]{1,0:T(8,128)}, bf16[2048,128]{1,0:T(8,128)(2,1)}, bf16[2048,128]{1,0:T(8,128)(2,1)}, bf16...) custom-call(f32[16,128,384]{2,1,0:T(8,128)} %get-tuple-element.244.own, bf16[16,128,384]{2,1,0:T(8,128)(2,1)} %copy-done.96, ...), custom_call_target="tpu_custom_call" | custom-call | flops 4000000000 | bytes 30000000 | tf_op jit(solution)/shard_map/pallas_call | solution.py:1020
  128.5 5.2 shard_map.296
  136.9 8.9 %collective-permute-done.19 = bf16[4,64,1024]{2,1,0:T(8,128)(2,1)S(1)} collective-permute-done((bf16[4,64,1024]{2,1,0:T(8,128)(2,1)}, bf16[4,64,1024]{2,1,0:T(8,128)(2,1)S(1)}, u32[]{:S(2)}, u32[]{:S(2)}) %collective-permute-start.19) | collective-permute-done | bytes 524320 | tf_op jit(solution)/shard_map/ppermute | solution.py:64
  156.6 5.1 collective-permute-done.24.b
  225.8 4.8 collective-permute-done.40.refs_1_
  235.1 9.3 %shard_map.301.grads = bf16[4,512,2048]{2,1,0:T(8,128)(2,1)} custom-call(s32[12]{0:T(128)} %stack.51.info, bf16[16,128,128]{2,1,0:T(8,128)(2,1)} %get-tuple-element.239.chosen, bf16[16,128,1024]{2,1,0:T(8,128)(2,1)} %all-gather.8.cloned.1.call-done.own, bf16[16,128,1024]{2,1,0:T(8,128)(2,1)} %collective-permute-done.32.other), custom_call_target="tpu_custom_call" | custom-call | flops 4000000000 | bytes 20000000 | tf_op jit(solution)/shard_map/pallas_call | solution.py:1057
  250.9 9.7 %shard_map.304 = (bf16[4,512,2048]{2,1,0:T(8,128)(2,1)}, bf16[4,512,128]{2,1,0:T(8,128)(2,1)}) custom-call(s32[12]{0:T(128)} %stack.51.info, bf16[16,128,128]{2,1,0:T(8,128)(2,1)} %get-tuple-element.239.chosen, bf16[4,64,1152]{2,1,0:T(8,128)(2,1)} %shard_map.302.refs_0_, bf16[4,64,1152]{2,1,0:T(8,128)(2,1)} %copy-done.100, bf16[4,64,1152]{2,1,0:T(8,128)(2,1)} %copy-done.102, ...), custom_call_target="tpu_custom_call" | custom-call | flops 4000000000 | bytes 20000000 | tf_op jit(solution)/shard_map/pallas_call | solution.py:1069
  260.6 6.5 %all-gather.12.cloned.1.call-done = bf16[16,384,512]{2,1,0:T(8,128)(2,1)} async-done(((bf16[4,384,512]{2,1,0:T(8,128)(2,1)}), bf16[16,384,512]{2,1,0:T(8,128)(2,1)}) %all-gather.12.cloned.1.call-update) | async-done | bytes 6291472 | tf_op jit(solution)/shard_map/all_gather | solution.py:1019
  267.1 30.1 %shard_map.305 = (bf16[4,512,1024]{2,1,0:T(8,128)(2,1)}, bf16[4,512,1024]{2,1,0:T(8,128)(2,1)}, bf16[4,512,128]{2,1,0:T(8,128)(2,1)}, bf16[4,512,384]{2,1,0:T(8,128)(2,1)}, bf16[4,512,768]{2,1,0:T(8,128)(2,1)}) custom-call(s32[12]{0:T(128)} %stack.51.info, bf16[4,512,2048]{2,1,0:T(8,128)(2,1)} %get-tuple-element.294.rows, ...), custom_call_target="tpu_custom_call" | custom-call | flops 16106127360 | bytes 50000000 | tf_op jit(solution)/shard_map/pallas_call | solution.py:797
  298.0 12.2 %shard_map.306 = (bf16[4,4,512,384]{3,2,1,0:T(8,128)(2,1)}, bf16[4,4,512,384]{3,2,1,0:T(8,128)(2,1)}) custom-call(s32[12]{0:T(128)} %stack.51.info, bf16[4,512,2048]{2,1,0:T(8,128)(2,1)} %get-tuple-element.294.rows, bf16[4,512,768]{2,1,0:T(8,128)(2,1)} %get-tuple-element.300.pairs), custom_call_target="tpu_custom_call" | custom-call | flops 6442450944 | bytes 30000000 | tf_op jit(solution)/shard_map/pallas_call | solution.py:797
  310.2 7.2 %shard_map.307 = (bf16[4,64,1152]{2,1,0:T(8,128)(2,1)}, bf16[4,64,1152]{2,1,0:T(8,128)(2,1)}, bf16[4,64,1152]{2,1,0:T(8,128)(2,1)}, bf16[4,64,1152]{2,1,0:T(8,12...) custom-call(s32[12]{0:T(128)} %stack.51.info, ...), custom_call_target="tpu_custom_call" | custom-call | flops 2000000000 | bytes 20000000 | tf_op jit(solution)/shard_map/pallas_call | solution.py:1096
  323.4 16.3 %shard_map.308 = (bf16[4,512,1024]{2,1,0:T(8,128)(2,1)}, bf16[4,512,1024]{2,1,0:T(8,128)(2,1)}, bf16[4,384,512]{2,1,0:T(8,128)(2,1)}, bf16[4,384,512]{2,1,0:T(8,...) custom-call(s32[12]{0:T(128)} %stack.51.info, bf16[4,512,2048]{2,1,0:T(8,128)(2,1)} %shard_map.301.grads, ...), custom_call_target="tpu_custom_call" | custom-call | flops 6442450944 | bytes 30000000 | tf_op jit(solution)/shard_map/pallas_call | solution.py:797
  345.7 5.0 collective-permute-done.60.b
  355.0 4.7 collective-permute-start.65
  366.2 4.9 collective-permute-done.61.refs_1_
  378.6 4.8 shard_map.313
  388.0 5.8 collective-permute-start.72
  410.8 5.8 collective-permute-done.77.refs_5_
  427.8 7.2 %shard_map.309 = bf16[16,128,1024]{2,1,0:T(8,128)(2,1)} custom-call(bf16[16,128,128]{2,1,0:T(8,128)(2,1)} %get-tuple-element.239.chosen, bf16[4,512,1024]{2,1,0:T(8,128)(2,1)} %get-tuple-element.306.own, bf16[4,512,1024]{2,1,0:T(8,128)(2,1)} %copy-done), custom_call_target="tpu_custom_call" | custom-call | flops 2000000000 | bytes 20000000 | tf_op jit(solution)/shard_map/pallas_call | solution.py:1111
  436.7 6.0 shard_map.316
  447.7 17.0 %shard_map.318 = (bf16[16,128,384]{2,1,0:T(8,128)(2,1)}, f32[8,128]{1,0:T(8,128)}) custom-call(f32[16,128,128]{2,1,0:T(8,128)} %get-tuple-element.355.own, f32[16,128,128]{2,1,0:T(8,128)} %collective-permute-done.81.came, f32[2048,256]{1,0:T(8,128)} %get-tuple-element.362.raw, bf16[2048,128]{1,0:T(8,128)(2,1)} %get-tuple-element.363.queries, ...), custom_call_target="tpu_custom_call" | custom-call | flops 8000000000 | bytes 30000000 | tf_op jit(solution)/shard_map/pallas_call | solution.py:1150
  469.8 8.1 %shard_map.319 = (bf16[384,1024]{1,0:T(8,128)(2,1)}, bf16[384,1024]{1,0:T(8,128)(2,1)}, f32[8,1024]{1,0:T(8,128)}) custom-call(bf16[16,128,384]{2,1,0:T(8,128)(2,1)} %get-tuple-element.367.grads, bf16[16,128,384]{2,1,0:T(8,128)(2,1)} %copy-done.95, bf16[16,128,1024]{2,1,0:T(8,128)(2,1)} %get-tuple-element.370.normed, ...), custom_call_target="tpu_custom_call" | custom-call | flops 3221225472 | bytes 20000000 | tf_op jit(solution)/shard_map/pallas_call | solution.py:1164
  490.5 8.1 %shard_map.322 = (bf16[4,64,1024]{2,1,0:T(8,128)(2,1)}, bf16[4,64,1024]{2,1,0:T(8,128)(2,1)}, bf16[4,64,1024]{2,1,0:T(8,128)(2,1)}, bf16[4,64,1024]{2,1,0:T(8,12...) custom-call(s32[12]{0:T(128)} %stack.51.info, ...), custom_call_target="tpu_custom_call" | custom-call | flops 3221225472 | bytes 30000000 | tf_op jit(solution)/shard_map/pallas_call | solution.py:1188
  498.6 5.8 collective-permute-done.88
  506.7 7.3 %collective-permute-done.90 = bf16[608,512]{1,0:T(8,128)(2,1)S(1)} collective-permute-done((bf16[608,512]{1,0:T(8,128)(2,1)S(1)}, bf16[608,512]{1,0:T(8,128)(2,1)S(1)}, u32[]{:S(2)}, u32[]{:S(2)}) %collective-permute-start.90) | collective-permute-done | bytes 622624 | tf_op jit(solution)/shard_map/ppermute | solution.py:64
  522.4 6.2 collective-permute-done.92
  528.6 6.0 collective-permute-done.93.c
  544.1 5.6 collective-permute-done.96.b
  591.3 23.5 %all-gather.14.cloned.1.call-done = bf16[9728,512]{1,0:T(8,128)(2,1)} async-done(((bf16[608,512]{1,0:T(8,128)(2,1)}), bf16[9728,512]{1,0:T(8,128)(2,1)}) %all-gather.14.cloned.1.call-update) | async-done | bytes 9961488 | tf_op jit(solution)/shard_map/all_gather | solution.py:1197
  614.8 8.9 %shard_map.327 = (f32[512,2048]{1,0:T(8,128)}, f32[2048,512]{1,0:T(8,128)}, f32[512,256]{1,0:T(8,128)}, f32[512,256]{1,0:T(8,128)}, f32[64,512]{1,0:T(8,128)}, /...) custom-call(s32[12]{0:T(128)} %stack.51.info, ...), custom_call_target="tpu_custom_call" | custom-call | flops 1000000 | bytes 1000000 | tf_op jit(solution)/shard_map/pallas_call | solution.py:1209
  (504 shorter events, 328.4 us)
Async XLA Ops:
  7.2 83.1 %all-gather.8.cloned.1.call-start = ((), (), s32[]{:S(2)}) async-start(), calls=%async_computation.3 | async-start | bytes 4456448 | tf_op jit(solution)/shard_map/all_gather | solution.py:974
  8.9 222.0 %all-gather.10.cloned.1.call-start = ((), (), s32[]{:S(2)}) async-start(), calls=%async_computation.6 | async-start | bytes 15728640 | tf_op jit(solution)/shard_map/all_gather | solution.py:975
  20.4 17.1 %collective-permute-start.4 = (bf16[592,512]{1,0:T(8,128)(2,1)}, bf16[592,512]{1,0:T(8,128)(2,1)S(1)}, u32[]{:S(2)}, u32[]{:S(2)}) collective-permute-start(bf16[592,512]{1,0:T(8,128)(2,1)} %shard_map.289.a), channel_id=1, source_target_pairs={{0,32},{1,97},{32,64},{33,1},{64,96},{65,33},{96,0},{97,65},{2,34}... | collective-permute-start | bytes 1818632 | tf_op jit(solution)/shard_map/ppermute | solution.py:64
  24.0 19.1 %collective-permute-start.7 = (bf16[592,512]{1,0:T(8,128)(2,1)}, bf16[592,512]{1,0:T(8,128)(2,1)S(1)}, u32[]{:S(2)}, u32[]{:S(2)}) collective-permute-start(bf16[592,512]{1,0:T(8,128)(2,1)} %shard_map.289.a), channel_id=1, source_target_pairs={{0,96},{1,33},{32,0},{33,65},{64,32},{65,97},{96,64},{97,1},{2,98}... | collective-permute-start | bytes 1818632 | tf_op jit(solution)/shard_map/ppermute | solution.py:64
  47.2 219.9 %all-gather.12.cloned.1.call-start = ((), (), s32[]{:S(2)}) async-start(), calls=%async_computation.7 | async-start | bytes 7864320 | tf_op jit(solution)/shard_map/all_gather | solution.py:1019
  48.7 16.6 %collective-permute-start.12 = (bf16[592,512]{1,0:T(8,128)(2,1)S(1)}, bf16[592,512]{1,0:T(8,128)(2,1)S(1)}, u32[]{:S(2)}, u32[]{:S(2)}) collective-permute-start(bf16[592,512]{1,0:T(8,128)(2,1)S(1)} %collective-permute-done.4.d), channel_id=1, source_target_pairs={{0,32},{1,97},{32,64},{33,1},{64,96},{65,33},{96,0},{97,65},{2,34}... | collective-permute-start | bytes 1818632 | tf_op jit(solution)/shard_map/ppermute | solution.py:64
  53.6 25.0 %collective-permute-start.9 = (bf16[4,64,1152]{2,1,0:T(8,128)(2,1)}, bf16[4,64,1152]{2,1,0:T(8,128)(2,1)S(1)}, u32[]{:S(2)}, u32[]{:S(2)}) collective-permute-start(bf16[4,64,1152]{2,1,0:T(8,128)(2,1)} %shard_map.290.refs_0_), channel_id=1, source_target_pairs={{0,24},{1,9},{2,26},{3,11},{4,28},{5,13},{6,30},{7,15},{8,0},{9,17... | collective-permute-start | bytes 1769480 | tf_op jit(solution)/shard_map/ppermute | solution.py:64
  54.4 24.2 %collective-permute-start.8 = (bf16[4,64,1152]{2,1,0:T(8,128)(2,1)}, bf16[4,64,1152]{2,1,0:T(8,128)(2,1)S(1)}, u32[]{:S(2)}, u32[]{:S(2)}) collective-permute-start(bf16[4,64,1152]{2,1,0:T(8,128)(2,1)} %shard_map.290.refs_0_), channel_id=1, source_target_pairs={{0,8},{1,25},{2,10},{3,27},{4,12},{5,29},{6,14},{7,31},{8,16},{9,1... | collective-permute-start | bytes 1769480 | tf_op jit(solution)/shard_map/ppermute | solution.py:64
  59.0 19.7 %collective-permute-start.11 = (bf16[4,64,1152]{2,1,0:T(8,128)(2,1)}, bf16[4,64,1152]{2,1,0:T(8,128)(2,1)S(1)}, u32[]{:S(2)}, u32[]{:S(2)}) collective-permute-start(bf16[4,64,1152]{2,1,0:T(8,128)(2,1)} %shard_map.291.refs_4_), channel_id=1, source_target_pairs={{0,6},{1,3},{2,0},{3,5},{4,2},{5,7},{6,4},{7,1},{8,14},{9,11},{10,... | collective-permute-start | bytes 1769480 | tf_op jit(solution)/shard_map/ppermute | solution.py:64
  59.0 19.7 %collective-permute-start.10 = (bf16[4,64,1152]{2,1,0:T(8,128)(2,1)}, bf16[4,64,1152]{2,1,0:T(8,128)(2,1)S(1)}, u32[]{:S(2)}, u32[]{:S(2)}) collective-permute-start(bf16[4,64,1152]{2,1,0:T(8,128)(2,1)} %shard_map.291.refs_4_), channel_id=1, source_target_pairs={{0,2},{1,7},{2,4},{3,1},{4,6},{5,3},{6,0},{7,5},{8,10},{9,15},{10,... | collective-permute-start | bytes 1769480 | tf_op jit(solution)/shard_map/ppermute | solution.py:64
  69.4 20.8 %collective-permute-start.15 = (bf16[384,1024]{1,0:T(8,128)(2,1)}, bf16[384,1024]{1,0:T(8,128)(2,1)}, u32[]{:S(2)}, u32[]{:S(2)}) collective-permute-start(bf16[384,1024]{1,0:T(8,128)(2,1)} %get-tuple-element.243), channel_id=1, source_target_pairs={{0,1},{1,0},{2,3},{3,2},{4,5},{5,4},{6,7},{7,6},{8,9},{9,8},{10,11... | collective-permute-start | bytes 2359304 | tf_op jit(solution)/shard_map/ppermute | solution.py:82
  105.1 341.6 %reduce-scatter.6.cloned.1.call-start = ((), (), s32[]{:S(2)}) async-start(), calls=%async_computation.4 | async-start | bytes 7864320 | tf_op jit(solution)/shard_map/reduce_scatter | solution.py:1118
  136.9 14.9 %collective-permute-start.22 = (bf16[4,64,1024]{2,1,0:T(8,128)(2,1)}, bf16[4,64,1024]{2,1,0:T(8,128)(2,1)S(1)}, u32[]{:S(2)}, u32[]{:S(2)}) collective-permute-start(bf16[4,64,1024]{2,1,0:T(8,128)(2,1)} %get-tuple-element.255), channel_id=1, source_target_pairs={{0,6},{1,3},{2,0},{3,5},{4,2},{5,7},{6,4},{7,1},{8,14},{9,11},{10,... | collective-permute-start | bytes 1572872 | tf_op jit(solution)/shard_map/ppermute | solution.py:64
  192.2 42.9 %collective-permute-start.32 = (bf16[16,128,1024]{2,1,0:T(8,128)(2,1)}, bf16[16,128,1024]{2,1,0:T(8,128)(2,1)}, u32[]{:S(2)}, u32[]{:S(2)}) collective-permute-start(bf16[16,128,1024]{2,1,0:T(8,128)(2,1)} %all-gather.8.cloned.1.call-done.own), channel_id=1, source_target_pairs={{0,1},{1,0},{2,3},{3,2},{4,5},{5,4},{6,7},{7,6},{8,9},{9,8},{10,11... | collective-permute-start | bytes 12582920 | tf_op jit(solution)/shard_map/ppermute | solution.py:82
  216.0 14.7 %collective-permute-start.40 = (bf16[4,64,1152]{2,1,0:T(8,128)(2,1)}, bf16[4,64,1152]{2,1,0:T(8,128)(2,1)S(1)}, u32[]{:S(2)}, u32[]{:S(2)}) collective-permute-start(bf16[4,64,1152]{2,1,0:T(8,128)(2,1)} %shard_map.302.refs_0_), channel_id=1, source_target_pairs={{0,24},{1,9},{2,26},{3,11},{4,28},{5,13},{6,30},{7,15},{8,0},{9,17... | collective-permute-start | bytes 1769480 | tf_op jit(solution)/shard_map/ppermute | solution.py:64
  216.0 15.0 %collective-permute-start.39 = (bf16[4,64,1152]{2,1,0:T(8,128)(2,1)}, bf16[4,64,1152]{2,1,0:T(8,128)(2,1)S(1)}, u32[]{:S(2)}, u32[]{:S(2)}) collective-permute-start(bf16[4,64,1152]{2,1,0:T(8,128)(2,1)} %shard_map.302.refs_0_), channel_id=1, source_target_pairs={{0,8},{1,25},{2,10},{3,27},{4,12},{5,29},{6,14},{7,31},{8,16},{9,1... | collective-permute-start | bytes 1769480 | tf_op jit(solution)/shard_map/ppermute | solution.py:64
  317.5 130.2 %reduce-scatter.8.cloned.1.call-start = ((), (), s32[]{:S(2)}) async-start(), calls=%async_computation.5 | async-start | bytes 7864320 | tf_op jit(solution)/shard_map/reduce_scatter | solution.py:1120
  318.1 258.8 %reduce-scatter.10.cloned.1.call-start = ((), (), s32[]{:S(2)}) async-start(), calls=%async_computation.9 | async-start | bytes 4456448
  318.1 23.1 %collective-permute-start.55 = (bf16[4,64,1152]{2,1,0:T(8,128)(2,1)}, bf16[4,64,1152]{2,1,0:T(8,128)(2,1)S(1)}, u32[]{:S(2)}, u32[]{:S(2)}) collective-permute-start(bf16[4,64,1152]{2,1,0:T(8,128)(2,1)} %get-tuple-element.309), channel_id=1, source_target_pairs={{0,8},{1,25},{2,10},{3,27},{4,12},{5,29},{6,14},{7,31},{8,16},{9,1... | collective-permute-start | bytes 1769480 | tf_op jit(solution)/shard_map/ppermute | solution.py:64
  320.6 20.7 %collective-permute-start.56 = (bf16[4,64,1152]{2,1,0:T(8,128)(2,1)}, bf16[4,64,1152]{2,1,0:T(8,128)(2,1)S(1)}, u32[]{:S(2)}, u32[]{:S(2)}) collective-permute-start(bf16[4,64,1152]{2,1,0:T(8,128)(2,1)} %get-tuple-element.310), channel_id=1, source_target_pairs={{0,24},{1,9},{2,26},{3,11},{4,28},{5,13},{6,30},{7,15},{8,0},{9,17... | collective-permute-start | bytes 1769480 | tf_op jit(solution)/shard_map/ppermute | solution.py:64
  320.6 20.7 %collective-permute-start.57 = (bf16[4,64,1152]{2,1,0:T(8,128)(2,1)S(1)}, bf16[4,64,1152]{2,1,0:T(8,128)(2,1)S(1)}, u32[]{:S(2)}, u32[]{:S(2)}) collective-permute-start(bf16[4,64,1152]{2,1,0:T(8,128)(2,1)S(1)} %copy-done.108), channel_id=1, source_target_pairs={{0,2},{1,7},{2,4},{3,1},{4,6},{5,3},{6,0},{7,5},{8,10},{9,15},{10,... | collective-permute-start | bytes 1769480 | tf_op jit(solution)/shard_map/ppermute | solution.py:64
  323.3 18.0 %collective-permute-start.58 = (bf16[4,64,1152]{2,1,0:T(8,128)(2,1)S(1)}, bf16[4,64,1152]{2,1,0:T(8,128)(2,1)S(1)}, u32[]{:S(2)}, u32[]{:S(2)}) collective-permute-start(bf16[4,64,1152]{2,1,0:T(8,128)(2,1)S(1)} %copy-done.106), channel_id=1, source_target_pairs={{0,6},{1,3},{2,0},{3,5},{4,2},{5,7},{6,4},{7,1},{8,14},{9,11},{10,... | collective-permute-start | bytes 1769480 | tf_op jit(solution)/shard_map/ppermute | solution.py:64
  339.7 86.1 %collective-permute-start.54 = (bf16[4,512,1024]{2,1,0:T(8,128)(2,1)}, bf16[4,512,1024]{2,1,0:T(8,128)(2,1)S(1)}, u32[]{:S(2)}, u32[]{:S(2)}) collective-permute-start(bf16[4,512,1024]{2,1,0:T(8,128)(2,1)} %get-tuple-element.307), channel_id=1, source_target_pairs={{0,1},{1,0},{2,3},{3,2},{4,5},{5,4},{6,7},{7,6},{8,9},{9,8},{10,11... | collective-permute-start | bytes 12582920 | tf_op jit(solution)/shard_map/ppermute | solution.py:82
  442.7 172.1 %all-gather.14.cloned.1.call-start = ((), (), s32[]{:S(2)}) async-start(), calls=%async_computation.8 | async-start | bytes 10584064 | tf_op jit(solution)/shard_map/all_gather | solution.py:1197
  443.9 21.5 %collective-permute-start.83 = (bf16[4,384,512]{2,1,0:T(8,128)(2,1)}, bf16[4,384,512]{2,1,0:T(8,128)(2,1)S(1)}, u32[]{:S(2)}, u32[]{:S(2)}) collective-permute-start(bf16[4,384,512]{2,1,0:T(8,128)(2,1)} %get-tuple-element.368), channel_id=1, source_target_pairs={{0,32},{1,97},{32,64},{33,1},{64,96},{65,33},{96,0},{97,65},{2,34}... | collective-permute-start | bytes 4718600 | tf_op jit(solution)/shard_map/ppermute | solution.py:64
  465.4 33.2 %collective-permute-start.89 = (bf16[4,384,512]{2,1,0:T(8,128)(2,1)S(1)}, bf16[4,384,512]{2,1,0:T(8,128)(2,1)S(1)}, u32[]{:S(2)}, u32[]{:S(2)}) collective-permute-start(bf16[4,384,512]{2,1,0:T(8,128)(2,1)S(1)} %copy-done.94), channel_id=1, source_target_pairs={{0,96},{1,33},{32,0},{33,65},{64,32},{65,97},{96,64},{97,1},{2,98}... | collective-permute-start | bytes 4718600 | tf_op jit(solution)/shard_map/ppermute | solution.py:64
  489.0 15.4 %collective-permute-start.88 = (bf16[608,512]{1,0:T(8,128)(2,1)}, bf16[608,512]{1,0:T(8,128)(2,1)S(1)}, u32[]{:S(2)}, u32[]{:S(2)}) collective-permute-start(bf16[608,512]{1,0:T(8,128)(2,1)} %get-tuple-element.381), channel_id=1, source_target_pairs={{0,32},{1,97},{32,64},{33,1},{64,96},{65,33},{96,0},{97,65},{2,34}... | collective-permute-start | bytes 1867784 | tf_op jit(solution)/shard_map/ppermute | solution.py:64
  489.5 17.2 %collective-permute-start.91 = (bf16[608,512]{1,0:T(8,128)(2,1)}, bf16[608,512]{1,0:T(8,128)(2,1)S(1)}, u32[]{:S(2)}, u32[]{:S(2)}) collective-permute-start(bf16[608,512]{1,0:T(8,128)(2,1)} %get-tuple-element.387), channel_id=1, source_target_pairs={{0,96},{1,33},{32,0},{33,65},{64,32},{65,97},{96,64},{97,1},{2,98}... | collective-permute-start | bytes 1867784 | tf_op jit(solution)/shard_map/ppermute | solution.py:64
  517.8 16.8 %collective-permute-start.93 = (bf16[4,64,1024]{2,1,0:T(8,128)(2,1)}, bf16[4,64,1024]{2,1,0:T(8,128)(2,1)S(1)}, u32[]{:S(2)}, u32[]{:S(2)}) collective-permute-start(bf16[4,64,1024]{2,1,0:T(8,128)(2,1)} %get-tuple-element.390), channel_id=1, source_target_pairs={{0,24},{1,9},{2,26},{3,11},{4,28},{5,13},{6,30},{7,15},{8,0},{9,17... | collective-permute-start | bytes 1572872 | tf_op jit(solution)/shard_map/ppermute | solution.py:64
  517.8 16.8 %collective-permute-start.94 = (bf16[4,64,1024]{2,1,0:T(8,128)(2,1)}, bf16[4,64,1024]{2,1,0:T(8,128)(2,1)S(1)}, u32[]{:S(2)}, u32[]{:S(2)}) collective-permute-start(bf16[4,64,1024]{2,1,0:T(8,128)(2,1)} %get-tuple-element.391), channel_id=1, source_target_pairs={{0,2},{1,7},{2,4},{3,1},{4,6},{5,3},{6,0},{7,5},{8,10},{9,15},{10,... | collective-permute-start | bytes 1572872 | tf_op jit(solution)/shard_map/ppermute | solution.py:64
  521.4 19.6 %collective-permute-start.98 = (bf16[4,384,512]{2,1,0:T(8,128)(2,1)S(1)}, bf16[4,384,512]{2,1,0:T(8,128)(2,1)S(1)}, u32[]{:S(2)}, u32[]{:S(2)}) collective-permute-start(bf16[4,384,512]{2,1,0:T(8,128)(2,1)S(1)} %add_convert_fusion), channel_id=1, source_target_pairs={{0,32},{1,97},{32,64},{33,1},{64,96},{65,33},{96,0},{97,65},{2,34}... | collective-permute-start | bytes 4718600 | tf_op jit(solution)/shard_map/ppermute | solution.py:64
  572.2 15.7 %collective-permute-start.105 = (f32[128,1024]{1,0:T(8,128)}, f32[128,1024]{1,0:T(8,128)}, u32[]{:S(2)}, u32[]{:S(2)}) collective-permute-start(f32[128,1024]{1,0:T(8,128)} %shard_map.325.own), channel_id=1, source_target_pairs={{0,1},{1,0},{2,3},{3,2},{4,5},{5,4},{6,7},{7,6},{8,9},{9,8},{10,11... | collective-permute-start | bytes 1572872 | tf_op jit(solution)/shard_map/ppermute | solution.py:82
  (196 other events, 1578.6 us)
Sparse Core Ops, SparseCore 0:
  10.7 63.1 all-gather.7
  76.2 122.5 all-gather.9
  200.4 66.6 all-gather.11
  317.6 64.1 reduce-scatter.5
  384.0 63.6 reduce-scatter.7
  450.9 76.8 reduce-scatter.9
  530.8 83.9 all-gather.13
